TPU v7x, 256 devices: a whole 4x4x8 slice. The times are simulated.
256 devices in a mesh: energy: 16 (over x, y), kmom: 16 (over z, core).
Axes of the slice: x: 4, y: 4, z: 8, core: 2. Of those that a mesh axis runs over, the one named last changes fastest.
Arguments:
- green_blocks: bfloat16 [32, 16, 144, 2048], P('energy', 'kmom'), may hold values from -6 to 6
- phonon: float32 [2, 8, 16], replicated, may hold values from -0.4 to 0.4
- offsets: int32 [8], replicated, may hold values from 1 to 2, as said below
- neighbours: int32 [2048, 8], P('kmom'), may hold values from 0 to 2047, as said below
- coupling: float32 [8, 12, 12], replicated, may hold values from -1.75 to 1.75
Outputs:
- self_energy: bfloat16 [32, 16, 144, 2048], P('energy', 'kmom')
Inputs may be any that keep to these rules, and one draw needn't show every extreme that they name: `offsets`: each value lies in 1 .. 2; at least one equals 2. Every neighbour of atom a lies within 32 of a in index; some atom has neighbours at exactly a + 32 and a - 32.
All inputs are finite; a program needn't handle non-finite values.
Results may differ from a plain program's by a relative error of at most 0.0064.
Values may be sent and summed in bfloat16 or wider, within the bound.
No kernel may reach another device: no remote copies, remote signals or barrier semaphores. Data moves between devices by JAX's collectives and lax.ppermute only.
A program may use at most 64 MiB of HBM per device.

v0:
```python
import jax
import jax.numpy as jnp
from jax import lax
from jax.sharding import Mesh
from jax.sharding import PartitionSpec as P

OFFSET = 2
RADIUS = 32
KMOM = ("kmom_0", "kmom_1")


def with_halo(block, sides, width):
    for axis, dim in sides:
        count = lax.axis_size(axis)
        forward = [(i, i + 1) for i in range(count - 1)]
        backward = [(target, source) for source, target in forward]
        low = lax.ppermute(
            lax.slice_in_dim(block, block.shape[dim] - width, None, axis=dim), axis, forward
        )
        high = lax.ppermute(lax.slice_in_dim(block, 0, width, axis=dim), axis, backward)
        block = jnp.concatenate([low, block, high], axis=dim)
    return block


def cut_along(x, dim, devices):
    dims = x.shape
    tiles = x.reshape(*dims[:dim], devices, dims[dim] // devices, *dims[dim + 1 :])
    return jnp.moveaxis(tiles, dim, 0)


def joined_along(tiles, dim):
    dims = list(tiles.shape[1:])
    dims[dim] *= tiles.shape[0]
    return jnp.moveaxis(tiles, 0, dim).reshape(dims)


def exchange_in_order(tiles, axes, order):
    dims = [lax.axis_size(a) for a in axes]
    tiles = tiles.reshape(*dims, *tiles.shape[1:])
    for k in order:
        tiles = lax.all_to_all(tiles, axes[k], split_axis=k, concat_axis=k, tiled=True)
    return tiles.reshape(-1, *tiles.shape[len(axes) :])


def exchange_by_chip(x, groups, order, split_dim, concat_dim):
    devices = lax.axis_size(groups[0]) * lax.axis_size(groups[1])
    tiles = cut_along(x, split_dim, devices)
    return joined_along(exchange_in_order(tiles, groups, order), concat_dim)


def energy_kernel(phonon, offsets, block_rows):
    mom_count = phonon.shape[2]
    rel_values = jnp.arange(2 * OFFSET + 1, dtype=jnp.int32) - OFFSET
    sign_values = jnp.array([-1, 1], dtype=jnp.int32)
    shifts = sign_values[:, None] * offsets[None, :]
    rel_hit = (shifts[:, :, None] == rel_values[None, None, :]).astype(jnp.float32)
    energy_taps = jnp.einsum("swr,swq->rq", rel_hit, phonon, precision=lax.Precision.HIGHEST)
    energy_taps = energy_taps.astype(jnp.bfloat16).astype(jnp.float32)
    out_rows = jnp.arange(block_rows, dtype=jnp.int32)
    in_rows = jnp.arange(block_rows + 2 * OFFSET, dtype=jnp.int32)
    tap_index = jnp.arange(2 * OFFSET + 1, dtype=jnp.int32)
    row_hit = (in_rows[None, :, None] - out_rows[:, None, None] == tap_index[None, None, :]).astype(
        jnp.float32
    )
    moms = jnp.arange(mom_count, dtype=jnp.int32)
    mom_hit = (
        (moms[:, None, None] - moms[None, :, None]) % mom_count == moms[None, None, :]
    ).astype(jnp.float32)
    kernel = jnp.einsum(
        "abr,kjq,rq->akbj", row_hit, mom_hit, energy_taps, precision=lax.Precision.HIGHEST
    )
    kernel = kernel.reshape(block_rows * mom_count, (block_rows + 2 * OFFSET) * mom_count)
    return kernel.astype(jnp.bfloat16)


def orbital_pairs(coupling):
    slots = coupling.shape[0]
    orbs = coupling.shape[1]
    outer = jnp.einsum("nip,njr->nijpr", coupling, coupling, precision=lax.Precision.HIGHEST)
    return outer.reshape(slots, orbs * orbs, orbs * orbs).astype(jnp.bfloat16)


def neighbour_sum(source, atom_index, pair_maps):
    lead = source.shape[:3]
    running = jnp.zeros(lead + (atom_index.shape[0],), jnp.float32)
    for slot in range(atom_index.shape[1]):
        taken = jnp.take(source, atom_index[:, slot], axis=3)
        running = running + jnp.einsum(
            "emca,dc->emda", taken, pair_maps[slot], preferred_element_type=jnp.float32
        )
    return running.astype(jnp.bfloat16)


def convolve(grouped, kernel):
    padded = with_halo(grouped, (("energy", 0),), OFFSET)
    flat_in = padded.reshape(padded.shape[0] * padded.shape[1], padded.shape[2] * padded.shape[3])
    smeared = jnp.dot(kernel, flat_in, preferred_element_type=jnp.float32).astype(jnp.bfloat16)
    return smeared.reshape(grouped.shape)


def body(green_blocks, phonon, offsets, neighbours, coupling):
    block_rows = green_blocks.shape[0]
    group_atoms = neighbours.shape[0]
    kernel = energy_kernel(phonon, offsets, block_rows)
    pair_maps = orbital_pairs(coupling)
    grouped = exchange_by_chip(green_blocks, ("kmom_0", "kmom_1"), (1, 0), 3, 1)
    rimmed = with_halo(grouped, ((KMOM, 3),), RADIUS)
    group_base = lax.axis_index(KMOM) * group_atoms
    local_index = neighbours - group_base + RADIUS
    coupled = neighbour_sum(rimmed, local_index, pair_maps)
    local_sigma = convolve(coupled, kernel)
    return lax.all_to_all(local_sigma, KMOM, split_axis=1, concat_axis=3, tiled=True)


def solution(mesh):
    torus = Mesh(mesh.devices.reshape(mesh.shape["energy"], 8, 2), ("energy", "kmom_0", "kmom_1"))
    placed = (P("energy", KMOM, None, None), P(), P(), P(KMOM, None), P())
    return jax.shard_map(
        body, mesh=torus, in_specs=placed, out_specs=P("energy", KMOM, None, None), check_vma=False
    )
```

profile of v0, /device:TPU:25, one launch (start us, length us, event | category | flops | bytes accessed | tf_op | source)
XLA Modules:
  0.0 179.5 jit_solution(5555827924203767841)
XLA Ops:
  1.9 5.0 %all_to_all.28 = bf16[8,2,2,1,144,128]{5,4,2,0,3,1:T(8,128)(2,1)S(1)} all-to-all(bf16[8,2,2,1,144,128]{5,4,2,0,3,1:T(8,128)(2,1)S(1)} %copy.70), channel_id=1, replica_groups=mesh['energy'=16,'kmom_0'=8,'kmom_1'=2] {'kmom_1'}, dimensions={1} | all-to-all | bytes 2359296 | tf_op jit(solution)/shard_map/all_to_all | solution.py:41
  7.9 8.2 %all-to-all-start.1 = ((bf16[8,2,2,1,144,128]{5,4,2,1,3,0:T(8,128)(2,1)}), bf16[8,2,2,1,144,128]{5,4,2,1,3,0:T(8,128)(2,1)S(1)}, u32[]{:S(2)}, u32[]{:S(2)}) async-start(bf16[8,2,2,1,144,128]{5,4,2,1,3,0:T(8,128)(2,1)} %copy.71), calls=%async_computation.1 | async-start | bytes 2359296 | tf_op jit(solution)/shard_map/all_to_all | solution.py:41
  17.1 2.2 %fusion.49 = (bf16[1,12,12,12,12]{4,3,2,1,0:T(8,128)(2,1)S(1)}, bf16[1,12,12,12,12]{4,3,2,1,0:T(8,128)(2,1)S(1)}, bf16[1,12,12,12,12]{4,3,2,1,0:T(8,128)(2,1)S(1...) fusion(bf16[8,12,12,12,12]{4,3,2,1,0:T(8,128)(2,1)S(1)} %fusion), kind=kLoop, calls=%fused_computation.100 | loop fusion | bytes 663552 | tf_op jit(solution)/shard_map/slice | solution.py:89
  19.3 2.1 %reshape.222 = bf16[144,144,1,1]{1,0,2,3:T(8,128)(2,1)} reshape(bf16[1,12,12,12,12]{4,3,2,1,0:T(8,128)(2,1)} %get-tuple-element.26) | data formatting | bytes 82944 | tf_op jit(solution)/shard_map/squeeze | solution.py:89
  21.4 2.1 %reshape.221 = bf16[144,144,1,1]{1,0,2,3:T(8,128)(2,1)} reshape(bf16[1,12,12,12,12]{4,3,2,1,0:T(8,128)(2,1)} %get-tuple-element.27) | data formatting | bytes 82944 | tf_op jit(solution)/shard_map/squeeze | solution.py:89
  23.5 2.1 %reshape.220 = bf16[144,144,1,1]{1,0,2,3:T(8,128)(2,1)} reshape(bf16[1,12,12,12,12]{4,3,2,1,0:T(8,128)(2,1)} %get-tuple-element.28) | data formatting | bytes 82944 | tf_op jit(solution)/shard_map/squeeze | solution.py:89
  25.6 2.1 %reshape.219 = bf16[144,144,1,1]{1,0,2,3:T(8,128)(2,1)} reshape(bf16[1,12,12,12,12]{4,3,2,1,0:T(8,128)(2,1)} %get-tuple-element.29) | data formatting | bytes 82944 | tf_op jit(solution)/shard_map/squeeze | solution.py:89
  30.9 17.3 %all-to-all-done.1 = bf16[8,2,2,1,144,128]{5,4,2,1,3,0:T(8,128)(2,1)S(1)} async-done(((bf16[8,2,2,1,144,128]{5,4,2,1,3,0:T(8,128)(2,1)}), bf16[8,2,2,1,144,128]{5,4,2,1,3,0:T(8,128)(2,1)S(1)}, u32[]{:S(2)}, u32[]{:S(2)}) %all-to-all-start.1) | async-done | bytes 1179680 | tf_op jit(solution)/shard_map/all_to_all | solution.py:41
  50.0 2.5 %collective-permute-start = (bf16[2,16,144,32]{2,1,3,0:T(8,128)(2,1)S(1)}, bf16[2,16,144,32]{2,1,3,0:T(8,128)(2,1)S(1)}, u32[]{:S(2)}, u32[]{:S(2)}) collective-permute-start(bf16[2,16,144,32]{2,1,3,0:T(8,128)(2,1)S(1)} %get-tuple-element.30), channel_id=1, source_target_pairs={{0,1},{1,2},{2,3},{3,4},{4,5},{5,6},{6,7},{7,8},{8,9},{9,10},{10,1... | collective-permute-start | bytes 884744 | tf_op jit(solution)/shard_map/ppermute | solution.py:17
  52.5 2.1 %collective-permute-start.1 = (bf16[2,16,144,32]{2,1,3,0:T(8,128)(2,1)S(1)}, bf16[2,16,144,32]{2,1,3,0:T(8,128)(2,1)S(1)}, u32[]{:S(2)}, u32[]{:S(2)}) collective-permute-start(bf16[2,16,144,32]{2,1,3,0:T(8,128)(2,1)S(1)} %get-tuple-element.31), channel_id=1, source_target_pairs={{1,0},{2,1},{3,2},{4,3},{5,4},{6,5},{7,6},{8,7},{9,8},{10,9},{11,1... | collective-permute-start | bytes 884744 | tf_op jit(solution)/shard_map/ppermute | solution.py:20
  54.7 3.9 %collective-permute-done = bf16[2,16,144,32]{2,1,3,0:T(8,128)(2,1)S(1)} collective-permute-done((bf16[2,16,144,32]{2,1,3,0:T(8,128)(2,1)S(1)}, bf16[2,16,144,32]{2,1,3,0:T(8,128)(2,1)S(1)}, u32[]{:S(2)}, u32[]{:S(2)}) %collective-permute-start) | collective-permute-done | bytes 294944 | tf_op jit(solution)/shard_map/ppermute | solution.py:17
  58.6 4.4 %collective-permute-done.1 = bf16[2,16,144,32]{2,1,3,0:T(8,128)(2,1)S(1)} collective-permute-done((bf16[2,16,144,32]{2,1,3,0:T(8,128)(2,1)S(1)}, bf16[2,16,144,32]{2,1,3,0:T(8,128)(2,1)S(1)}, u32[]{:S(2)}, u32[]{:S(2)}) %collective-permute-start.1) | collective-permute-done | bytes 294944 | tf_op jit(solution)/shard_map/ppermute | solution.py:20
  68.9 2.0 %gather_fusion = bf16[128,2,16,144]{3,2,1,0:T(8,128)(2,1)} fusion(bf16[2,16,144,192]{2,1,3,0:T(8,128)(2,1)S(1)} %pad_maximum_fusion.1, s32[1024]{0:T(1024)S(1)} %pad_clamp_fusion.7), kind=kCustom, calls=%fused_computation.clone | custom fusion | bytes 2359808 | tf_op jit(solution)/shard_map/jit(_take)/gather | solution.py:87
  70.9 2.0 %gather_fusion.1 = bf16[128,2,16,144]{3,2,1,0:T(8,128)(2,1)} fusion(bf16[2,16,144,192]{2,1,3,0:T(8,128)(2,1)S(1)} %pad_maximum_fusion.1, s32[1024]{0:T(1024)S(1)} %pad_clamp_fusion.6), kind=kCustom, calls=%fused_computation.1.clone | custom fusion | bytes 2359808 | tf_op jit(solution)/shard_map/jit(_take)/gather | solution.py:87
  73.0 2.1 %gather_fusion.4 = bf16[128,2,16,144]{3,2,1,0:T(8,128)(2,1)} fusion(bf16[2,16,144,192]{2,1,3,0:T(8,128)(2,1)S(1)} %pad_maximum_fusion.1, s32[1024]{0:T(1024)S(1)} %pad_clamp_fusion.3), kind=kCustom, calls=%fused_computation.4.clone | custom fusion | bytes 2359808 | tf_op jit(solution)/shard_map/jit(_take)/gather | solution.py:87
  75.0 2.1 %gather_fusion.5 = bf16[128,2,16,144]{3,2,1,0:T(8,128)(2,1)} fusion(bf16[2,16,144,192]{2,1,3,0:T(8,128)(2,1)S(1)} %pad_maximum_fusion.1, s32[1024]{0:T(1024)S(1)} %pad_clamp_fusion.2), kind=kCustom, calls=%fused_computation.5.clone | custom fusion | bytes 2359808 | tf_op jit(solution)/shard_map/jit(_take)/gather | solution.py:87
  77.1 2.0 %gather_fusion.6 = bf16[128,2,16,144]{3,2,1,0:T(8,128)(2,1)} fusion(bf16[2,16,144,192]{2,1,3,0:T(8,128)(2,1)S(1)} %pad_maximum_fusion.1, s32[1024]{0:T(1024)S(1)} %pad_clamp_fusion.1), kind=kCustom, calls=%fused_computation.6.clone | custom fusion | bytes 2359808 | tf_op jit(solution)/shard_map/jit(_take)/gather | solution.py:87
  79.1 2.0 %gather_fusion.7 = bf16[128,2,16,144]{3,2,1,0:T(8,128)(2,1)} fusion(bf16[2,16,144,192]{2,1,3,0:T(8,128)(2,1)S(1)} %pad_maximum_fusion.1, s32[1024]{0:T(1024)S(1)} %pad_clamp_fusion), kind=kCustom, calls=%fused_computation.7.clone | custom fusion | bytes 2359808 | tf_op jit(solution)/shard_map/jit(_take)/gather | solution.py:87
  81.1 2.6 %select_bitcast_fusion.4 = (bf16[2,16,144,128]{2,1,0,3:T(8,128)(2,1)S(1)}, bf16[2,16,144,128]{2,1,0,3:T(8,128)(2,1)S(1)}) fusion(bf16[128,2,16,144]{3,2,1,0:T(8,128)(2,1)} %gather_fusion.3, pred[128]{0:T(512)(128)(4,1)S(1)} %copy-done.17, bf16[128,2,16,144]{3,2,1,0:T(8,128)(2,1)} %gather_fusion.2, pred[128]{0:T(512)(128)(4,1)S(1)} %copy-done.18), kind=kLoop, calls=%fused_computation.36 | loop fusion | flops 1179648 | bytes 4718848 | tf_op jit(solution)/shard_map/jit(_take)/select_n | solution.py:87
  83.7 2.5 %fusion.11 = f32[144,2,16,128]{3,0,2,1:T(8,128)S(1)} fusion(bf16[2,16,144,128]{2,1,0,3:T(8,128)(2,1)S(1)} %get-tuple-element.50, bf16[144,144,1,1]{1,0,2,3:T(8,128)(2,1)S(1)} %copy-done.12), kind=kOutput, calls=%fused_computation.24 | convolution fusion | flops 169869312 | bytes 3580416 | tf_op jit(solution)/shard_map/emca,dc->emda/dot_general | solution.py:88
  86.3 2.5 %fusion.13 = f32[144,2,16,128]{3,0,2,1:T(8,128)S(1)} fusion(bf16[2,16,144,128]{2,1,0,3:T(8,128)(2,1)S(1)} %get-tuple-element.51, bf16[144,144,1,1]{1,0,2,3:T(8,128)(2,1)S(1)} %copy-done.11), kind=kOutput, calls=%fused_computation.26 | convolution fusion | flops 169869312 | bytes 3580416 | tf_op jit(solution)/shard_map/emca,dc->emda/dot_general | solution.py:88
  89.9 2.5 %fusion.15 = f32[144,2,16,128]{3,0,2,1:T(8,128)S(1)} fusion(bf16[2,16,144,128]{2,1,0,3:T(8,128)(2,1)S(1)} %get-tuple-element.52, bf16[144,144,1,1]{1,0,2,3:T(8,128)(2,1)S(1)} %copy-done.10), kind=kOutput, calls=%fused_computation.28 | convolution fusion | flops 169869312 | bytes 3580416 | tf_op jit(solution)/shard_map/emca,dc->emda/dot_general | solution.py:88
  92.4 2.5 %fusion.17 = f32[144,2,16,128]{3,0,2,1:T(8,128)S(1)} fusion(bf16[2,16,144,128]{2,1,0,3:T(8,128)(2,1)S(1)} %get-tuple-element.53, bf16[144,144,1,1]{1,0,2,3:T(8,128)(2,1)S(1)} %copy-done.9), kind=kOutput, calls=%fused_computation.30 | convolution fusion | flops 169869312 | bytes 3580416 | tf_op jit(solution)/shard_map/emca,dc->emda/dot_general | solution.py:88
  95.8 2.5 %fusion.9 = f32[144,2,16,128]{3,0,2,1:T(8,128)S(1)} fusion(bf16[2,16,144,128]{2,1,0,3:T(8,128)(2,1)S(1)} %get-tuple-element.49, bf16[144,144,1,1]{1,0,2,3:T(8,128)(2,1)S(1)} %copy-done.8), kind=kOutput, calls=%fused_computation.22 | convolution fusion | flops 169869312 | bytes 3580416 | tf_op jit(solution)/shard_map/emca,dc->emda/dot_general | solution.py:88
  98.4 2.5 %fusion.7 = f32[144,2,16,128]{3,0,2,1:T(8,128)S(1)} fusion(bf16[2,16,144,128]{2,1,0,3:T(8,128)(2,1)S(1)} %get-tuple-element.48, bf16[144,144,1,1]{1,0,2,3:T(8,128)(2,1)S(1)} %reshape.224), kind=kOutput, calls=%fused_computation.20 | convolution fusion | flops 169869312 | bytes 3580416 | tf_op jit(solution)/shard_map/emca,dc->emda/dot_general | solution.py:88
  102.0 2.5 %fusion.5 = f32[144,2,16,128]{3,0,2,1:T(8,128)S(1)} fusion(bf16[2,16,144,128]{2,1,0,3:T(8,128)(2,1)S(1)} %get-tuple-element.47, bf16[144,144,1,1]{1,0,2,3:T(8,128)(2,1)S(1)} %reshape.225), kind=kOutput, calls=%fused_computation.18 | convolution fusion | flops 169869312 | bytes 3580416 | tf_op jit(solution)/shard_map/emca,dc->emda/dot_general | solution.py:88
  104.5 3.3 %fusion.24 = bf16[2,16,144,128]{3,2,1,0:T(8,128)(2,1)S(1)} fusion(bf16[2,16,144,128]{2,1,0,3:T(8,128)(2,1)S(1)} %get-tuple-element.46, f32[144,2,16,128]{3,0,2,1:T(8,128)S(1)} %fusion.5, f32[144,2,16,128]{3,0,2,1:T(8,128)S(1)} %fusion.7, f32[144,2,16,128]{3,0,2,1:T(8,128)S(1)} %fusion.9, f32[144,2,16,128]{3,0,2,1:T(8,128)S(1)} %fusion.11, ...), kind=kOutput, calls=%fused_computation.41 | convolution fusion | flops 174587904 | bytes 18915840 | tf_op jit(solution)/shard_map/emca,dc->emda/dot_general | solution.py:88
  107.8 2.8 %collective-permute-start.2 = (bf16[2,16,144,128]{3,2,1,0:T(8,128)(2,1)S(1)}, bf16[2,16,144,128]{3,2,1,0:T(8,128)(2,1)S(1)}, u32[]{:S(2)}, u32[]{:S(2)}) collective-permute-start(bf16[2,16,144,128]{3,2,1,0:T(8,128)(2,1)S(1)} %fusion.24), channel_id=1, source_target_pairs={{0,16},{16,32},{32,48},{48,64},{64,80},{80,96},{96,112},{112,128},... | collective-permute-start | bytes 3538952 | tf_op jit(solution)/shard_map/ppermute | solution.py:17
  110.6 2.5 %collective-permute-start.3 = (bf16[2,16,144,128]{3,2,1,0:T(8,128)(2,1)S(1)}, bf16[2,16,144,128]{3,2,1,0:T(8,128)(2,1)S(1)}, u32[]{:S(2)}, u32[]{:S(2)}) collective-permute-start(bf16[2,16,144,128]{3,2,1,0:T(8,128)(2,1)S(1)} %fusion.24), channel_id=1, source_target_pairs={{16,0},{32,16},{48,32},{64,48},{80,64},{96,80},{112,96},{128,112},... | collective-permute-start | bytes 3538952 | tf_op jit(solution)/shard_map/ppermute | solution.py:20
  115.7 15.5 %collective-permute-done.2 = bf16[2,16,144,128]{3,2,1,0:T(8,128)(2,1)S(1)} collective-permute-done((bf16[2,16,144,128]{3,2,1,0:T(8,128)(2,1)S(1)}, bf16[2,16,144,128]{3,2,1,0:T(8,128)(2,1)S(1)}, u32[]{:S(2)}, u32[]{:S(2)}) %collective-permute-start.2) | collective-permute-done | bytes 1179680 | tf_op jit(solution)/shard_map/ppermute | solution.py:17
  131.1 5.2 %collective-permute-done.3 = bf16[2,16,144,128]{3,2,1,0:T(8,128)(2,1)S(1)} collective-permute-done((bf16[2,16,144,128]{3,2,1,0:T(8,128)(2,1)S(1)}, bf16[2,16,144,128]{3,2,1,0:T(8,128)(2,1)S(1)}, u32[]{:S(2)}, u32[]{:S(2)}) %collective-permute-start.3) | collective-permute-done | bytes 1179680 | tf_op jit(solution)/shard_map/ppermute | solution.py:20
  137.7 40.6 %all_to_all.29 = bf16[2,16,144,128]{3,2,0,1:T(8,128)(2,1)S(1)} all-to-all(bf16[2,16,144,128]{3,2,0,1:T(8,128)(2,1)S(1)} %copy.81), channel_id=1, replica_groups=mesh['energy'=16,'kmom_0'=8,'kmom_1'=2] {'kmom_0','kmom_1'}, dimensions={1} | all-to-all | bytes 2359296 | tf_op jit(solution)/shard_map/all_to_all | solution.py:112
  (85 shorter events, 22.6 us)
Async XLA Ops:
  0.0 113.2 %copy-start = (f32[2,8,16]{2,1,0:T(8,128)S(1)}, f32[2,8,16]{2,1,0:T(8,128)}, u32[]{:S(2)}) copy-start(f32[2,8,16]{2,1,0:T(8,128)} %param.9) | copy-start | bytes 3076
  6.8 9.3 %copy-start.13 = (f32[8,12,12]{2,0,1:T(8,128)S(1)}, f32[8,12,12]{2,0,1:T(8,128)}, u32[]{:S(2)}) copy-start(f32[8,12,12]{2,0,1:T(8,128)} %param.12) | copy-start | bytes 13828
  7.9 40.3 %all-to-all-start.1 = ((bf16[8,2,2,1,144,128]{5,4,2,1,3,0:T(8,128)(2,1)}), bf16[8,2,2,1,144,128]{5,4,2,1,3,0:T(8,128)(2,1)S(1)}, u32[]{:S(2)}, u32[]{:S(2)}) async-start(bf16[8,2,2,1,144,128]{5,4,2,1,3,0:T(8,128)(2,1)} %copy.71), calls=%async_computation.1 | async-start | bytes 2359296 | tf_op jit(solution)/shard_map/all_to_all | solution.py:41
  23.5 6.7 %copy-start.14 = (s32[128,8]{0,1:T(8,128)S(1)}, s32[128,8]{0,1:T(8,128)}, u32[]{:S(2)}) copy-start(s32[128,8]{0,1:T(8,128)} %param.11) | copy-start | bytes 12292
  49.9 8.7 %copy-start.1 = (bf16[16,2,1,144,128]{3,0,4,1,2:T(8,128)(2,1)}, bf16[16,2,1,144,128]{3,0,4,1,2:T(8,128)(2,1)S(1)}, u32[]{:S(2)}) copy-start(bf16[16,2,1,144,128]{3,0,4,1,2:T(8,128)(2,1)S(1)} %copy.72) | copy-start | bytes 3538948
  49.9 4.7 %copy-start.19 = (s32[128]{0:T(128)S(1)}, s32[128]{0:T(128)}, u32[]{:S(2)}) copy-start(s32[128]{0:T(128)} %get-tuple-element.33) | copy-start | bytes 1540
  50.0 8.6 %collective-permute-start = (bf16[2,16,144,32]{2,1,3,0:T(8,128)(2,1)S(1)}, bf16[2,16,144,32]{2,1,3,0:T(8,128)(2,1)S(1)}, u32[]{:S(2)}, u32[]{:S(2)}) collective-permute-start(bf16[2,16,144,32]{2,1,3,0:T(8,128)(2,1)S(1)} %get-tuple-element.30), channel_id=1, source_target_pairs={{0,1},{1,2},{2,3},{3,4},{4,5},{5,6},{6,7},{7,8},{8,9},{9,10},{10,1... | collective-permute-start | bytes 884744 | tf_op jit(solution)/shard_map/ppermute | solution.py:17
  52.5 10.5 %collective-permute-start.1 = (bf16[2,16,144,32]{2,1,3,0:T(8,128)(2,1)S(1)}, bf16[2,16,144,32]{2,1,3,0:T(8,128)(2,1)S(1)}, u32[]{:S(2)}, u32[]{:S(2)}) collective-permute-start(bf16[2,16,144,32]{2,1,3,0:T(8,128)(2,1)S(1)} %get-tuple-element.31), channel_id=1, source_target_pairs={{1,0},{2,1},{3,2},{4,3},{5,4},{6,5},{7,6},{8,7},{9,8},{10,9},{11,1... | collective-permute-start | bytes 884744 | tf_op jit(solution)/shard_map/ppermute | solution.py:20
  77.1 4.0 %copy-start.17 = (pred[128]{0:T(512)(128)(4,1)S(1)}, pred[128]{0:T(512)(128)(4,1)}, u32[]{:S(2)}) copy-start(pred[128]{0:T(512)(128)(4,1)} %get-tuple-element.40) | copy-start | bytes 388
  77.1 4.0 %copy-start.18 = (pred[128]{0:T(512)(128)(4,1)S(1)}, pred[128]{0:T(512)(128)(4,1)}, u32[]{:S(2)}) copy-start(pred[128]{0:T(512)(128)(4,1)} %get-tuple-element.42) | copy-start | bytes 388
  81.1 2.6 %copy-start.12 = (bf16[144,144,1,1]{1,0,2,3:T(8,128)(2,1)S(1)}, bf16[144,144,1,1]{1,0,2,3:T(8,128)(2,1)}, u32[]{:S(2)}) copy-start(bf16[144,144,1,1]{1,0,2,3:T(8,128)(2,1)} %reshape.222) | copy-start | bytes 124420
  83.7 2.5 %copy-start.11 = (bf16[144,144,1,1]{1,0,2,3:T(8,128)(2,1)S(1)}, bf16[144,144,1,1]{1,0,2,3:T(8,128)(2,1)}, u32[]{:S(2)}) copy-start(bf16[144,144,1,1]{1,0,2,3:T(8,128)(2,1)} %reshape.221) | copy-start | bytes 124420
  86.3 2.6 %copy-start.6 = (bf16[128,2,16,144]{3,2,1,0:T(8,128)(2,1)S(1)}, bf16[128,2,16,144]{3,2,1,0:T(8,128)(2,1)}, u32[]{:S(2)}) copy-start(bf16[128,2,16,144]{3,2,1,0:T(8,128)(2,1)} %gather_fusion) | copy-start | bytes 3538948
  86.3 2.6 %copy-start.7 = (bf16[128,2,16,144]{3,2,1,0:T(8,128)(2,1)S(1)}, bf16[128,2,16,144]{3,2,1,0:T(8,128)(2,1)}, u32[]{:S(2)}) copy-start(bf16[128,2,16,144]{3,2,1,0:T(8,128)(2,1)} %gather_fusion.1) | copy-start | bytes 3538948
  86.3 2.6 %copy-start.15 = (pred[128]{0:T(512)(128)(4,1)S(1)}, pred[128]{0:T(512)(128)(4,1)}, u32[]{:S(2)}) copy-start(pred[128]{0:T(512)(128)(4,1)} %get-tuple-element.6) | copy-start | bytes 388
  86.3 2.6 %copy-start.16 = (pred[128]{0:T(512)(128)(4,1)S(1)}, pred[128]{0:T(512)(128)(4,1)}, u32[]{:S(2)}) copy-start(pred[128]{0:T(512)(128)(4,1)} %get-tuple-element.44) | copy-start | bytes 388
  88.9 1.0 copy-start.10
  89.9 2.5 %copy-start.9 = (bf16[144,144,1,1]{1,0,2,3:T(8,128)(2,1)S(1)}, bf16[144,144,1,1]{1,0,2,3:T(8,128)(2,1)}, u32[]{:S(2)}) copy-start(bf16[144,144,1,1]{1,0,2,3:T(8,128)(2,1)} %reshape.219) | copy-start | bytes 124420
  92.4 2.5 %copy-start.4 = (bf16[128,2,16,144]{3,2,1,0:T(8,128)(2,1)S(1)}, bf16[128,2,16,144]{3,2,1,0:T(8,128)(2,1)}, u32[]{:S(2)}) copy-start(bf16[128,2,16,144]{3,2,1,0:T(8,128)(2,1)} %gather_fusion.4) | copy-start | bytes 3538948
  92.4 2.5 %copy-start.5 = (bf16[128,2,16,144]{3,2,1,0:T(8,128)(2,1)S(1)}, bf16[128,2,16,144]{3,2,1,0:T(8,128)(2,1)}, u32[]{:S(2)}) copy-start(bf16[128,2,16,144]{3,2,1,0:T(8,128)(2,1)} %gather_fusion.5) | copy-start | bytes 3538948
  95.0 0.9 copy-start.8
  98.4 2.5 %copy-start.2 = (bf16[128,2,16,144]{3,2,1,0:T(8,128)(2,1)S(1)}, bf16[128,2,16,144]{3,2,1,0:T(8,128)(2,1)}, u32[]{:S(2)}) copy-start(bf16[128,2,16,144]{3,2,1,0:T(8,128)(2,1)} %gather_fusion.6) | copy-start | bytes 3538948
  98.4 2.5 %copy-start.3 = (bf16[128,2,16,144]{3,2,1,0:T(8,128)(2,1)S(1)}, bf16[128,2,16,144]{3,2,1,0:T(8,128)(2,1)}, u32[]{:S(2)}) copy-start(bf16[128,2,16,144]{3,2,1,0:T(8,128)(2,1)} %gather_fusion.7) | copy-start | bytes 3538948
  104.5 8.6 %copy-start.20 = (s32[8]{0:T(128)S(1)}, s32[8]{0:T(128)}, u32[]{:S(2)}) copy-start(s32[8]{0:T(128)} %param.10) | copy-start | bytes 100
  104.5 8.6 %copy-start.21 = (s32[2]{0:T(128)S(1)}, s32[2]{0:T(128)}, u32[]{:S(2)}) copy-start(s32[2]{0:T(128)} %constant.44.clone) | copy-start | bytes 28
  107.8 23.4 %collective-permute-start.2 = (bf16[2,16,144,128]{3,2,1,0:T(8,128)(2,1)S(1)}, bf16[2,16,144,128]{3,2,1,0:T(8,128)(2,1)S(1)}, u32[]{:S(2)}, u32[]{:S(2)}) collective-permute-start(bf16[2,16,144,128]{3,2,1,0:T(8,128)(2,1)S(1)} %fusion.24), channel_id=1, source_target_pairs={{0,16},{16,32},{32,48},{48,64},{64,80},{80,96},{96,112},{112,128},... | collective-permute-start | bytes 3538952 | tf_op jit(solution)/shard_map/ppermute | solution.py:17
  110.6 25.8 %collective-permute-start.3 = (bf16[2,16,144,128]{3,2,1,0:T(8,128)(2,1)S(1)}, bf16[2,16,144,128]{3,2,1,0:T(8,128)(2,1)S(1)}, u32[]{:S(2)}, u32[]{:S(2)}) collective-permute-start(bf16[2,16,144,128]{3,2,1,0:T(8,128)(2,1)S(1)} %fusion.24), channel_id=1, source_target_pairs={{16,0},{32,16},{48,32},{64,48},{80,64},{96,80},{112,96},{128,112},... | collective-permute-start | bytes 3538952 | tf_op jit(solution)/shard_map/ppermute | solution.py:20
where the time goes:
time: 180 us; the launch traced here: 179 us
  waiting for transfers between devices  46.3 us (26%)
  blocking collectives  45.6 us (25%)
  local copies, waits for them, and re-layouts  37.3 us (21%)
  matrix products  22.4 us (12%)
  starting transfers between devices  18.1 us (10%)
  other arithmetic  9.27 us (5%)
    all_to_all x1, blocking collectives, body(): lax.all_to_all(local_sigma, KMOM, split_axis=1, concat_axis=3, tiled=True)  40.6 us
    dot_general x8, matrix products, neighbour_sum(): jnp.einsum('emca,dc->emda', taken, pair_maps[slot], preferred_element_typ...  20.9 us
    ppermute x2, waiting for transfers between devices, with_halo(): lax.ppermute(lax.slice_in_dim(block, block.shape[dim] - width, None, axis...  19.4 us
    all_to_all x1, waiting for transfers between devices, exchange_in_order(): lax.all_to_all(tiles, axes[k], split_axis=k, concat_axis=k, tiled=True)  17.3 us
    gather x8, local copies, waits for them, and re-layouts, neighbour_sum(): taken = jnp.take(source, atom_index[:, slot], axis=3)  16.2 us
    squeeze x8, local copies, waits for them, and re-layouts, neighbour_sum(): pair_maps[slot]  11 us
    ppermute x2, waiting for transfers between devices, with_halo(): lax.ppermute(lax.slice_in_dim(block, 0, width, axis=dim), axis, backward)  9.56 us
    all_to_all x1, starting transfers between devices, exchange_in_order(): lax.all_to_all(tiles, axes[k], split_axis=k, concat_axis=k, tiled=True)  8.19 us
  transfers between devices with their start and end apart: 5, of which 5 were waited for; matrix products, arithmetic and copies ran while one was open for 10% of the time, Pallas kernels for 0%

commit v1 on v0

v1 whole, which is shorter than its diff:
```python
import functools

import jax
import jax.numpy as jnp
from jax import lax
from jax.experimental import pallas as pl
from jax.experimental.pallas import tpu as pltpu
from jax.sharding import Mesh
from jax.sharding import PartitionSpec as P

OFFSET = 2
RADIUS = 32
CHUNKS = 2
ROWS = 16
LANES = 128
KMOM = ("z", "core")
SHIFTS = (4, 3, -3, 2, -2, 1, -1, 0)
VMEM = pl.BlockSpec(memory_space=pltpu.VMEM)
SMEM = pl.BlockSpec(memory_space=pltpu.SMEM)
ROOM = pltpu.CompilerParams(vmem_limit_bytes=40 * 2**20)


def energy_taps(phonon, offsets):
    rel_values = jnp.arange(2 * OFFSET + 1, dtype=jnp.int32) - OFFSET
    sign_values = jnp.array([-1, 1], dtype=jnp.int32)
    shifts = sign_values[:, None] * offsets[None, :]
    rel_hit = (shifts[:, :, None] == rel_values[None, None, :]).astype(jnp.float32)
    taps = jnp.sum(rel_hit[:, :, :, None] * phonon[:, :, None, :], axis=(0, 1))
    return taps.astype(jnp.bfloat16).astype(jnp.float32)


def mixing(taps, core, e_dev, groups):
    moms = taps.shape[1]
    shift = jnp.asarray(SHIFTS, dtype=jnp.int32)
    e_out = jnp.arange(e_dev, dtype=jnp.int32)
    e_in = (jnp.arange(3, dtype=jnp.int32)[:, None] - 1) * e_dev + jnp.arange(e_dev, dtype=jnp.int32)[None, :]
    r = e_in[None] - e_out[:, None, None] + OFFSET
    r_hit = (r[..., None] == jnp.arange(2 * OFFSET + 1, dtype=jnp.int32)).astype(jnp.float32)
    parity = jnp.stack([jnp.int32(0), 1 - 2 * core])
    q = (2 * (shift[None, :, None] + shift[None, None, :]) + parity[:, None, None]) % moms
    q_hit = (q[..., None] == jnp.arange(moms, dtype=jnp.int32)).astype(jnp.float32)
    t = jnp.einsum("otir,rq,pusq->oputsi", r_hit, taps, q_hit, precision=lax.Precision.HIGHEST)
    t = t.reshape(e_dev * 2 * groups, 3 * groups * e_dev)
    eye = jnp.eye(ROWS, dtype=jnp.float32)
    wide = t[:, None, :, None] * eye[None, :, None, :]
    return wide.reshape(t.shape[0] * ROWS, t.shape[1] * ROWS).astype(jnp.bfloat16)


def orbital_pairs(coupling):
    slots, orbs = coupling.shape[0], coupling.shape[1]
    pairs = jnp.arange(orbs * orbs, dtype=jnp.int32)
    orb = jnp.arange(orbs, dtype=jnp.int32)
    first = (pairs[:, None] // orbs == orb[None, :]).astype(jnp.float32)
    second = (pairs[:, None] % orbs == orb[None, :]).astype(jnp.float32)

    def spread(pick):
        half = jnp.einsum("nip,di->dnp", coupling, pick, precision=lax.Precision.HIGHEST)
        return jnp.einsum("dnp,cp->dnc", half, pick, precision=lax.Precision.HIGHEST)

    return (spread(first) * spread(second)).reshape(orbs * orbs, -1).astype(jnp.bfloat16)


def cut_kernel(chunk, groups, z_ref, green_ref, *out_refs):
    width = out_refs[0].shape[2]
    for out, shift in zip(out_refs, SHIFTS):
        group = lax.rem(z_ref[0] + shift + groups, groups)
        start = pl.multiple_of((chunk * groups + group) * width, LANES)
        out[...] = green_ref[:, :, pl.ds(start, width)]


def cut(green, z, chunk, groups):
    e_dev, pairs, atoms = green.shape
    width = atoms // (groups * CHUNKS)
    return pl.pallas_call(
        functools.partial(cut_kernel, chunk, groups),
        out_shape=[jax.ShapeDtypeStruct((e_dev, pairs, width), green.dtype)] * groups,
        in_specs=[SMEM, VMEM],
        out_specs=[VMEM] * groups,
        compiler_params=ROOM,
    )(z, green)


def stack_kernel(*refs):
    out = refs[-1]
    for i, block in enumerate(refs[:-1]):
        out[i] = block[...]


def stack(blocks):
    return pl.pallas_call(
        stack_kernel,
        out_shape=jax.ShapeDtypeStruct((len(blocks), *blocks[0].shape), blocks[0].dtype),
        in_specs=[VMEM] * len(blocks),
        out_specs=VMEM,
        compiler_params=ROOM,
    )(*blocks)


def mix_kernel(mix_ref, low_ref, own_ref, high_ref, same_ref, other_ref):
    groups, e_dev, pairs, width = own_ref.shape
    for g in range(pairs // ROWS):
        rows = pl.ds(g * ROWS, ROWS)
        tiles = [ref[:, :, rows, :].reshape(groups * e_dev * ROWS, width) for ref in (low_ref, own_ref, high_ref)]
        mixed = jnp.dot(mix_ref[...], jnp.concatenate(tiles, axis=0), preferred_element_type=jnp.float32)
        mixed = mixed.reshape(e_dev, 2, groups, ROWS, width)
        for e in range(e_dev):
            same_ref[:, e, rows, :] = mixed[e, 0]
            other_ref[:, e, rows, :] = mixed[e, 1].astype(jnp.bfloat16)


def mix(matrix, low, own, high):
    return pl.pallas_call(
        mix_kernel,
        out_shape=[jax.ShapeDtypeStruct(own.shape, jnp.float32), jax.ShapeDtypeStruct(own.shape, jnp.bfloat16)],
        in_specs=[VMEM] * 4,
        out_specs=[VMEM] * 2,
        compiler_params=ROOM,
    )(matrix, low, own, high)


def add_kernel(same_ref, other_ref, *out_refs):
    for i, out in enumerate(out_refs):
        out[...] = (same_ref[i] + other_ref[i].astype(jnp.float32)).astype(jnp.bfloat16)


def add(same, other):
    groups = same.shape[0]
    return pl.pallas_call(
        add_kernel,
        out_shape=[jax.ShapeDtypeStruct(same.shape[1:], jnp.bfloat16)] * groups,
        in_specs=[VMEM] * 2,
        out_specs=[VMEM] * groups,
        compiler_params=ROOM,
    )(same, other)


def couple_kernel(groups, z_ref, pair_ref, near_ref, *refs):
    blocks, out_ref, line, seen = refs[:-3], refs[-3], refs[-2], refs[-1]
    e_dev, pairs, width = blocks[0].shape
    slots = near_ref.shape[0]
    atoms = out_ref.shape[2]
    span = 2 * LANES
    pad = LANES // 2
    line[:, 0:LANES] = jnp.zeros((e_dev * pairs, LANES), jnp.bfloat16)
    line[:, atoms : atoms + LANES] = jnp.zeros((e_dev * pairs, LANES), jnp.bfloat16)
    for i, block in enumerate(blocks):
        chunk, shift = i // groups, SHIFTS[i % groups]
        group = lax.rem(z_ref[0] - shift + groups, groups)
        start = pl.multiple_of((chunk * groups + group) * width, LANES)
        seen[:, pl.ds(start, width)] = block[...].reshape(e_dev * pairs, width)
    line[:, pad : pad + atoms] = seen[...]
    place = lax.broadcasted_iota(jnp.int32, (span, LANES), 0)

    def step(b, carry):
        start = pl.multiple_of(b * LANES, LANES)
        lanes = pl.ds(start, LANES)
        window = line[:, pl.ds(start, span)]
        base = start - pad
        hits = []
        for n in range(slots):
            near = near_ref[n : n + 1, lanes] - base
            hits.append((place == near).astype(jnp.bfloat16))
        taken = jnp.dot(window, jnp.concatenate(hits, axis=1), preferred_element_type=jnp.float32).astype(jnp.bfloat16)
        columns = [
            jnp.concatenate([taken[e * pairs : (e + 1) * pairs, n * LANES : (n + 1) * LANES] for n in range(slots)], axis=0)
            for e in range(e_dev)
        ]
        total = jnp.dot(pair_ref[...], jnp.concatenate(columns, axis=1), preferred_element_type=jnp.float32)
        for e in range(e_dev):
            out_ref[e, :, lanes] = total[:, e * LANES : (e + 1) * LANES].astype(jnp.bfloat16)
        return carry

    lax.fori_loop(0, atoms // LANES, step, 0)


def couple(blocks, z, pair_maps, near, groups):
    e_dev, pairs, width = blocks[0].shape
    atoms = near.shape[1]
    return pl.pallas_call(
        functools.partial(couple_kernel, groups),
        out_shape=jax.ShapeDtypeStruct((e_dev, pairs, atoms), jnp.bfloat16),
        in_specs=[SMEM] + [VMEM] * (2 + len(blocks)),
        out_specs=VMEM,
        scratch_shapes=[
            pltpu.VMEM((e_dev * pairs, atoms + LANES), jnp.bfloat16),
            pltpu.VMEM((e_dev * pairs, atoms), jnp.bfloat16),
        ],
        compiler_params=ROOM,
    )(z, pair_maps, near, *blocks)


def along_z(x, shift):
    groups = lax.axis_size("z")
    return lax.ppermute(x, "z", [(i, (i + shift) % groups) for i in range(groups)])


def exchange(blocks):
    return [along_z(b, s) if s else b for b, s in zip(blocks, SHIFTS)]


def body(green_blocks, phonon, offsets, neighbours, coupling):
    groups, tiles = lax.axis_size("z"), lax.axis_size("energy")
    z = lax.axis_index("z")[None]
    green = green_blocks[:, 0]
    forward = [(i, i + 1) for i in range(tiles - 1)]
    backward = [(i + 1, i) for i in range(tiles - 1)]
    arrived = [exchange(cut(green, z, c, groups)) for c in range(CHUNKS)]
    matrix = mixing(energy_taps(phonon, offsets), lax.axis_index("core"), green.shape[0], groups)
    near = lax.all_gather(neighbours, KMOM, axis=0, tiled=True).T
    pair_maps = orbital_pairs(coupling)
    back = []
    for blocks in arrived:
        own = stack(blocks)
        low, high = lax.ppermute(own, "energy", forward), lax.ppermute(own, "energy", backward)
        same, other = mix(matrix, low, own, high)
        other = lax.ppermute(other, "core", [(0, 1), (1, 0)])
        back += exchange(add(same, other))
    return couple(back, z, pair_maps, near, groups)[:, None]


def solution(mesh):
    torus = Mesh(mesh.devices.reshape(mesh.shape["energy"], -1, 2), ("energy", *KMOM))
    placed = (P("energy", KMOM, None, None), P(), P(), P(KMOM, None), P())
    return jax.shard_map(body, mesh=torus, in_specs=placed, out_specs=P("energy", KMOM, None, None), check_vma=False)
```

time: 180 us -> 142 us (0.79)
  starting transfers between devices: 18.1 us -> 66.8 us
  waiting for transfers between devices: 46.3 us -> 15.4 us
  blocking collectives: 45.6 us -> 16.7 us
  local copies, waits for them, and re-layouts: 37.3 us -> 11.3 us
  Pallas kernels: 0 us -> 20.8 us
  matrix products: 22.4 us -> 5.81 us
  other arithmetic: 9.27 us -> 4.27 us
    ppermute x4 -> x34, starting transfers between devices: 9.87 us -> 66.8 us  [the longest x28 47.1 us: along_z(): lax.ppermute(x, 'z', [(i, (i + shift) % groups) for i in range(groups)])]
    all_to_all x2 -> x0, blocking collectives: 45.6 us -> none  [the longest x1 40.6 us: body(): lax.all_to_all(local_sigma, KMOM, split_axis=1, concat_axis=3, tiled=True)]
    pallas_call x0 -> x9, Pallas kernels: none -> 20.8 us  [the longest x1 11 us: couple(): pl.pallas_call(functools.partial(couple_kernel, groups), out_shape=jax.Sh...]
    all_to_all x1 -> x0, waiting for transfers between devices: 17.3 us -> none  [exchange_in_order(): lax.all_to_all(tiles, axes[k], split_axis=k, concat_axis=k, tiled=True)]
    all_gather x0 -> x1, blocking collectives: none -> 16.7 us  [body(): near = lax.all_gather(neighbours, KMOM, axis=0, tiled=True).T]
    dot_general x12 -> x6, matrix products: 22.4 us -> 5.81 us  [the longest x2 4.57 us: spread(): jnp.einsum('dnp,cp->dnc', half, pick, precision=lax.Precision.HIGHEST)]
    gather x8 -> x0, local copies, waits for them, and re-layouts: 16.2 us -> none  [neighbour_sum(): taken = jnp.take(source, atom_index[:, slot], axis=3)]
    ppermute x4 -> x34, waiting for transfers between devices: 29 us -> 15.4 us  [the longest x28 15.4 us: along_z(): lax.ppermute(x, 'z', [(i, (i + shift) % groups) for i in range(groups)])]
  transfers between devices with their start and end apart: 5 -> 34, of which waited for: 5 -> 5; matrix products, arithmetic and copies ran while one was open for 10% -> 14% of each run, Pallas kernels for 0% -> 7%
where the time goes in v1:
time: 142 us
  starting transfers between devices  66.8 us (47%)
  Pallas kernels  20.8 us (15%)
  blocking collectives  16.7 us (12%)
  waiting for transfers between devices  15.4 us (11%)
  local copies, waits for them, and re-layouts  11.3 us (8%)
  matrix products  5.81 us (4%)
  other arithmetic  4.27 us (3%)
    ppermute x28, starting transfers between devices, along_z(): lax.ppermute(x, 'z', [(i, (i + shift) % groups) for i in range(groups)])  47.1 us
    all_gather x1, blocking collectives, body(): near = lax.all_gather(neighbours, KMOM, axis=0, tiled=True).T  16.7 us
    ppermute x28, waiting for transfers between devices, along_z(): lax.ppermute(x, 'z', [(i, (i + shift) % groups) for i in range(groups)])  15.4 us
    pallas_call x1, Pallas kernels, couple(): pl.pallas_call(functools.partial(couple_kernel, groups), out_shape=jax.Sh...  11 us
    ppermute x2, starting transfers between devices, body(): lax.ppermute(own, 'energy', forward)  7.66 us
    convert_element_type x1, local copies, waits for them, and re-layouts, mixing(): wide.reshape(t.shape[0] * ROWS, t.shape[1] * ROWS).astype(jnp.bfloat16)  7.62 us
    ppermute x2, starting transfers between devices, body(): other = lax.ppermute(other, 'core', [(0, 1), (1, 0)])  7.46 us
    pallas_call x2, Pallas kernels, mix(): pl.pallas_call(mix_kernel, out_shape=[jax.ShapeDtypeStruct(own.shape, jnp...  6.89 us
  transfers between devices with their start and end apart: 34, of which 5 were waited for; matrix products, arithmetic and copies ran while one was open for 14% of the time, Pallas kernels for 7%

profile of v1, /device:TPU:25, one launch (start us, length us, event | category | flops | bytes accessed | tf_op | source)
XLA Modules:
  0.0 141.6 jit_solution(7322539125428830191)
XLA Ops:
  1.5 7.0 %collective-permute-start = (bf16[2,144,128]{2,1,0:T(8,128)(2,1)S(1)}, bf16[2,144,128]{2,1,0:T(8,128)(2,1)S(1)}, u32[]{:S(2)}, u32[]{:S(2)}) collective-permute-start(bf16[2,144,128]{2,1,0:T(8,128)(2,1)S(1)} %get-tuple-element.41), channel_id=1, source_target_pairs={{0,8},{2,10},{4,12},{6,14},{8,0},{10,2},{12,4},{14,6},{1,9},{3,11}... | collective-permute-start | bytes 221192 | tf_op jit(solution)/shard_map/ppermute | solution.py:194
  8.5 1.6 %collective-permute-start.1 = (bf16[2,144,128]{2,1,0:T(8,128)(2,1)S(1)}, bf16[2,144,128]{2,1,0:T(8,128)(2,1)S(1)}, u32[]{:S(2)}, u32[]{:S(2)}) collective-permute-start(bf16[2,144,128]{2,1,0:T(8,128)(2,1)S(1)} %get-tuple-element.42), channel_id=1, source_target_pairs={{0,6},{2,8},{4,10},{6,12},{8,14},{10,0},{12,2},{14,4},{1,7},{3,9},... | collective-permute-start | bytes 221192 | tf_op jit(solution)/shard_map/ppermute | solution.py:194
  10.1 2.8 %collective-permute-start.2 = (bf16[2,144,128]{2,1,0:T(8,128)(2,1)S(1)}, bf16[2,144,128]{2,1,0:T(8,128)(2,1)S(1)}, u32[]{:S(2)}, u32[]{:S(2)}) collective-permute-start(bf16[2,144,128]{2,1,0:T(8,128)(2,1)S(1)} %get-tuple-element.43), channel_id=1, source_target_pairs={{0,10},{2,12},{4,14},{6,0},{8,2},{10,4},{12,6},{14,8},{1,11},{3,13... | collective-permute-start | bytes 221192 | tf_op jit(solution)/shard_map/ppermute | solution.py:194
  14.2 2.4 %collective-permute-start.4 = (bf16[2,144,128]{2,1,0:T(8,128)(2,1)S(1)}, bf16[2,144,128]{2,1,0:T(8,128)(2,1)S(1)}, u32[]{:S(2)}, u32[]{:S(2)}) collective-permute-start(bf16[2,144,128]{2,1,0:T(8,128)(2,1)S(1)} %get-tuple-element.45), channel_id=1, source_target_pairs={{0,12},{2,14},{4,0},{6,2},{8,4},{10,6},{12,8},{14,10},{1,13},{3,15... | collective-permute-start | bytes 221192 | tf_op jit(solution)/shard_map/ppermute | solution.py:194
  18.0 1.9 %collective-permute-done.1.refs_1_ = bf16[2,144,128]{2,1,0:T(8,128)(2,1)S(1)} collective-permute-done((bf16[2,144,128]{2,1,0:T(8,128)(2,1)S(1)}, bf16[2,144,128]{2,1,0:T(8,128)(2,1)S(1)}, u32[]{:S(2)}, u32[]{:S(2)}) %collective-permute-start.1) | collective-permute-done | bytes 73760 | tf_op jit(solution)/shard_map/ppermute | solution.py:194
  20.1 2.3 %collective-permute-start.17 = (bf16[2,144,128]{2,1,0:T(8,128)(2,1)S(1)}, bf16[2,144,128]{2,1,0:T(8,128)(2,1)S(1)}, u32[]{:S(2)}, u32[]{:S(2)}) collective-permute-start(bf16[2,144,128]{2,1,0:T(8,128)(2,1)S(1)} %get-tuple-element.59), channel_id=1, source_target_pairs={{0,8},{2,10},{4,12},{6,14},{8,0},{10,2},{12,4},{14,6},{1,9},{3,11}... | collective-permute-start | bytes 221192 | tf_op jit(solution)/shard_map/ppermute | solution.py:194
  23.2 3.7 %collective-permute-start.19 = (bf16[2,144,128]{2,1,0:T(8,128)(2,1)S(1)}, bf16[2,144,128]{2,1,0:T(8,128)(2,1)S(1)}, u32[]{:S(2)}, u32[]{:S(2)}) collective-permute-start(bf16[2,144,128]{2,1,0:T(8,128)(2,1)S(1)} %get-tuple-element.61), channel_id=1, source_target_pairs={{0,10},{2,12},{4,14},{6,0},{8,2},{10,4},{12,6},{14,8},{1,11},{3,13... | collective-permute-start | bytes 221192 | tf_op jit(solution)/shard_map/ppermute | solution.py:194
  27.1 3.6 %collective-permute-start.21 = (bf16[2,144,128]{2,1,0:T(8,128)(2,1)S(1)}, bf16[2,144,128]{2,1,0:T(8,128)(2,1)S(1)}, u32[]{:S(2)}, u32[]{:S(2)}) collective-permute-start(bf16[2,144,128]{2,1,0:T(8,128)(2,1)S(1)} %get-tuple-element.63), channel_id=1, source_target_pairs={{0,12},{2,14},{4,0},{6,2},{8,4},{10,6},{12,8},{14,10},{1,13},{3,15... | collective-permute-start | bytes 221192 | tf_op jit(solution)/shard_map/ppermute | solution.py:194
  31.7 3.0 %collective-permute-done.18.refs_1_ = bf16[2,144,128]{2,1,0:T(8,128)(2,1)S(1)} collective-permute-done((bf16[2,144,128]{2,1,0:T(8,128)(2,1)S(1)}, bf16[2,144,128]{2,1,0:T(8,128)(2,1)S(1)}, u32[]{:S(2)}, u32[]{:S(2)}) %collective-permute-start.18) | collective-permute-done | bytes 73760 | tf_op jit(solution)/shard_map/ppermute | solution.py:194
  34.7 2.8 %collective-permute-start.7 = (bf16[8,2,144,128]{3,2,1,0:T(8,128)(2,1)S(1)}, bf16[8,2,144,128]{3,2,1,0:T(8,128)(2,1)S(1)}, u32[]{:S(2)}, u32[]{:S(2)}) collective-permute-start(bf16[8,2,144,128]{3,2,1,0:T(8,128)(2,1)S(1)} %shard_map.74.own_ref), channel_id=1, source_target_pairs={{0,16},{16,32},{32,48},{48,64},{64,80},{80,96},{96,112},{112,128},... | collective-permute-start | bytes 1769480 | tf_op jit(solution)/shard_map/ppermute | solution.py:214
  37.5 2.5 %collective-permute-start.8 = (bf16[8,2,144,128]{3,2,1,0:T(8,128)(2,1)S(1)}, bf16[8,2,144,128]{3,2,1,0:T(8,128)(2,1)S(1)}, u32[]{:S(2)}, u32[]{:S(2)}) collective-permute-start(bf16[8,2,144,128]{3,2,1,0:T(8,128)(2,1)S(1)} %shard_map.74.own_ref), channel_id=1, source_target_pairs={{16,0},{32,16},{48,32},{64,48},{80,64},{96,80},{112,96},{128,112},... | collective-permute-start | bytes 1769480 | tf_op jit(solution)/shard_map/ppermute | solution.py:214
  41.2 4.9 %collective-permute-start.24 = (bf16[8,2,144,128]{3,2,1,0:T(8,128)(2,1)S(1)}, bf16[8,2,144,128]{3,2,1,0:T(8,128)(2,1)}, u32[]{:S(2)}, u32[]{:S(2)}) collective-permute-start(bf16[8,2,144,128]{3,2,1,0:T(8,128)(2,1)S(1)} %shard_map.78.own_ref), channel_id=1, source_target_pairs={{0,16},{16,32},{32,48},{48,64},{64,80},{80,96},{96,112},{112,128},... | collective-permute-start | bytes 1769480 | tf_op jit(solution)/shard_map/ppermute | solution.py:214
  46.1 2.1 %collective-permute-start.25 = (bf16[8,2,144,128]{3,2,1,0:T(8,128)(2,1)S(1)}, bf16[8,2,144,128]{3,2,1,0:T(8,128)(2,1)}, u32[]{:S(2)}, u32[]{:S(2)}) collective-permute-start(bf16[8,2,144,128]{3,2,1,0:T(8,128)(2,1)S(1)} %shard_map.78.own_ref), channel_id=1, source_target_pairs={{16,0},{32,16},{48,32},{64,48},{80,64},{96,80},{112,96},{128,112},... | collective-permute-start | bytes 1769480 | tf_op jit(solution)/shard_map/ppermute | solution.py:214
  48.2 3.8 %multiply_convert_fusion = bf16[32,16,48,16]{3,2,1,0:T(8,128)(2,1)} fusion(f32[16,16]{1,0:T(8,128)S(1)} %fusion.18, f32[32,48]{1,0:T(8,128)S(1)} %copy.17), kind=kLoop, calls=%fused_computation | loop fusion | flops 786432 | bytes 793600 | tf_op jit(solution)/shard_map/convert_element_type | solution.py:46
  52.0 7.6 %convert_element_type.38.mix_ref = bf16[512,768]{1,0:T(8,128)(2,1)S(1)} reshape(bf16[32,16,48,16]{3,2,1,0:T(8,128)(2,1)} %multiply_convert_fusion) | data formatting | bytes 1572864 | tf_op jit(solution)/shard_map/convert_element_type | solution.py:46
  59.6 2.8 %shard_map.75 = (f32[8,2,144,128]{3,2,1,0:T(8,128)S(1)}, bf16[8,2,144,128]{3,2,1,0:T(8,128)(2,1)}) custom-call(bf16[512,768]{1,0:T(8,128)(2,1)S(1)} %convert_element_type.38.mix_ref, bf16[8,2,144,128]{3,2,1,0:T(8,128)(2,1)S(1)} %collective-permute-done.7.low_ref, bf16[8,2,144,128]{3,2,1,0:T(8,128)(2,1)S(1)} %shard_map.74.own_ref, ...), custom_call_target="tpu_custom_call" | custom-call | tf_op jit(solution)/shard_map/pallas_call | solution.py:112
  62.5 3.7 %collective-permute-start.9 = (bf16[8,2,144,128]{3,2,1,0:T(8,128)(2,1)}, bf16[8,2,144,128]{3,2,1,0:T(8,128)(2,1)}, u32[]{:S(2)}, u32[]{:S(2)}) collective-permute-start(bf16[8,2,144,128]{3,2,1,0:T(8,128)(2,1)} %get-tuple-element.50), channel_id=1, source_target_pairs={{0,1},{1,0},{2,3},{3,2},{4,5},{5,4},{6,7},{7,6},{8,9},{9,8},{10,11... | collective-permute-start | bytes 1769480 | tf_op jit(solution)/shard_map/ppermute | solution.py:216
  66.2 4.1 %shard_map.79 = (f32[8,2,144,128]{3,2,1,0:T(8,128)S(1)}, bf16[8,2,144,128]{3,2,1,0:T(8,128)(2,1)}) custom-call(bf16[512,768]{1,0:T(8,128)(2,1)S(1)} %convert_element_type.38.mix_ref, bf16[8,2,144,128]{3,2,1,0:T(8,128)(2,1)} %collective-permute-done.24.low_ref, bf16[8,2,144,128]{3,2,1,0:T(8,128)(2,1)S(1)} %shard_map.78.own_ref, ...), custom_call_target="tpu_custom_call" | custom-call | tf_op jit(solution)/shard_map/pallas_call | solution.py:112
  70.3 3.7 %collective-permute-start.26 = (bf16[8,2,144,128]{3,2,1,0:T(8,128)(2,1)}, bf16[8,2,144,128]{3,2,1,0:T(8,128)(2,1)S(1)}, u32[]{:S(2)}, u32[]{:S(2)}) collective-permute-start(bf16[8,2,144,128]{3,2,1,0:T(8,128)(2,1)} %get-tuple-element.68), channel_id=1, source_target_pairs={{0,1},{1,0},{2,3},{3,2},{4,5},{5,4},{6,7},{7,6},{8,9},{9,8},{10,11... | collective-permute-start | bytes 1769480 | tf_op jit(solution)/shard_map/ppermute | solution.py:216
  75.3 2.7 %fusion.3 = f32[144,8,144]{2,1,0:T(8,128)} fusion(f32[144,8,12]{2,1,0:T(8,128)} %copy.13, s32[144]{0:T(256)S(1)} %and_select_fusion.1), kind=kOutput, calls=%fused_computation.11 | convolution fusion | flops 23889600 | bytes 719424 | tf_op jit(solution)/shard_map/dnp,cp->dnc/dot_general | solution.py:58
  78.0 1.8 %shard_map.76 = (bf16[2,144,128]{2,1,0:T(8,128)(2,1)S(1)}, bf16[2,144,128]{2,1,0:T(8,128)(2,1)S(1)}, bf16[2,144,128]{2,1,0:T(8,128)(2,1)S(1)}, bf16[2,144,128]{2...) custom-call(f32[8,2,144,128]{3,2,1,0:T(8,128)S(1)} %copy-done.3, ...), custom_call_target="tpu_custom_call" | custom-call | tf_op jit(solution)/shard_map/pallas_call | solution.py:128
  79.8 1.9 %collective-permute-start.10 = (bf16[2,144,128]{2,1,0:T(8,128)(2,1)S(1)}, bf16[2,144,128]{2,1,0:T(8,128)(2,1)S(1)}, u32[]{:S(2)}, u32[]{:S(2)}) collective-permute-start(bf16[2,144,128]{2,1,0:T(8,128)(2,1)S(1)} %get-tuple-element.51), channel_id=1, source_target_pairs={{0,8},{2,10},{4,12},{6,14},{8,0},{10,2},{12,4},{14,6},{1,9},{3,11}... | collective-permute-start | bytes 221192 | tf_op jit(solution)/shard_map/ppermute | solution.py:194
  83.1 3.1 %collective-permute-start.12 = (bf16[2,144,128]{2,1,0:T(8,128)(2,1)S(1)}, bf16[2,144,128]{2,1,0:T(8,128)(2,1)S(1)}, u32[]{:S(2)}, u32[]{:S(2)}) collective-permute-start(bf16[2,144,128]{2,1,0:T(8,128)(2,1)S(1)} %get-tuple-element.53), channel_id=1, source_target_pairs={{0,10},{2,12},{4,14},{6,0},{8,2},{10,4},{12,6},{14,8},{1,11},{3,13... | collective-permute-start | bytes 221192 | tf_op jit(solution)/shard_map/ppermute | solution.py:194
  86.7 3.2 %collective-permute-start.14 = (bf16[2,144,128]{2,1,0:T(8,128)(2,1)}, bf16[2,144,128]{2,1,0:T(8,128)(2,1)S(1)}, u32[]{:S(2)}, u32[]{:S(2)}) collective-permute-start(bf16[2,144,128]{2,1,0:T(8,128)(2,1)} %get-tuple-element.55), channel_id=1, source_target_pairs={{0,12},{2,14},{4,0},{6,2},{8,4},{10,6},{12,8},{14,10},{1,13},{3,15... | collective-permute-start | bytes 221192 | tf_op jit(solution)/shard_map/ppermute | solution.py:194
  90.8 4.7 %collective-permute-done.11.refs_1_ = bf16[2,144,128]{2,1,0:T(8,128)(2,1)S(1)} collective-permute-done((bf16[2,144,128]{2,1,0:T(8,128)(2,1)S(1)}, bf16[2,144,128]{2,1,0:T(8,128)(2,1)S(1)}, u32[]{:S(2)}, u32[]{:S(2)}) %collective-permute-start.11) | collective-permute-done | bytes 73760 | tf_op jit(solution)/shard_map/ppermute | solution.py:194
  96.8 3.0 %collective-permute-start.28 = (bf16[2,144,128]{2,1,0:T(8,128)(2,1)S(1)}, bf16[2,144,128]{2,1,0:T(8,128)(2,1)S(1)}, u32[]{:S(2)}, u32[]{:S(2)}) collective-permute-start(bf16[2,144,128]{2,1,0:T(8,128)(2,1)S(1)} %get-tuple-element.70), channel_id=1, source_target_pairs={{0,6},{2,8},{4,10},{6,12},{8,14},{10,0},{12,2},{14,4},{1,7},{3,9},... | collective-permute-start | bytes 221192 | tf_op jit(solution)/shard_map/ppermute | solution.py:194
  100.4 1.5 %collective-permute-start.29 = (bf16[2,144,128]{2,1,0:T(8,128)(2,1)}, bf16[2,144,128]{2,1,0:T(8,128)(2,1)S(1)}, u32[]{:S(2)}, u32[]{:S(2)}) collective-permute-start(bf16[2,144,128]{2,1,0:T(8,128)(2,1)} %get-tuple-element.71), channel_id=1, source_target_pairs={{0,10},{2,12},{4,14},{6,0},{8,2},{10,4},{12,6},{14,8},{1,11},{3,13... | collective-permute-start | bytes 221192 | tf_op jit(solution)/shard_map/ppermute | solution.py:194
  103.0 2.5 %collective-permute-start.31 = (bf16[2,144,128]{2,1,0:T(8,128)(2,1)S(1)}, bf16[2,144,128]{2,1,0:T(8,128)(2,1)S(1)}, u32[]{:S(2)}, u32[]{:S(2)}) collective-permute-start(bf16[2,144,128]{2,1,0:T(8,128)(2,1)S(1)} %get-tuple-element.73), channel_id=1, source_target_pairs={{0,12},{2,14},{4,0},{6,2},{8,4},{10,6},{12,8},{14,10},{1,13},{3,15... | collective-permute-start | bytes 221192 | tf_op jit(solution)/shard_map/ppermute | solution.py:194
  105.7 5.7 %collective-permute-done.28.refs_9_ = bf16[2,144,128]{2,1,0:T(8,128)(2,1)S(1)} collective-permute-done((bf16[2,144,128]{2,1,0:T(8,128)(2,1)S(1)}, bf16[2,144,128]{2,1,0:T(8,128)(2,1)S(1)}, u32[]{:S(2)}, u32[]{:S(2)}) %collective-permute-start.28) | collective-permute-done | bytes 73760 | tf_op jit(solution)/shard_map/ppermute | solution.py:194
  111.3 1.9 %fusion = bf16[144,8,144]{2,1,0:T(8,128)(2,1)S(1)} fusion(f32[144,8,144]{2,1,0:T(8,128)} %fusion.3, f32[144,8,12]{2,1,0:T(8,128)S(1)} %copy.15, s32[144]{0:T(256)S(1)} %and_select_fusion), kind=kOutput, calls=%fused_computation.2 | convolution fusion | flops 24221376 | bytes 1051200 | tf_op jit(solution)/shard_map/dnp,cp->dnc/dot_general | solution.py:58
  113.8 16.7 %all_gather.3 = s32[2048,8]{0,1:T(8,128)S(1)} all-gather(s32[128,8]{0,1:T(8,128)S(1)} %copy-done.8), channel_id=1, replica_groups=mesh['energy'=16,'z'=8,'core'=2] {'z','core'}, dimensions={0}, use_global_device_ids=true | all-gather | bytes 69632 | tf_op jit(solution)/shard_map/all_gather | solution.py:209
  130.6 11.0 %shard_map.81 = bf16[2,144,2048]{2,1,0:T(8,128)(2,1)} custom-call(s32[1]{0:T(128)} %bitcast.z_ref, bf16[144,1152]{1,0:T(8,128)(2,1)S(1)} %convert_element_type.33.pair_ref, s32[8,2048]{1,0:T(8,128)S(1)} %bitcast.42, bf16[2,144,128]{2,1,0:T(8,128)(2,1)S(1)} %collective-permute-done.10.refs_0_, bf16[2,144,128]{2,1,0:T(8,128)(2,1)S(1)} %collective-permute-done.11.refs_1_, ...), custom_call_target="tpu_custom_call" | custom-call | tf_op jit(solution)/shard_map/pallas_call | solution.py:179
  (98 shorter events, 15.0 us)
Async XLA Ops:
  1.5 15.6 %collective-permute-start = (bf16[2,144,128]{2,1,0:T(8,128)(2,1)S(1)}, bf16[2,144,128]{2,1,0:T(8,128)(2,1)S(1)}, u32[]{:S(2)}, u32[]{:S(2)}) collective-permute-start(bf16[2,144,128]{2,1,0:T(8,128)(2,1)S(1)} %get-tuple-element.41), channel_id=1, source_target_pairs={{0,8},{2,10},{4,12},{6,14},{8,0},{10,2},{12,4},{14,6},{1,9},{3,11}... | collective-permute-start | bytes 221192 | tf_op jit(solution)/shard_map/ppermute | solution.py:194
  8.5 11.5 %collective-permute-start.1 = (bf16[2,144,128]{2,1,0:T(8,128)(2,1)S(1)}, bf16[2,144,128]{2,1,0:T(8,128)(2,1)S(1)}, u32[]{:S(2)}, u32[]{:S(2)}) collective-permute-start(bf16[2,144,128]{2,1,0:T(8,128)(2,1)S(1)} %get-tuple-element.42), channel_id=1, source_target_pairs={{0,6},{2,8},{4,10},{6,12},{8,14},{10,0},{12,2},{14,4},{1,7},{3,9},... | collective-permute-start | bytes 221192 | tf_op jit(solution)/shard_map/ppermute | solution.py:194
  10.1 9.9 %collective-permute-start.2 = (bf16[2,144,128]{2,1,0:T(8,128)(2,1)S(1)}, bf16[2,144,128]{2,1,0:T(8,128)(2,1)S(1)}, u32[]{:S(2)}, u32[]{:S(2)}) collective-permute-start(bf16[2,144,128]{2,1,0:T(8,128)(2,1)S(1)} %get-tuple-element.43), channel_id=1, source_target_pairs={{0,10},{2,12},{4,14},{6,0},{8,2},{10,4},{12,6},{14,8},{1,11},{3,13... | collective-permute-start | bytes 221192 | tf_op jit(solution)/shard_map/ppermute | solution.py:194
  13.0 9.4 %collective-permute-start.3 = (bf16[2,144,128]{2,1,0:T(8,128)(2,1)S(1)}, bf16[2,144,128]{2,1,0:T(8,128)(2,1)S(1)}, u32[]{:S(2)}, u32[]{:S(2)}) collective-permute-start(bf16[2,144,128]{2,1,0:T(8,128)(2,1)S(1)} %get-tuple-element.44), channel_id=1, source_target_pairs={{0,4},{2,6},{4,8},{6,10},{8,12},{10,14},{12,0},{14,2},{1,5},{3,7},... | collective-permute-start | bytes 221192 | tf_op jit(solution)/shard_map/ppermute | solution.py:194
  14.2 9.0 %collective-permute-start.4 = (bf16[2,144,128]{2,1,0:T(8,128)(2,1)S(1)}, bf16[2,144,128]{2,1,0:T(8,128)(2,1)S(1)}, u32[]{:S(2)}, u32[]{:S(2)}) collective-permute-start(bf16[2,144,128]{2,1,0:T(8,128)(2,1)S(1)} %get-tuple-element.45), channel_id=1, source_target_pairs={{0,12},{2,14},{4,0},{6,2},{8,4},{10,6},{12,8},{14,10},{1,13},{3,15... | collective-permute-start | bytes 221192 | tf_op jit(solution)/shard_map/ppermute | solution.py:194
  17.1 9.8 %collective-permute-start.5 = (bf16[2,144,128]{2,1,0:T(8,128)(2,1)S(1)}, bf16[2,144,128]{2,1,0:T(8,128)(2,1)S(1)}, u32[]{:S(2)}, u32[]{:S(2)}) collective-permute-start(bf16[2,144,128]{2,1,0:T(8,128)(2,1)S(1)} %get-tuple-element.46), channel_id=1, source_target_pairs={{0,2},{2,4},{4,6},{6,8},{8,10},{10,12},{12,14},{14,0},{1,3},{3,5},... | collective-permute-start | bytes 221192 | tf_op jit(solution)/shard_map/ppermute | solution.py:194
  20.1 10.7 %collective-permute-start.17 = (bf16[2,144,128]{2,1,0:T(8,128)(2,1)S(1)}, bf16[2,144,128]{2,1,0:T(8,128)(2,1)S(1)}, u32[]{:S(2)}, u32[]{:S(2)}) collective-permute-start(bf16[2,144,128]{2,1,0:T(8,128)(2,1)S(1)} %get-tuple-element.59), channel_id=1, source_target_pairs={{0,8},{2,10},{4,12},{6,14},{8,0},{10,2},{12,4},{14,6},{1,9},{3,11}... | collective-permute-start | bytes 221192 | tf_op jit(solution)/shard_map/ppermute | solution.py:194
  22.4 12.3 %collective-permute-start.18 = (bf16[2,144,128]{2,1,0:T(8,128)(2,1)S(1)}, bf16[2,144,128]{2,1,0:T(8,128)(2,1)S(1)}, u32[]{:S(2)}, u32[]{:S(2)}) collective-permute-start(bf16[2,144,128]{2,1,0:T(8,128)(2,1)S(1)} %get-tuple-element.60), channel_id=1, source_target_pairs={{0,6},{2,8},{4,10},{6,12},{8,14},{10,0},{12,2},{14,4},{1,7},{3,9},... | collective-permute-start | bytes 221192 | tf_op jit(solution)/shard_map/ppermute | solution.py:194
  23.2 11.5 %collective-permute-start.19 = (bf16[2,144,128]{2,1,0:T(8,128)(2,1)S(1)}, bf16[2,144,128]{2,1,0:T(8,128)(2,1)S(1)}, u32[]{:S(2)}, u32[]{:S(2)}) collective-permute-start(bf16[2,144,128]{2,1,0:T(8,128)(2,1)S(1)} %get-tuple-element.61), channel_id=1, source_target_pairs={{0,10},{2,12},{4,14},{6,0},{8,2},{10,4},{12,6},{14,8},{1,11},{3,13... | collective-permute-start | bytes 221192 | tf_op jit(solution)/shard_map/ppermute | solution.py:194
  26.9 10.6 %collective-permute-start.20 = (bf16[2,144,128]{2,1,0:T(8,128)(2,1)S(1)}, bf16[2,144,128]{2,1,0:T(8,128)(2,1)S(1)}, u32[]{:S(2)}, u32[]{:S(2)}) collective-permute-start(bf16[2,144,128]{2,1,0:T(8,128)(2,1)S(1)} %get-tuple-element.62), channel_id=1, source_target_pairs={{0,4},{2,6},{4,8},{6,10},{8,12},{10,14},{12,0},{14,2},{1,5},{3,7},... | collective-permute-start | bytes 221192 | tf_op jit(solution)/shard_map/ppermute | solution.py:194
  27.1 14.0 %collective-permute-start.21 = (bf16[2,144,128]{2,1,0:T(8,128)(2,1)S(1)}, bf16[2,144,128]{2,1,0:T(8,128)(2,1)S(1)}, u32[]{:S(2)}, u32[]{:S(2)}) collective-permute-start(bf16[2,144,128]{2,1,0:T(8,128)(2,1)S(1)} %get-tuple-element.63), channel_id=1, source_target_pairs={{0,12},{2,14},{4,0},{6,2},{8,4},{10,6},{12,8},{14,10},{1,13},{3,15... | collective-permute-start | bytes 221192 | tf_op jit(solution)/shard_map/ppermute | solution.py:194
  30.8 10.3 %collective-permute-start.22 = (bf16[2,144,128]{2,1,0:T(8,128)(2,1)S(1)}, bf16[2,144,128]{2,1,0:T(8,128)(2,1)S(1)}, u32[]{:S(2)}, u32[]{:S(2)}) collective-permute-start(bf16[2,144,128]{2,1,0:T(8,128)(2,1)S(1)} %get-tuple-element.64), channel_id=1, source_target_pairs={{0,2},{2,4},{4,6},{6,8},{8,10},{10,12},{12,14},{14,0},{1,3},{3,5},... | collective-permute-start | bytes 221192 | tf_op jit(solution)/shard_map/ppermute | solution.py:194
  34.7 25.0 %collective-permute-start.7 = (bf16[8,2,144,128]{3,2,1,0:T(8,128)(2,1)S(1)}, bf16[8,2,144,128]{3,2,1,0:T(8,128)(2,1)S(1)}, u32[]{:S(2)}, u32[]{:S(2)}) collective-permute-start(bf16[8,2,144,128]{3,2,1,0:T(8,128)(2,1)S(1)} %shard_map.74.own_ref), channel_id=1, source_target_pairs={{0,16},{16,32},{32,48},{48,64},{64,80},{80,96},{96,112},{112,128},... | collective-permute-start | bytes 1769480 | tf_op jit(solution)/shard_map/ppermute | solution.py:214
  37.5 22.2 %collective-permute-start.8 = (bf16[8,2,144,128]{3,2,1,0:T(8,128)(2,1)S(1)}, bf16[8,2,144,128]{3,2,1,0:T(8,128)(2,1)S(1)}, u32[]{:S(2)}, u32[]{:S(2)}) collective-permute-start(bf16[8,2,144,128]{3,2,1,0:T(8,128)(2,1)S(1)} %shard_map.74.own_ref), channel_id=1, source_target_pairs={{16,0},{32,16},{48,32},{64,48},{80,64},{96,80},{112,96},{128,112},... | collective-permute-start | bytes 1769480 | tf_op jit(solution)/shard_map/ppermute | solution.py:214
  41.2 25.0 %collective-permute-start.24 = (bf16[8,2,144,128]{3,2,1,0:T(8,128)(2,1)S(1)}, bf16[8,2,144,128]{3,2,1,0:T(8,128)(2,1)}, u32[]{:S(2)}, u32[]{:S(2)}) collective-permute-start(bf16[8,2,144,128]{3,2,1,0:T(8,128)(2,1)S(1)} %shard_map.78.own_ref), channel_id=1, source_target_pairs={{0,16},{16,32},{32,48},{48,64},{64,80},{80,96},{96,112},{112,128},... | collective-permute-start | bytes 1769480 | tf_op jit(solution)/shard_map/ppermute | solution.py:214
  46.1 20.1 %collective-permute-start.25 = (bf16[8,2,144,128]{3,2,1,0:T(8,128)(2,1)S(1)}, bf16[8,2,144,128]{3,2,1,0:T(8,128)(2,1)}, u32[]{:S(2)}, u32[]{:S(2)}) collective-permute-start(bf16[8,2,144,128]{3,2,1,0:T(8,128)(2,1)S(1)} %shard_map.78.own_ref), channel_id=1, source_target_pairs={{16,0},{32,16},{48,32},{64,48},{80,64},{96,80},{112,96},{128,112},... | collective-permute-start | bytes 1769480 | tf_op jit(solution)/shard_map/ppermute | solution.py:214
  62.5 15.5 %collective-permute-start.9 = (bf16[8,2,144,128]{3,2,1,0:T(8,128)(2,1)}, bf16[8,2,144,128]{3,2,1,0:T(8,128)(2,1)}, u32[]{:S(2)}, u32[]{:S(2)}) collective-permute-start(bf16[8,2,144,128]{3,2,1,0:T(8,128)(2,1)} %get-tuple-element.50), channel_id=1, source_target_pairs={{0,1},{1,0},{2,3},{3,2},{4,5},{5,4},{6,7},{7,6},{8,9},{9,8},{10,11... | collective-permute-start | bytes 1769480 | tf_op jit(solution)/shard_map/ppermute | solution.py:216
  70.3 16.4 %collective-permute-start.26 = (bf16[8,2,144,128]{3,2,1,0:T(8,128)(2,1)}, bf16[8,2,144,128]{3,2,1,0:T(8,128)(2,1)S(1)}, u32[]{:S(2)}, u32[]{:S(2)}) collective-permute-start(bf16[8,2,144,128]{3,2,1,0:T(8,128)(2,1)} %get-tuple-element.68), channel_id=1, source_target_pairs={{0,1},{1,0},{2,3},{3,2},{4,5},{5,4},{6,7},{7,6},{8,9},{9,8},{10,11... | collective-permute-start | bytes 1769480 | tf_op jit(solution)/shard_map/ppermute | solution.py:216
  79.8 10.9 %collective-permute-start.10 = (bf16[2,144,128]{2,1,0:T(8,128)(2,1)S(1)}, bf16[2,144,128]{2,1,0:T(8,128)(2,1)S(1)}, u32[]{:S(2)}, u32[]{:S(2)}) collective-permute-start(bf16[2,144,128]{2,1,0:T(8,128)(2,1)S(1)} %get-tuple-element.51), channel_id=1, source_target_pairs={{0,8},{2,10},{4,12},{6,14},{8,0},{10,2},{12,4},{14,6},{1,9},{3,11}... | collective-permute-start | bytes 221192 | tf_op jit(solution)/shard_map/ppermute | solution.py:194
  81.8 13.7 %collective-permute-start.11 = (bf16[2,144,128]{2,1,0:T(8,128)(2,1)S(1)}, bf16[2,144,128]{2,1,0:T(8,128)(2,1)S(1)}, u32[]{:S(2)}, u32[]{:S(2)}) collective-permute-start(bf16[2,144,128]{2,1,0:T(8,128)(2,1)S(1)} %get-tuple-element.52), channel_id=1, source_target_pairs={{0,6},{2,8},{4,10},{6,12},{8,14},{10,0},{12,2},{14,4},{1,7},{3,9},... | collective-permute-start | bytes 221192 | tf_op jit(solution)/shard_map/ppermute | solution.py:194
  83.1 12.4 %collective-permute-start.12 = (bf16[2,144,128]{2,1,0:T(8,128)(2,1)S(1)}, bf16[2,144,128]{2,1,0:T(8,128)(2,1)S(1)}, u32[]{:S(2)}, u32[]{:S(2)}) collective-permute-start(bf16[2,144,128]{2,1,0:T(8,128)(2,1)S(1)} %get-tuple-element.53), channel_id=1, source_target_pairs={{0,10},{2,12},{4,14},{6,0},{8,2},{10,4},{12,6},{14,8},{1,11},{3,13... | collective-permute-start | bytes 221192 | tf_op jit(solution)/shard_map/ppermute | solution.py:194
  86.2 10.6 %collective-permute-start.13 = (bf16[2,144,128]{2,1,0:T(8,128)(2,1)S(1)}, bf16[2,144,128]{2,1,0:T(8,128)(2,1)S(1)}, u32[]{:S(2)}, u32[]{:S(2)}) collective-permute-start(bf16[2,144,128]{2,1,0:T(8,128)(2,1)S(1)} %get-tuple-element.54), channel_id=1, source_target_pairs={{0,4},{2,6},{4,8},{6,10},{8,12},{10,14},{12,0},{14,2},{1,5},{3,7},... | collective-permute-start | bytes 221192 | tf_op jit(solution)/shard_map/ppermute | solution.py:194
  86.7 13.7 %collective-permute-start.14 = (bf16[2,144,128]{2,1,0:T(8,128)(2,1)}, bf16[2,144,128]{2,1,0:T(8,128)(2,1)S(1)}, u32[]{:S(2)}, u32[]{:S(2)}) collective-permute-start(bf16[2,144,128]{2,1,0:T(8,128)(2,1)} %get-tuple-element.55), channel_id=1, source_target_pairs={{0,12},{2,14},{4,0},{6,2},{8,4},{10,6},{12,8},{14,10},{1,13},{3,15... | collective-permute-start | bytes 221192 | tf_op jit(solution)/shard_map/ppermute | solution.py:194
  90.7 11.2 %collective-permute-start.15 = (bf16[2,144,128]{2,1,0:T(8,128)(2,1)}, bf16[2,144,128]{2,1,0:T(8,128)(2,1)S(1)}, u32[]{:S(2)}, u32[]{:S(2)}) collective-permute-start(bf16[2,144,128]{2,1,0:T(8,128)(2,1)} %get-tuple-element.56), channel_id=1, source_target_pairs={{0,2},{2,4},{4,6},{6,8},{8,10},{10,12},{12,14},{14,0},{1,3},{3,5},... | collective-permute-start | bytes 221192 | tf_op jit(solution)/shard_map/ppermute | solution.py:194
  95.5 7.5 %collective-permute-start.16 = (bf16[2,144,128]{2,1,0:T(8,128)(2,1)S(1)}, bf16[2,144,128]{2,1,0:T(8,128)(2,1)S(1)}, u32[]{:S(2)}, u32[]{:S(2)}) collective-permute-start(bf16[2,144,128]{2,1,0:T(8,128)(2,1)S(1)} %get-tuple-element.57), channel_id=1, source_target_pairs={{0,14},{2,0},{4,2},{6,4},{8,6},{10,8},{12,10},{14,12},{1,15},{3,1}... | collective-permute-start | bytes 221192 | tf_op jit(solution)/shard_map/ppermute | solution.py:194
  95.5 10.0 %collective-permute-start.27 = (bf16[2,144,128]{2,1,0:T(8,128)(2,1)S(1)}, bf16[2,144,128]{2,1,0:T(8,128)(2,1)S(1)}, u32[]{:S(2)}, u32[]{:S(2)}) collective-permute-start(bf16[2,144,128]{2,1,0:T(8,128)(2,1)S(1)} %get-tuple-element.69), channel_id=1, source_target_pairs={{0,8},{2,10},{4,12},{6,14},{8,0},{10,2},{12,4},{14,6},{1,9},{3,11}... | collective-permute-start | bytes 221192 | tf_op jit(solution)/shard_map/ppermute | solution.py:194
  96.8 14.5 %collective-permute-start.28 = (bf16[2,144,128]{2,1,0:T(8,128)(2,1)S(1)}, bf16[2,144,128]{2,1,0:T(8,128)(2,1)S(1)}, u32[]{:S(2)}, u32[]{:S(2)}) collective-permute-start(bf16[2,144,128]{2,1,0:T(8,128)(2,1)S(1)} %get-tuple-element.70), channel_id=1, source_target_pairs={{0,6},{2,8},{4,10},{6,12},{8,14},{10,0},{12,2},{14,4},{1,7},{3,9},... | collective-permute-start | bytes 221192 | tf_op jit(solution)/shard_map/ppermute | solution.py:194
  100.4 30.1 %collective-permute-start.29 = (bf16[2,144,128]{2,1,0:T(8,128)(2,1)}, bf16[2,144,128]{2,1,0:T(8,128)(2,1)S(1)}, u32[]{:S(2)}, u32[]{:S(2)}) collective-permute-start(bf16[2,144,128]{2,1,0:T(8,128)(2,1)} %get-tuple-element.71), channel_id=1, source_target_pairs={{0,10},{2,12},{4,14},{6,0},{8,2},{10,4},{12,6},{14,8},{1,11},{3,13... | collective-permute-start | bytes 221192 | tf_op jit(solution)/shard_map/ppermute | solution.py:194
  101.9 28.6 %collective-permute-start.30 = (bf16[2,144,128]{2,1,0:T(8,128)(2,1)S(1)}, bf16[2,144,128]{2,1,0:T(8,128)(2,1)S(1)}, u32[]{:S(2)}, u32[]{:S(2)}) collective-permute-start(bf16[2,144,128]{2,1,0:T(8,128)(2,1)S(1)} %get-tuple-element.72), channel_id=1, source_target_pairs={{0,4},{2,6},{4,8},{6,10},{8,12},{10,14},{12,0},{14,2},{1,5},{3,7},... | collective-permute-start | bytes 221192 | tf_op jit(solution)/shard_map/ppermute | solution.py:194
  103.0 27.5 %collective-permute-start.31 = (bf16[2,144,128]{2,1,0:T(8,128)(2,1)S(1)}, bf16[2,144,128]{2,1,0:T(8,128)(2,1)S(1)}, u32[]{:S(2)}, u32[]{:S(2)}) collective-permute-start(bf16[2,144,128]{2,1,0:T(8,128)(2,1)S(1)} %get-tuple-element.73), channel_id=1, source_target_pairs={{0,12},{2,14},{4,0},{6,2},{8,4},{10,6},{12,8},{14,10},{1,13},{3,15... | collective-permute-start | bytes 221192 | tf_op jit(solution)/shard_map/ppermute | solution.py:194
  105.5 25.1 %collective-permute-start.32 = (bf16[2,144,128]{2,1,0:T(8,128)(2,1)S(1)}, bf16[2,144,128]{2,1,0:T(8,128)(2,1)S(1)}, u32[]{:S(2)}, u32[]{:S(2)}) collective-permute-start(bf16[2,144,128]{2,1,0:T(8,128)(2,1)S(1)} %get-tuple-element.74), channel_id=1, source_target_pairs={{0,2},{2,4},{4,6},{6,8},{8,10},{10,12},{12,14},{14,0},{1,3},{3,5},... | collective-permute-start | bytes 221192 | tf_op jit(solution)/shard_map/ppermute | solution.py:194
  111.3 19.2 %collective-permute-start.33 = (bf16[2,144,128]{2,1,0:T(8,128)(2,1)S(1)}, bf16[2,144,128]{2,1,0:T(8,128)(2,1)S(1)}, u32[]{:S(2)}, u32[]{:S(2)}) collective-permute-start(bf16[2,144,128]{2,1,0:T(8,128)(2,1)S(1)} %get-tuple-element.75), channel_id=1, source_target_pairs={{0,14},{2,0},{4,2},{6,4},{8,6},{10,8},{12,10},{14,12},{1,15},{3,1}... | collective-permute-start | bytes 221192 | tf_op jit(solution)/shard_map/ppermute | solution.py:194
  (14 other events, 188.3 us)

commit v2 on v0

v2 whole, which is shorter than its diff:
```python
import functools

import jax
import jax.numpy as jnp
import numpy as np
from jax import lax
from jax.experimental import pallas as pl
from jax.experimental.pallas import tpu as pltpu
from jax.sharding import Mesh
from jax.sharding import PartitionSpec as P

OFFSET = 2
TAPS = 2 * OFFSET + 1
CHUNKS = 2
ROWS = 16
LANES = 128
SPAN = 2 * LANES
PAD = LANES // 2
KMOM = ("z", "core")
VMEM = pl.BlockSpec(memory_space=pltpu.VMEM)
SMEM = pl.BlockSpec(memory_space=pltpu.SMEM)
BF16, F32 = jnp.bfloat16, jnp.float32

NEAR = (1, 2, 3)
PLACES = tuple((j, other) for j in NEAR for other in (0, 1)) + ((4, 0), (0, 0))


def call(kernel, outs, *args, scratch=(), cost=None):
    return pl.pallas_call(
        kernel,
        out_shape=[jax.ShapeDtypeStruct(shape, dtype) for shape, dtype in outs],
        in_specs=[SMEM if a.ndim == 1 else VMEM for a in args],
        out_specs=[VMEM] * len(outs),
        scratch_shapes=[pltpu.VMEM(shape, dtype) for shape, dtype in scratch],
        compiler_params=pltpu.CompilerParams(vmem_limit_bytes=40 * 2**20),
    )(*args)


def mixing_index(e_dev):
    rel = np.zeros((e_dev, 2, 8, 3, 8, e_dev), np.int32)
    mom = np.zeros_like(rel)
    for e_out in range(e_dev):
        for tile in range(3):
            for e_in in range(e_dev):
                rel[e_out, :, :, tile, :, e_in] = (tile - 1) * e_dev + e_in - e_out + OFFSET
    for d, (j_to, to_other) in enumerate(PLACES):
        for s, (j_from, from_other) in enumerate(PLACES):
            mom[:, 0, d, :, s, :] = 2 * (j_to + j_from) + to_other - from_other
            mom[:, 1, d, :, s, :] = 2 * (j_from - j_to) + 1 - to_other - from_other
    return rel.reshape(e_dev * 16, -1), mom.reshape(e_dev * 16, -1)


def tables_kernel(moms, pos_ref, offsets_ref, phonon_ref, coupling_ref, rel_ref, mom_ref, first_ref, second_ref,
                  wide_first_ref, wide_second_ref, mix_ref, pair_ref):
    slots = coupling_ref.shape[0]
    taps = jnp.zeros((8, moms), F32)
    row = lax.broadcasted_iota(jnp.int32, (8, moms), 0)
    for s in range(2):
        for w in range(phonon_ref.shape[1]):
            hit = row == (2 * s - 1) * offsets_ref[w] + OFFSET
            taps = taps + jnp.where(hit, phonon_ref[s, w : w + 1, :], 0.0)
    taps = taps.astype(BF16).astype(F32)
    rel, mom = rel_ref[...], (mom_ref[...] * pos_ref[1]) & (moms - 1)
    table = jnp.zeros(rel.shape, F32)
    for r in range(TAPS):
        for q in range(moms):
            table = jnp.where((rel == r) & (mom == q), taps[r : r + 1, q : q + 1], table)
    outs, ins = table.shape
    tall = (lax.broadcasted_iota(jnp.int32, (outs * ROWS, outs), 0) >> 4) == lax.broadcasted_iota(
        jnp.int32, (outs * ROWS, outs), 1)
    flat = lax.broadcasted_iota(jnp.int32, (ins, ins * ROWS), 0) == (
        lax.broadcasted_iota(jnp.int32, (ins, ins * ROWS), 1) >> 4)
    half = jnp.dot(tall.astype(BF16), table.astype(BF16), preferred_element_type=F32).astype(BF16)
    full = jnp.dot(half, flat.astype(BF16), preferred_element_type=F32)
    same = (lax.broadcasted_iota(jnp.int32, full.shape, 0) & (ROWS - 1)) == (
        lax.broadcasted_iota(jnp.int32, full.shape, 1) & (ROWS - 1))
    mix_ref[...] = jnp.where(same, full, 0.0).astype(BF16)
    bonds = jnp.concatenate([coupling_ref[n] for n in range(slots)], axis=1)

    def spread(tall_ref, wide_ref):
        half = jnp.dot(tall_ref[...], bonds, precision=lax.Precision.HIGHEST, preferred_element_type=F32)
        return jnp.dot(half, wide_ref[...], precision=lax.Precision.HIGHEST, preferred_element_type=F32)

    pair_ref[...] = (spread(first_ref, wide_first_ref) * spread(second_ref, wide_second_ref)).astype(BF16)


def tables(pos, phonon, offsets, coupling, e_dev):
    slots, orbs = coupling.shape[0], coupling.shape[1]
    moms = phonon.shape[2]
    rel, mom = mixing_index(e_dev)
    pairs = np.arange(orbs * orbs)
    picks = [(index[:, None] == np.arange(orbs)).astype(np.float32) for index in (pairs // orbs, pairs % orbs)]
    wide = [np.kron(np.eye(slots, dtype=np.float32), pick.T) for pick in picks]
    return call(
        functools.partial(tables_kernel, moms),
        [((rel.shape[0] * ROWS, rel.shape[1] * ROWS), BF16), ((orbs * orbs, slots * orbs * orbs), BF16)],
        pos, offsets, phonon, coupling, *map(jnp.asarray, (rel, mom, *picks, *wide)),
    )


def cut_kernel(chunk, groups, pos_ref, green_ref, *refs):
    extra, (own_ref, give_ref, far_ref, home_ref) = refs[:-4], refs[-4:]
    e_dev, pairs, _ = green_ref.shape
    rows = e_dev * pairs

    def put(ref, at, distance):
        group = (pos_ref[0] + distance) & (groups - 1)
        start = pl.multiple_of((chunk * groups + group) * LANES, LANES)
        ref[at, 0:rows, :] = green_ref[:, :, pl.ds(start, LANES)].reshape(rows, LANES)
        for near in extra:
            ref[at, rows:, :] = near[...]

    for i, j in enumerate(NEAR):
        put(own_ref, i, pos_ref[1] * j)
        put(give_ref, i, -pos_ref[1] * j)
    put(far_ref, 0, 4)
    put(home_ref, 0, 0)


def cut(pos, green, chunk, groups, *extra):
    height = green.shape[0] * green.shape[1] + sum(x.shape[0] for x in extra)
    return call(
        functools.partial(cut_kernel, chunk, groups),
        [((n, height, LANES), BF16) for n in (len(NEAR), len(NEAR), 1, 1)],
        pos, green, *extra,
    )


def merge_kernel(own_ref, got_ref, *out_refs):
    for i, out in enumerate(out_refs):
        out[0] = own_ref[i]
        out[1] = got_ref[i]


def merge(own, got):
    return call(merge_kernel, [((2, *own.shape[1:]), BF16)] * len(NEAR), own, got)


def stack_kernel(rows, *refs):
    blocks, outs = refs[: len(NEAR) + 2], refs[len(NEAR) + 2 :]
    at = 0
    for block in blocks:
        for i in range(block.shape[0]):
            outs[0][at] = block[i, 0:rows, :]
            for out in outs[1:]:
                out[at] = block[i, rows:, :]
            at += 1


def stack(blocks, rows):
    height = blocks[0].shape[1]
    outs = [((len(PLACES), h, LANES), BF16) for h in (rows, height - rows) if h]
    return call(functools.partial(stack_kernel, rows), outs, *blocks)


def mix_kernel(e_dev, mix_ref, low_ref, own_ref, high_ref, kept_ref, other_ref):
    places, height, width = own_ref.shape
    for g in range(height // e_dev // ROWS):
        tiles = []
        for ref in (low_ref, own_ref, high_ref):
            for i in range(places):
                for e in range(e_dev):
                    tiles.append(ref[i, pl.ds((e * (height // e_dev)) + g * ROWS, ROWS), :])
        mixed = jnp.dot(mix_ref[...], jnp.concatenate(tiles, axis=0), preferred_element_type=F32)
        mixed = mixed.reshape(e_dev, 2, places, ROWS, width)
        for e in range(e_dev):
            rows = pl.ds(e * (height // e_dev) + g * ROWS, ROWS)
            kept_ref[:, rows, :] = mixed[e, 0]
            other_ref[:, rows, :] = mixed[e, 1].astype(BF16)


def mix(matrix, low, own, high, e_dev):
    return call(functools.partial(mix_kernel, e_dev), [(own.shape, F32), (own.shape, BF16)], matrix, low, own, high)


def add_kernel(kept_ref, got_ref, *out_refs):
    at = 0
    for out in out_refs:
        for i in range(out.shape[0]):
            out[i] = (kept_ref[at] + got_ref[at].astype(F32)).astype(BF16)
            at += 1


def add(kept, got):
    return call(add_kernel, [((n, *kept.shape[1:]), BF16) for n in (2, 2, 2, 1, 1)], kept, got)


def pick_kernel(*refs):
    blocks, extra, out = refs[: len(NEAR)], refs[len(NEAR) : -1], refs[-1]
    rows = blocks[0].shape[1]
    for i, block in enumerate(blocks):
        out[i * rows : (i + 1) * rows, :] = block[1]
    at = len(NEAR) * rows
    for near in extra:
        for i in range(near.shape[0]):
            out[at : at + near.shape[1], :] = near[i]
            at += near.shape[1]


def pick(blocks, *extra):
    height = len(NEAR) * blocks[0].shape[1] + sum(x.shape[0] * x.shape[1] for x in extra)
    return call(pick_kernel, [((height, LANES), BF16)], *blocks[: len(NEAR)], *extra)[0]


def couple_kernel(groups, slots, pos_ref, pair_ref, near_ref, *refs):
    fields, (out_ref, line, seen, nears) = refs[:-4], refs[-4:]
    e_dev, pairs, atoms = out_ref.shape
    rows = e_dev * pairs
    z, way = pos_ref[0], pos_ref[1]
    core = (1 - way) >> 1

    def rank(distance, parity):
        return 2 * ((z + distance) & (groups - 1)) + parity

    given = fields[len(NEAR) + 2]
    at = len(NEAR) * rows
    for i, (j, other) in enumerate(PLACES):
        nears[rank(-way * j, core + way * other)] = near_ref[i]
        nears[rank(way * j, core + way - way * other)] = given[at : at + ROWS, :]
        at += ROWS
    line[:, 0:LANES] = jnp.zeros((rows, LANES), BF16)
    line[:, atoms : atoms + LANES] = jnp.zeros((rows, LANES), BF16)
    for chunk in range(CHUNKS):
        part = fields[chunk * (len(NEAR) + 3) :]

        def put(block, distance):
            group = (z + distance) & (groups - 1)
            seen[:, pl.ds(pl.multiple_of((chunk * groups + group) * LANES, LANES), LANES)] = block

        for i, j in enumerate(NEAR):
            put(part[i][0], -way * j)
            put(part[len(NEAR) + 2][i * rows : (i + 1) * rows, :], way * j)
        put(part[len(NEAR)][0], 4)
        put(part[len(NEAR) + 1][0], 0)
    line[:, PAD : PAD + atoms] = seen[...]
    place = lax.broadcasted_iota(jnp.int32, (SPAN, LANES), 0) - lax.broadcasted_iota(jnp.int32, (SPAN, LANES), 1) - PAD

    def step(b, carry):
        start = pl.multiple_of(b * LANES, LANES)
        window = line[:, pl.ds(start, SPAN)]
        near = nears[b].astype(F32).astype(jnp.int32)
        hits = [(place == near[n : n + 1, :]).astype(BF16) for n in range(slots)]
        taken = jnp.dot(window, jnp.concatenate(hits, axis=1), preferred_element_type=F32).astype(BF16)
        columns = [
            jnp.concatenate([taken[e * pairs : (e + 1) * pairs, n * LANES : (n + 1) * LANES] for n in range(slots)], axis=0)
            for e in range(e_dev)
        ]
        total = jnp.dot(pair_ref[...], jnp.concatenate(columns, axis=1), preferred_element_type=F32)
        for e in range(e_dev):
            out_ref[e, :, pl.ds(start, LANES)] = total[:, e * LANES : (e + 1) * LANES].astype(BF16)
        return carry

    lax.fori_loop(0, atoms // LANES, step, 0, unroll=4)


def couple(pos, pair_maps, near, fields, groups, slots, shape):
    rows = shape[0] * shape[1]
    return call(
        functools.partial(couple_kernel, groups, slots),
        [(shape, BF16)],
        pos, pair_maps, near, *fields,
        scratch=[((rows, shape[2] + LANES), BF16), ((rows, shape[2]), BF16), ((2 * groups, ROWS, LANES), BF16)],
    )[0]


def swap(x):
    return lax.ppermute(x, "core", [(0, 1), (1, 0)])


def round_ring(x, j):
    groups = lax.axis_size("z")
    pairs = [(2 * z + c, 2 * ((z + (j if c == 0 else -j)) % groups) + c) for z in range(groups) for c in range(2)]
    return lax.ppermute(x, KMOM, pairs)


def exchange(blocks):
    far = round_ring(blocks[len(NEAR)], 4)
    near = [round_ring(blocks[i], j) for i, j in reversed(list(enumerate(NEAR)))]
    return [*reversed(near), far, blocks[len(NEAR) + 1]]


def body(green_blocks, phonon, offsets, neighbours, coupling):
    groups, tiles = lax.axis_size("z"), lax.axis_size("energy")
    green = green_blocks[:, 0]
    e_dev, pairs, atoms = green.shape
    rows = e_dev * pairs
    slots = neighbours.shape[1]
    core = lax.axis_index("core")
    pos = jnp.stack([lax.axis_index("z"), 1 - 2 * core])
    forward = [(i, i + 1) for i in range(tiles - 1)]
    backward = [(i + 1, i) for i in range(tiles - 1)]
    atom = lax.axis_index(KMOM) * LANES + jnp.arange(LANES, dtype=jnp.int32)
    steps = (neighbours - atom[:, None]).T.astype(BF16)
    steps = jnp.concatenate([steps, jnp.zeros((ROWS - slots, LANES), BF16)], axis=0)
    arrived = []
    for chunk, extra in ((0, ()), (1, (steps,))):
        own, give, far, home = cut(pos, green, chunk, groups, *extra)
        arrived.append(exchange([*merge(own, swap(give)), far, home]))
    matrix, pair_maps = tables(pos, phonon, offsets, coupling, e_dev)
    stacks = [stack(arrived[0], rows), stack(arrived[1], rows)]
    near = stacks[1][1]
    fields = []
    for chunk in range(CHUNKS):
        own = stacks[chunk][0]
        low, high = lax.ppermute(own, "energy", forward), lax.ppermute(own, "energy", backward)
        kept, other = mix(matrix, low, own, high, e_dev)
        back = exchange(add(kept, swap(other)))
        fields += [*back, swap(pick(back, *((near,) if chunk == 0 else ())))]
    return couple(pos, pair_maps, near, fields, groups, slots, green.shape)[:, None]


def solution(mesh):
    torus = Mesh(mesh.devices.reshape(mesh.shape["energy"], -1, 2), ("energy", *KMOM))
    placed = (P("energy", KMOM, None, None), P(), P(), P(KMOM, None), P())
    return jax.shard_map(body, mesh=torus, in_specs=placed, out_specs=P("energy", KMOM, None, None), check_vma=False)
```

time: 180 us -> 115 us (0.64)
  starting transfers between devices: 18.1 us -> 66.6 us
  blocking collectives: 45.6 us -> 0 us
  local copies, waits for them, and re-layouts: 37.3 us -> 1.34 us
  matrix products: 22.4 us -> 0 us
  waiting for transfers between devices: 46.3 us -> 28.7 us
  Pallas kernels: 0 us -> 16.6 us
  other arithmetic: 9.27 us -> 0.08 us
    ppermute x4 -> x26, starting transfers between devices: 9.87 us -> 66.6 us  [the longest x16 35.3 us: round_ring(): return lax.ppermute(x, KMOM, pairs)]
    all_to_all x2 -> x0, blocking collectives: 45.6 us -> none  [the longest x1 40.6 us: body(): lax.all_to_all(local_sigma, KMOM, split_axis=1, concat_axis=3, tiled=True)]
    dot_general x12 -> x0, matrix products: 22.4 us -> none  [the longest x8 20.9 us: neighbour_sum(): jnp.einsum('emca,dc->emda', taken, pair_maps[slot], preferred_element_typ...]
    all_to_all x1 -> x0, waiting for transfers between devices: 17.3 us -> none  [exchange_in_order(): lax.all_to_all(tiles, axes[k], split_axis=k, concat_axis=k, tiled=True)]
    pallas_call x0 -> x14, Pallas kernels: none -> 16.6 us  [call(): pl.pallas_call(kernel, out_shape=[jax.ShapeDtypeStruct(shape, dtype) for...]
    gather x8 -> x0, local copies, waits for them, and re-layouts: 16.2 us -> none  [neighbour_sum(): taken = jnp.take(source, atom_index[:, slot], axis=3)]
    squeeze x8 -> x0, local copies, waits for them, and re-layouts: 11 us -> none  [neighbour_sum(): pair_maps[slot]]
    all_to_all x1 -> x0, starting transfers between devices: 8.19 us -> none  [exchange_in_order(): lax.all_to_all(tiles, axes[k], split_axis=k, concat_axis=k, tiled=True)]
  transfers between devices with their start and end apart: 5 -> 26, of which waited for: 5 -> 9; matrix products, arithmetic and copies ran while one was open for 10% -> 0% of each run, Pallas kernels for 0% -> 7%
where the time goes in v2:
time: 115 us; the launch traced here: 114 us
  starting transfers between devices  66.6 us (58%)
  waiting for transfers between devices  28.7 us (25%)
  Pallas kernels  16.6 us (14%)
  local copies, waits for them, and re-layouts  1.34 us (1%)
    ppermute x16, starting transfers between devices, round_ring(): return lax.ppermute(x, KMOM, pairs)  35.3 us
    ppermute x16, waiting for transfers between devices, round_ring(): return lax.ppermute(x, KMOM, pairs)  23.8 us
    ppermute x6, starting transfers between devices, swap(): return lax.ppermute(x, 'core', [(0, 1), (1, 0)])  20.8 us
    pallas_call x14, Pallas kernels, call(): pl.pallas_call(kernel, out_shape=[jax.ShapeDtypeStruct(shape, dtype) for...  16.6 us
    ppermute x2, starting transfers between devices, body(): lax.ppermute(own, 'energy', forward)  5.56 us
    ppermute x2, starting transfers between devices, body(): lax.ppermute(own, 'energy', backward)  5.01 us
    ppermute x2, waiting for transfers between devices, body(): lax.ppermute(own, 'energy', backward)  4.89 us
  transfers between devices with their start and end apart: 26, of which 9 were waited for; matrix products, arithmetic and copies ran while one was open for 0% of the time, Pallas kernels for 7%

profile of v2, /device:TPU:25, one launch (start us, length us, event | category | flops | bytes accessed | tf_op | source)
XLA Modules:
  0.0 113.8 jit_solution(14637754639632569594)
XLA Ops:
  0.1 1.3 %copy-done = bf16[2,1,144,2048]{3,2,1,0:T(8,128)(2,1)S(1)} copy-done((bf16[2,1,144,2048]{3,2,1,0:T(8,128)(2,1)S(1)}, bf16[2,1,144,2048]{3,2,1,0:T(8,128)(2,1)}, u32[]{:S(2)}) %copy-start) | copy-done | bytes 1179672
  2.1 0.8 collective-permute-start.5
  4.1 5.7 %collective-permute-start.6 = (bf16[2,288,128]{2,1,0:T(8,128)(2,1)S(1)}, bf16[2,288,128]{2,1,0:T(8,128)(2,1)S(1)}, u32[]{:S(2)}, u32[]{:S(2)}) collective-permute-start(bf16[2,288,128]{2,1,0:T(8,128)(2,1)S(1)} %get-tuple-element.49), channel_id=1, source_target_pairs={{0,2},{1,15},{2,4},{3,1},{4,6},{5,3},{6,8},{7,5},{8,10},{9,7},{10,... | collective-permute-start | bytes 442376 | tf_op jit(solution)/shard_map/ppermute | solution.py:273
  9.8 1.2 %collective-permute-start.7 = (bf16[2,288,128]{2,1,0:T(8,128)(2,1)S(1)}, bf16[2,288,128]{2,1,0:T(8,128)(2,1)S(1)}, u32[]{:S(2)}, u32[]{:S(2)}) collective-permute-start(bf16[2,288,128]{2,1,0:T(8,128)(2,1)S(1)} %get-tuple-element.50), channel_id=1, source_target_pairs={{0,4},{1,13},{2,6},{3,15},{4,8},{5,1},{6,10},{7,3},{8,12},{9,5},{1... | collective-permute-start | bytes 442376 | tf_op jit(solution)/shard_map/ppermute | solution.py:273
  11.4 4.5 %collective-permute-start.9 = (bf16[1,288,128]{2,1,0:T(8,128)(2,1)S(1)}, bf16[1,288,128]{2,1,0:T(8,128)(2,1)S(1)}, u32[]{:S(2)}, u32[]{:S(2)}) collective-permute-start(bf16[1,288,128]{2,1,0:T(8,128)(2,1)S(1)} %get-tuple-element.52), channel_id=1, source_target_pairs={{0,8},{1,9},{2,10},{3,11},{4,12},{5,13},{6,14},{7,15},{8,0},{9,1},... | collective-permute-start | bytes 221192 | tf_op jit(solution)/shard_map/ppermute | solution.py:273
  15.9 0.9 collective-permute-start.4
  16.9 6.0 %collective-permute-done.9.refs_3_ = bf16[1,288,128]{2,1,0:T(8,128)(2,1)S(1)} collective-permute-done((bf16[1,288,128]{2,1,0:T(8,128)(2,1)S(1)}, bf16[1,288,128]{2,1,0:T(8,128)(2,1)S(1)}, u32[]{:S(2)}, u32[]{:S(2)}) %collective-permute-start.9) | collective-permute-done | bytes 73760 | tf_op jit(solution)/shard_map/ppermute | solution.py:273
  22.9 8.0 %collective-permute-start.2 = (bf16[2,304,128]{2,1,0:T(8,128)(2,1)S(1)}, bf16[2,304,128]{2,1,0:T(8,128)(2,1)S(1)}, u32[]{:S(2)}, u32[]{:S(2)}) collective-permute-start(bf16[2,304,128]{2,1,0:T(8,128)(2,1)S(1)} %get-tuple-element.41), channel_id=1, source_target_pairs={{0,4},{1,13},{2,6},{3,15},{4,8},{5,1},{6,10},{7,3},{8,12},{9,5},{1... | collective-permute-start | bytes 466952 | tf_op jit(solution)/shard_map/ppermute | solution.py:273
  30.9 2.8 %collective-permute-start.10 = (bf16[8,288,128]{2,1,0:T(8,128)(2,1)S(1)}, bf16[8,288,128]{2,1,0:T(8,128)(2,1)S(1)}, u32[]{:S(2)}, u32[]{:S(2)}) collective-permute-start(bf16[8,288,128]{2,1,0:T(8,128)(2,1)S(1)} %shard_map.115.own_ref), channel_id=1, source_target_pairs={{0,16},{16,32},{32,48},{48,64},{64,80},{80,96},{96,112},{112,128},... | collective-permute-start | bytes 1769480 | tf_op jit(solution)/shard_map/ppermute | solution.py:305
  33.7 2.5 %collective-permute-start.11 = (bf16[8,288,128]{2,1,0:T(8,128)(2,1)S(1)}, bf16[8,288,128]{2,1,0:T(8,128)(2,1)S(1)}, u32[]{:S(2)}, u32[]{:S(2)}) collective-permute-start(bf16[8,288,128]{2,1,0:T(8,128)(2,1)S(1)} %shard_map.115.own_ref), channel_id=1, source_target_pairs={{16,0},{32,16},{48,32},{64,48},{80,64},{96,80},{112,96},{128,112},... | collective-permute-start | bytes 1769480 | tf_op jit(solution)/shard_map/ppermute | solution.py:305
  36.2 1.1 collective-permute-done.2.refs_1_
  37.3 3.6 %collective-permute-done.3.refs_2_ = bf16[2,304,128]{2,1,0:T(8,128)(2,1)S(1)} collective-permute-done((bf16[2,304,128]{2,1,0:T(8,128)(2,1)S(1)}, bf16[2,304,128]{2,1,0:T(8,128)(2,1)S(1)}, u32[]{:S(2)}, u32[]{:S(2)}) %collective-permute-start.3) | collective-permute-done | bytes 155680 | tf_op jit(solution)/shard_map/ppermute | solution.py:273
  41.0 2.8 %collective-permute-start.18 = (bf16[8,288,128]{2,1,0:T(8,128)(2,1)S(1)}, bf16[8,288,128]{2,1,0:T(8,128)(2,1)S(1)}, u32[]{:S(2)}, u32[]{:S(2)}) collective-permute-start(bf16[8,288,128]{2,1,0:T(8,128)(2,1)S(1)} %get-tuple-element.61.own_ref), channel_id=1, source_target_pairs={{0,16},{16,32},{32,48},{48,64},{64,80},{80,96},{96,112},{112,128},... | collective-permute-start | bytes 1769480 | tf_op jit(solution)/shard_map/ppermute | solution.py:305
  43.7 2.5 %collective-permute-start.19 = (bf16[8,288,128]{2,1,0:T(8,128)(2,1)S(1)}, bf16[8,288,128]{2,1,0:T(8,128)(2,1)S(1)}, u32[]{:S(2)}, u32[]{:S(2)}) collective-permute-start(bf16[8,288,128]{2,1,0:T(8,128)(2,1)S(1)} %get-tuple-element.61.own_ref), channel_id=1, source_target_pairs={{16,0},{32,16},{48,32},{64,48},{80,64},{96,80},{112,96},{128,112},... | collective-permute-start | bytes 1769480 | tf_op jit(solution)/shard_map/ppermute | solution.py:305
  46.4 2.7 %shard_map.109 = (bf16[512,768]{1,0:T(8,128)(2,1)S(1)}, bf16[144,1152]{1,0:T(8,128)(2,1)S(1)}) custom-call(s32[2]{0:T(128)S(1)} %pad_add_fusion.pos_ref, s32[8]{0:T(128)S(1)} %copy-done.9, f32[2,8,16]{2,1,0:T(8,128)S(1)} %copy-done.8, f32[8,12,12]{2,1,0:T(8,128)S(1)} %copy.12.coupling_ref, s32[32,48]{1,0:T(8,128)S(1)} %copy-done.6, s32[32,48]{1,0:T(8,128)S(1)} %copy-done.7, ...), custom_call_target="tpu_custom_call" | custom-call | tf_op jit(solution)/shard_map/pallas_call | solution.py:29
  49.1 2.0 %shard_map.116 = (f32[8,288,128]{2,1,0:T(8,128)S(1)}, bf16[8,288,128]{2,1,0:T(8,128)(2,1)S(1)}) custom-call(bf16[512,768]{1,0:T(8,128)(2,1)S(1)} %get-tuple-element.46.mix_ref, bf16[8,288,128]{2,1,0:T(8,128)(2,1)S(1)} %collective-permute-done.10.low_ref, bf16[8,288,128]{2,1,0:T(8,128)(2,1)S(1)} %shard_map.115.own_ref, ...), custom_call_target="tpu_custom_call" | custom-call | tf_op jit(solution)/shard_map/pallas_call | solution.py:29
  51.1 7.1 %collective-permute-start.12 = (bf16[8,288,128]{2,1,0:T(8,128)(2,1)S(1)}, bf16[8,288,128]{2,1,0:T(8,128)(2,1)S(1)}, u32[]{:S(2)}, u32[]{:S(2)}) collective-permute-start(bf16[8,288,128]{2,1,0:T(8,128)(2,1)S(1)} %get-tuple-element.55), channel_id=1, source_target_pairs={{0,1},{1,0},{2,3},{3,2},{4,5},{5,4},{6,7},{7,6},{8,9},{9,8},{10,11... | collective-permute-start | bytes 1769480 | tf_op jit(solution)/shard_map/ppermute | solution.py:267
  58.3 4.9 %collective-permute-done.19.high_ref = bf16[8,288,128]{2,1,0:T(8,128)(2,1)S(1)} collective-permute-done((bf16[8,288,128]{2,1,0:T(8,128)(2,1)S(1)}, bf16[8,288,128]{2,1,0:T(8,128)(2,1)S(1)}, u32[]{:S(2)}, u32[]{:S(2)}) %collective-permute-start.19) | collective-permute-done | bytes 589856 | tf_op jit(solution)/shard_map/ppermute | solution.py:305
  63.2 2.0 %shard_map.119 = (f32[8,288,128]{2,1,0:T(8,128)S(1)}, bf16[8,288,128]{2,1,0:T(8,128)(2,1)S(1)}) custom-call(bf16[512,768]{1,0:T(8,128)(2,1)S(1)} %get-tuple-element.46.mix_ref, bf16[8,288,128]{2,1,0:T(8,128)(2,1)S(1)} %collective-permute-done.18.low_ref, bf16[8,288,128]{2,1,0:T(8,128)(2,1)S(1)} %get-tuple-element.61.own_ref, ...), custom_call_target="tpu_custom_call" | custom-call | tf_op jit(solution)/shard_map/pallas_call | solution.py:29
  65.2 3.0 %collective-permute-start.20 = (bf16[8,288,128]{2,1,0:T(8,128)(2,1)S(1)}, bf16[8,288,128]{2,1,0:T(8,128)(2,1)S(1)}, u32[]{:S(2)}, u32[]{:S(2)}) collective-permute-start(bf16[8,288,128]{2,1,0:T(8,128)(2,1)S(1)} %get-tuple-element.63), channel_id=1, source_target_pairs={{0,1},{1,0},{2,3},{3,2},{4,5},{5,4},{6,7},{7,6},{8,9},{9,8},{10,11... | collective-permute-start | bytes 1769480 | tf_op jit(solution)/shard_map/ppermute | solution.py:267
  68.3 3.3 %collective-permute-start.13 = (bf16[2,288,128]{2,1,0:T(8,128)(2,1)S(1)}, bf16[2,288,128]{2,1,0:T(8,128)(2,1)S(1)}, u32[]{:S(2)}, u32[]{:S(2)}) collective-permute-start(bf16[2,288,128]{2,1,0:T(8,128)(2,1)S(1)} %get-tuple-element.56), channel_id=1, source_target_pairs={{0,2},{1,15},{2,4},{3,1},{4,6},{5,3},{6,8},{7,5},{8,10},{9,7},{10,... | collective-permute-start | bytes 442376 | tf_op jit(solution)/shard_map/ppermute | solution.py:273
  71.6 2.5 %collective-permute-start.15 = (bf16[2,288,128]{2,1,0:T(8,128)(2,1)S(1)}, bf16[2,288,128]{2,1,0:T(8,128)(2,1)S(1)}, u32[]{:S(2)}, u32[]{:S(2)}) collective-permute-start(bf16[2,288,128]{2,1,0:T(8,128)(2,1)S(1)} %get-tuple-element.58), channel_id=1, source_target_pairs={{0,6},{1,11},{2,8},{3,13},{4,10},{5,15},{6,12},{7,1},{8,14},{9,3},... | collective-permute-start | bytes 442376 | tf_op jit(solution)/shard_map/ppermute | solution.py:273
  74.6 3.1 %collective-permute-start.22 = (bf16[2,288,128]{2,1,0:T(8,128)(2,1)S(1)}, bf16[2,288,128]{2,1,0:T(8,128)(2,1)S(1)}, u32[]{:S(2)}, u32[]{:S(2)}) collective-permute-start(bf16[2,288,128]{2,1,0:T(8,128)(2,1)S(1)} %get-tuple-element.65), channel_id=1, source_target_pairs={{0,4},{1,13},{2,6},{3,15},{4,8},{5,1},{6,10},{7,3},{8,12},{9,5},{1... | collective-permute-start | bytes 442376 | tf_op jit(solution)/shard_map/ppermute | solution.py:273
  77.7 1.5 %collective-permute-done.14.refs_1_ = bf16[2,288,128]{2,1,0:T(8,128)(2,1)S(1)} collective-permute-done((bf16[2,288,128]{2,1,0:T(8,128)(2,1)S(1)}, bf16[2,288,128]{2,1,0:T(8,128)(2,1)S(1)}, u32[]{:S(2)}, u32[]{:S(2)}) %collective-permute-start.14) | collective-permute-done | bytes 147488 | tf_op jit(solution)/shard_map/ppermute | solution.py:273
  79.3 4.6 %collective-permute-start.17 = (bf16[992,128]{1,0:T(8,128)(2,1)S(1)}, bf16[992,128]{1,0:T(8,128)(2,1)S(1)}, u32[]{:S(2)}, u32[]{:S(2)}) collective-permute-start(bf16[992,128]{1,0:T(8,128)(2,1)S(1)} %shard_map.118), channel_id=1, source_target_pairs={{0,1},{1,0},{2,3},{3,2},{4,5},{5,4},{6,7},{7,6},{8,9},{9,8},{10,11... | collective-permute-start | bytes 761864 | tf_op jit(solution)/shard_map/ppermute | solution.py:267
  84.0 4.8 %collective-permute-done.22.refs_1_.refs_7_ = bf16[2,288,128]{2,1,0:T(8,128)(2,1)S(1)} collective-permute-done((bf16[2,288,128]{2,1,0:T(8,128)(2,1)S(1)}, bf16[2,288,128]{2,1,0:T(8,128)(2,1)S(1)}, u32[]{:S(2)}, u32[]{:S(2)}) %collective-permute-start.22) | collective-permute-done | bytes 147488 | tf_op jit(solution)/shard_map/ppermute | solution.py:273
  88.8 4.7 %collective-permute-start.25 = (bf16[864,128]{1,0:T(8,128)(2,1)S(1)}, bf16[864,128]{1,0:T(8,128)(2,1)S(1)}, u32[]{:S(2)}, u32[]{:S(2)}) collective-permute-start(bf16[864,128]{1,0:T(8,128)(2,1)S(1)} %shard_map.121), channel_id=1, source_target_pairs={{0,1},{1,0},{2,3},{3,2},{4,5},{5,4},{6,7},{7,6},{8,9},{9,8},{10,11... | collective-permute-start | bytes 663560 | tf_op jit(solution)/shard_map/ppermute | solution.py:267
  93.5 3.3 %collective-permute-start.16 = (bf16[1,288,128]{2,1,0:T(8,128)(2,1)S(1)}, bf16[1,288,128]{2,1,0:T(8,128)(2,1)S(1)}, u32[]{:S(2)}, u32[]{:S(2)}) collective-permute-start(bf16[1,288,128]{2,1,0:T(8,128)(2,1)S(1)} %get-tuple-element.59), channel_id=1, source_target_pairs={{0,8},{1,9},{2,10},{3,11},{4,12},{5,13},{6,14},{7,15},{8,0},{9,1},... | collective-permute-start | bytes 221192 | tf_op jit(solution)/shard_map/ppermute | solution.py:273
  96.8 2.1 %collective-permute-start.24 = (bf16[1,288,128]{2,1,0:T(8,128)(2,1)S(1)}, bf16[1,288,128]{2,1,0:T(8,128)(2,1)S(1)}, u32[]{:S(2)}, u32[]{:S(2)}) collective-permute-start(bf16[1,288,128]{2,1,0:T(8,128)(2,1)S(1)} %get-tuple-element.67), channel_id=1, source_target_pairs={{0,8},{1,9},{2,10},{3,11},{4,12},{5,13},{6,14},{7,15},{8,0},{9,1},... | collective-permute-start | bytes 221192 | tf_op jit(solution)/shard_map/ppermute | solution.py:273
  98.9 3.9 %collective-permute-done.16.refs_3_ = bf16[1,288,128]{2,1,0:T(8,128)(2,1)S(1)} collective-permute-done((bf16[1,288,128]{2,1,0:T(8,128)(2,1)S(1)}, bf16[1,288,128]{2,1,0:T(8,128)(2,1)S(1)}, u32[]{:S(2)}, u32[]{:S(2)}) %collective-permute-start.16) | collective-permute-done | bytes 73760 | tf_op jit(solution)/shard_map/ppermute | solution.py:273
  102.8 2.8 %collective-permute-done.24.refs_9_ = bf16[1,288,128]{2,1,0:T(8,128)(2,1)S(1)} collective-permute-done((bf16[1,288,128]{2,1,0:T(8,128)(2,1)S(1)}, bf16[1,288,128]{2,1,0:T(8,128)(2,1)S(1)}, u32[]{:S(2)}, u32[]{:S(2)}) %collective-permute-start.24) | collective-permute-done | bytes 73760 | tf_op jit(solution)/shard_map/ppermute | solution.py:273
  105.6 8.1 %shard_map.122 = bf16[2,144,2048]{2,1,0:T(8,128)(2,1)} custom-call(s32[2]{0:T(128)S(1)} %pad_add_fusion.pos_ref, bf16[144,1152]{1,0:T(8,128)(2,1)S(1)} %get-tuple-element.37.pair_ref, bf16[8,16,128]{2,1,0:T(8,128)(2,1)S(1)} %get-tuple-element.45.refs_3_.near_ref, bf16[2,288,128]{2,1,0:T(8,128)(2,1)S(1)} %collective-permute-done.13.refs_0_, ...), custom_call_target="tpu_custom_call" | custom-call | tf_op jit(solution)/shard_map/pallas_call | solution.py:29
  (63 shorter events, 3.5 us)
Async XLA Ops:
  2.1 2.0 %collective-permute-start.5 = (bf16[3,288,128]{2,1,0:T(8,128)(2,1)S(1)}, bf16[3,288,128]{2,1,0:T(8,128)(2,1)S(1)}, u32[]{:S(2)}, u32[]{:S(2)}) collective-permute-start(bf16[3,288,128]{2,1,0:T(8,128)(2,1)S(1)} %get-tuple-element.48), channel_id=1, source_target_pairs={{0,1},{1,0},{2,3},{3,2},{4,5},{5,4},{6,7},{7,6},{8,9},{9,8},{10,11... | collective-permute-start | bytes 663560 | tf_op jit(solution)/shard_map/ppermute | solution.py:267
  3.6 12.3 %collective-permute-start = (bf16[3,304,128]{2,1,0:T(8,128)(2,1)S(1)}, bf16[3,304,128]{2,1,0:T(8,128)(2,1)S(1)}, u32[]{:S(2)}, u32[]{:S(2)}) collective-permute-start(bf16[3,304,128]{2,1,0:T(8,128)(2,1)S(1)} %get-tuple-element.39), channel_id=1, source_target_pairs={{0,1},{1,0},{2,3},{3,2},{4,5},{5,4},{6,7},{7,6},{8,9},{9,8},{10,11... | collective-permute-start | bytes 700424 | tf_op jit(solution)/shard_map/ppermute | solution.py:267
  4.1 42.1 %copy-start.10 = (f32[8,12,12]{2,0,1:T(8,128)S(1)}, f32[8,12,12]{2,0,1:T(8,128)}, u32[]{:S(2)}) copy-start(f32[8,12,12]{2,0,1:T(8,128)} %param.15) | copy-start | bytes 13828
  4.1 18.7 %collective-permute-start.6 = (bf16[2,288,128]{2,1,0:T(8,128)(2,1)S(1)}, bf16[2,288,128]{2,1,0:T(8,128)(2,1)S(1)}, u32[]{:S(2)}, u32[]{:S(2)}) collective-permute-start(bf16[2,288,128]{2,1,0:T(8,128)(2,1)S(1)} %get-tuple-element.49), channel_id=1, source_target_pairs={{0,2},{1,15},{2,4},{3,1},{4,6},{5,3},{6,8},{7,5},{8,10},{9,7},{10,... | collective-permute-start | bytes 442376 | tf_op jit(solution)/shard_map/ppermute | solution.py:273
  9.8 21.1 %collective-permute-start.7 = (bf16[2,288,128]{2,1,0:T(8,128)(2,1)S(1)}, bf16[2,288,128]{2,1,0:T(8,128)(2,1)S(1)}, u32[]{:S(2)}, u32[]{:S(2)}) collective-permute-start(bf16[2,288,128]{2,1,0:T(8,128)(2,1)S(1)} %get-tuple-element.50), channel_id=1, source_target_pairs={{0,4},{1,13},{2,6},{3,15},{4,8},{5,1},{6,10},{7,3},{8,12},{9,5},{1... | collective-permute-start | bytes 442376 | tf_op jit(solution)/shard_map/ppermute | solution.py:273
  11.0 19.9 %collective-permute-start.8 = (bf16[2,288,128]{2,1,0:T(8,128)(2,1)S(1)}, bf16[2,288,128]{2,1,0:T(8,128)(2,1)S(1)}, u32[]{:S(2)}, u32[]{:S(2)}) collective-permute-start(bf16[2,288,128]{2,1,0:T(8,128)(2,1)S(1)} %get-tuple-element.51), channel_id=1, source_target_pairs={{0,6},{1,11},{2,8},{3,13},{4,10},{5,15},{6,12},{7,1},{8,14},{9,3},... | collective-permute-start | bytes 442376 | tf_op jit(solution)/shard_map/ppermute | solution.py:273
  11.4 11.5 %collective-permute-start.9 = (bf16[1,288,128]{2,1,0:T(8,128)(2,1)S(1)}, bf16[1,288,128]{2,1,0:T(8,128)(2,1)S(1)}, u32[]{:S(2)}, u32[]{:S(2)}) collective-permute-start(bf16[1,288,128]{2,1,0:T(8,128)(2,1)S(1)} %get-tuple-element.52), channel_id=1, source_target_pairs={{0,8},{1,9},{2,10},{3,11},{4,12},{5,13},{6,14},{7,15},{8,0},{9,1},... | collective-permute-start | bytes 221192 | tf_op jit(solution)/shard_map/ppermute | solution.py:273
  15.9 17.8 %collective-permute-start.4 = (bf16[1,304,128]{2,1,0:T(8,128)(2,1)S(1)}, bf16[1,304,128]{2,1,0:T(8,128)(2,1)S(1)}, u32[]{:S(2)}, u32[]{:S(2)}) collective-permute-start(bf16[1,304,128]{2,1,0:T(8,128)(2,1)S(1)} %get-tuple-element.43), channel_id=1, source_target_pairs={{0,8},{1,9},{2,10},{3,11},{4,12},{5,13},{6,14},{7,15},{8,0},{9,1},... | collective-permute-start | bytes 233480 | tf_op jit(solution)/shard_map/ppermute | solution.py:273
  16.8 29.5 %copy-start.5 = (f32[144,12]{1,0:T(8,128)S(1)}, f32[144,12]{1,0:T(8,128)}, u32[]{:S(2)}) copy-start(f32[144,12]{1,0:T(8,128)} %constant.31.clone.second_ref) | copy-start | bytes 20740
  16.8 29.5 %copy-start.6 = (s32[32,48]{1,0:T(8,128)S(1)}, s32[32,48]{1,0:T(8,128)}, u32[]{:S(2)}) copy-start(s32[32,48]{1,0:T(8,128)} %constant.28.clone.rel_ref) | copy-start | bytes 18436
  16.8 29.5 %copy-start.7 = (s32[32,48]{1,0:T(8,128)S(1)}, s32[32,48]{1,0:T(8,128)}, u32[]{:S(2)}) copy-start(s32[32,48]{1,0:T(8,128)} %constant.29.clone.mom_ref) | copy-start | bytes 18436
  16.8 29.5 %copy-start.8 = (f32[2,8,16]{2,1,0:T(8,128)S(1)}, f32[2,8,16]{2,1,0:T(8,128)}, u32[]{:S(2)}) copy-start(f32[2,8,16]{2,1,0:T(8,128)} %phonon_ref.1) | copy-start | bytes 3076
  16.8 29.5 %copy-start.9 = (s32[8]{0:T(128)S(1)}, s32[8]{0:T(128)}, u32[]{:S(2)}) copy-start(s32[8]{0:T(128)} %offsets_ref.1) | copy-start | bytes 100
  22.9 13.3 %collective-permute-start.1 = (bf16[2,304,128]{2,1,0:T(8,128)(2,1)S(1)}, bf16[2,304,128]{2,1,0:T(8,128)(2,1)S(1)}, u32[]{:S(2)}, u32[]{:S(2)}) collective-permute-start(bf16[2,304,128]{2,1,0:T(8,128)(2,1)S(1)} %get-tuple-element.40), channel_id=1, source_target_pairs={{0,2},{1,15},{2,4},{3,1},{4,6},{5,3},{6,8},{7,5},{8,10},{9,7},{10,... | collective-permute-start | bytes 466952 | tf_op jit(solution)/shard_map/ppermute | solution.py:273
  22.9 14.4 %collective-permute-start.2 = (bf16[2,304,128]{2,1,0:T(8,128)(2,1)S(1)}, bf16[2,304,128]{2,1,0:T(8,128)(2,1)S(1)}, u32[]{:S(2)}, u32[]{:S(2)}) collective-permute-start(bf16[2,304,128]{2,1,0:T(8,128)(2,1)S(1)} %get-tuple-element.41), channel_id=1, source_target_pairs={{0,4},{1,13},{2,6},{3,15},{4,8},{5,1},{6,10},{7,3},{8,12},{9,5},{1... | collective-permute-start | bytes 466952 | tf_op jit(solution)/shard_map/ppermute | solution.py:273
  30.9 10.1 %collective-permute-start.3 = (bf16[2,304,128]{2,1,0:T(8,128)(2,1)S(1)}, bf16[2,304,128]{2,1,0:T(8,128)(2,1)S(1)}, u32[]{:S(2)}, u32[]{:S(2)}) collective-permute-start(bf16[2,304,128]{2,1,0:T(8,128)(2,1)S(1)} %get-tuple-element.42), channel_id=1, source_target_pairs={{0,6},{1,11},{2,8},{3,13},{4,10},{5,15},{6,12},{7,1},{8,14},{9,3},... | collective-permute-start | bytes 466952 | tf_op jit(solution)/shard_map/ppermute | solution.py:273
  30.9 18.2 %collective-permute-start.10 = (bf16[8,288,128]{2,1,0:T(8,128)(2,1)S(1)}, bf16[8,288,128]{2,1,0:T(8,128)(2,1)S(1)}, u32[]{:S(2)}, u32[]{:S(2)}) collective-permute-start(bf16[8,288,128]{2,1,0:T(8,128)(2,1)S(1)} %shard_map.115.own_ref), channel_id=1, source_target_pairs={{0,16},{16,32},{32,48},{48,64},{64,80},{80,96},{96,112},{112,128},... | collective-permute-start | bytes 1769480 | tf_op jit(solution)/shard_map/ppermute | solution.py:305
  33.7 15.4 %collective-permute-start.11 = (bf16[8,288,128]{2,1,0:T(8,128)(2,1)S(1)}, bf16[8,288,128]{2,1,0:T(8,128)(2,1)S(1)}, u32[]{:S(2)}, u32[]{:S(2)}) collective-permute-start(bf16[8,288,128]{2,1,0:T(8,128)(2,1)S(1)} %shard_map.115.own_ref), channel_id=1, source_target_pairs={{16,0},{32,16},{48,32},{64,48},{80,64},{96,80},{112,96},{128,112},... | collective-permute-start | bytes 1769480 | tf_op jit(solution)/shard_map/ppermute | solution.py:305
  41.0 17.3 %collective-permute-start.18 = (bf16[8,288,128]{2,1,0:T(8,128)(2,1)S(1)}, bf16[8,288,128]{2,1,0:T(8,128)(2,1)S(1)}, u32[]{:S(2)}, u32[]{:S(2)}) collective-permute-start(bf16[8,288,128]{2,1,0:T(8,128)(2,1)S(1)} %get-tuple-element.61.own_ref), channel_id=1, source_target_pairs={{0,16},{16,32},{32,48},{48,64},{64,80},{80,96},{96,112},{112,128},... | collective-permute-start | bytes 1769480 | tf_op jit(solution)/shard_map/ppermute | solution.py:305
  43.7 19.4 %collective-permute-start.19 = (bf16[8,288,128]{2,1,0:T(8,128)(2,1)S(1)}, bf16[8,288,128]{2,1,0:T(8,128)(2,1)S(1)}, u32[]{:S(2)}, u32[]{:S(2)}) collective-permute-start(bf16[8,288,128]{2,1,0:T(8,128)(2,1)S(1)} %get-tuple-element.61.own_ref), channel_id=1, source_target_pairs={{16,0},{32,16},{48,32},{64,48},{80,64},{96,80},{112,96},{128,112},... | collective-permute-start | bytes 1769480 | tf_op jit(solution)/shard_map/ppermute | solution.py:305
  51.1 17.0 %collective-permute-start.12 = (bf16[8,288,128]{2,1,0:T(8,128)(2,1)S(1)}, bf16[8,288,128]{2,1,0:T(8,128)(2,1)S(1)}, u32[]{:S(2)}, u32[]{:S(2)}) collective-permute-start(bf16[8,288,128]{2,1,0:T(8,128)(2,1)S(1)} %get-tuple-element.55), channel_id=1, source_target_pairs={{0,1},{1,0},{2,3},{3,2},{4,5},{5,4},{6,7},{7,6},{8,9},{9,8},{10,11... | collective-permute-start | bytes 1769480 | tf_op jit(solution)/shard_map/ppermute | solution.py:267
  65.2 8.9 %collective-permute-start.20 = (bf16[8,288,128]{2,1,0:T(8,128)(2,1)S(1)}, bf16[8,288,128]{2,1,0:T(8,128)(2,1)S(1)}, u32[]{:S(2)}, u32[]{:S(2)}) collective-permute-start(bf16[8,288,128]{2,1,0:T(8,128)(2,1)S(1)} %get-tuple-element.63), channel_id=1, source_target_pairs={{0,1},{1,0},{2,3},{3,2},{4,5},{5,4},{6,7},{7,6},{8,9},{9,8},{10,11... | collective-permute-start | bytes 1769480 | tf_op jit(solution)/shard_map/ppermute | solution.py:267
  68.3 9.4 %collective-permute-start.13 = (bf16[2,288,128]{2,1,0:T(8,128)(2,1)S(1)}, bf16[2,288,128]{2,1,0:T(8,128)(2,1)S(1)}, u32[]{:S(2)}, u32[]{:S(2)}) collective-permute-start(bf16[2,288,128]{2,1,0:T(8,128)(2,1)S(1)} %get-tuple-element.56), channel_id=1, source_target_pairs={{0,2},{1,15},{2,4},{3,1},{4,6},{5,3},{6,8},{7,5},{8,10},{9,7},{10,... | collective-permute-start | bytes 442376 | tf_op jit(solution)/shard_map/ppermute | solution.py:273
  71.5 7.7 %collective-permute-start.14 = (bf16[2,288,128]{2,1,0:T(8,128)(2,1)S(1)}, bf16[2,288,128]{2,1,0:T(8,128)(2,1)S(1)}, u32[]{:S(2)}, u32[]{:S(2)}) collective-permute-start(bf16[2,288,128]{2,1,0:T(8,128)(2,1)S(1)} %get-tuple-element.57), channel_id=1, source_target_pairs={{0,4},{1,13},{2,6},{3,15},{4,8},{5,1},{6,10},{7,3},{8,12},{9,5},{1... | collective-permute-start | bytes 442376 | tf_op jit(solution)/shard_map/ppermute | solution.py:273
  71.6 7.6 %collective-permute-start.15 = (bf16[2,288,128]{2,1,0:T(8,128)(2,1)S(1)}, bf16[2,288,128]{2,1,0:T(8,128)(2,1)S(1)}, u32[]{:S(2)}, u32[]{:S(2)}) collective-permute-start(bf16[2,288,128]{2,1,0:T(8,128)(2,1)S(1)} %get-tuple-element.58), channel_id=1, source_target_pairs={{0,6},{1,11},{2,8},{3,13},{4,10},{5,15},{6,12},{7,1},{8,14},{9,3},... | collective-permute-start | bytes 442376 | tf_op jit(solution)/shard_map/ppermute | solution.py:273
  74.2 9.8 %collective-permute-start.21 = (bf16[2,288,128]{2,1,0:T(8,128)(2,1)S(1)}, bf16[2,288,128]{2,1,0:T(8,128)(2,1)S(1)}, u32[]{:S(2)}, u32[]{:S(2)}) collective-permute-start(bf16[2,288,128]{2,1,0:T(8,128)(2,1)S(1)} %get-tuple-element.64), channel_id=1, source_target_pairs={{0,2},{1,15},{2,4},{3,1},{4,6},{5,3},{6,8},{7,5},{8,10},{9,7},{10,... | collective-permute-start | bytes 442376 | tf_op jit(solution)/shard_map/ppermute | solution.py:273
  74.6 14.2 %collective-permute-start.22 = (bf16[2,288,128]{2,1,0:T(8,128)(2,1)S(1)}, bf16[2,288,128]{2,1,0:T(8,128)(2,1)S(1)}, u32[]{:S(2)}, u32[]{:S(2)}) collective-permute-start(bf16[2,288,128]{2,1,0:T(8,128)(2,1)S(1)} %get-tuple-element.65), channel_id=1, source_target_pairs={{0,4},{1,13},{2,6},{3,15},{4,8},{5,1},{6,10},{7,3},{8,12},{9,5},{1... | collective-permute-start | bytes 442376 | tf_op jit(solution)/shard_map/ppermute | solution.py:273
  77.7 11.1 %collective-permute-start.23 = (bf16[2,288,128]{2,1,0:T(8,128)(2,1)S(1)}, bf16[2,288,128]{2,1,0:T(8,128)(2,1)S(1)}, u32[]{:S(2)}, u32[]{:S(2)}) collective-permute-start(bf16[2,288,128]{2,1,0:T(8,128)(2,1)S(1)} %get-tuple-element.66), channel_id=1, source_target_pairs={{0,6},{1,11},{2,8},{3,13},{4,10},{5,15},{6,12},{7,1},{8,14},{9,3},... | collective-permute-start | bytes 442376 | tf_op jit(solution)/shard_map/ppermute | solution.py:273
  79.3 26.4 %collective-permute-start.17 = (bf16[992,128]{1,0:T(8,128)(2,1)S(1)}, bf16[992,128]{1,0:T(8,128)(2,1)S(1)}, u32[]{:S(2)}, u32[]{:S(2)}) collective-permute-start(bf16[992,128]{1,0:T(8,128)(2,1)S(1)} %shard_map.118), channel_id=1, source_target_pairs={{0,1},{1,0},{2,3},{3,2},{4,5},{5,4},{6,7},{7,6},{8,9},{9,8},{10,11... | collective-permute-start | bytes 761864 | tf_op jit(solution)/shard_map/ppermute | solution.py:267
  88.8 16.8 %collective-permute-start.25 = (bf16[864,128]{1,0:T(8,128)(2,1)S(1)}, bf16[864,128]{1,0:T(8,128)(2,1)S(1)}, u32[]{:S(2)}, u32[]{:S(2)}) collective-permute-start(bf16[864,128]{1,0:T(8,128)(2,1)S(1)} %shard_map.121), channel_id=1, source_target_pairs={{0,1},{1,0},{2,3},{3,2},{4,5},{5,4},{6,7},{7,6},{8,9},{9,8},{10,11... | collective-permute-start | bytes 663560 | tf_op jit(solution)/shard_map/ppermute | solution.py:267
  93.5 9.3 %collective-permute-start.16 = (bf16[1,288,128]{2,1,0:T(8,128)(2,1)S(1)}, bf16[1,288,128]{2,1,0:T(8,128)(2,1)S(1)}, u32[]{:S(2)}, u32[]{:S(2)}) collective-permute-start(bf16[1,288,128]{2,1,0:T(8,128)(2,1)S(1)} %get-tuple-element.59), channel_id=1, source_target_pairs={{0,8},{1,9},{2,10},{3,11},{4,12},{5,13},{6,14},{7,15},{8,0},{9,1},... | collective-permute-start | bytes 221192 | tf_op jit(solution)/shard_map/ppermute | solution.py:273
  96.8 8.8 %collective-permute-start.24 = (bf16[1,288,128]{2,1,0:T(8,128)(2,1)S(1)}, bf16[1,288,128]{2,1,0:T(8,128)(2,1)S(1)}, u32[]{:S(2)}, u32[]{:S(2)}) collective-permute-start(bf16[1,288,128]{2,1,0:T(8,128)(2,1)S(1)} %get-tuple-element.67), channel_id=1, source_target_pairs={{0,8},{1,9},{2,10},{3,11},{4,12},{5,13},{6,14},{7,15},{8,0},{9,1},... | collective-permute-start | bytes 221192 | tf_op jit(solution)/shard_map/ppermute | solution.py:273
  (6 other events, 94.1 us)

commit v3 on v2

v3 whole, which is shorter than its diff:
```python
import functools

import jax
import jax.numpy as jnp
import numpy as np
from jax import lax
from jax.experimental import pallas as pl
from jax.experimental.pallas import tpu as pltpu
from jax.sharding import Mesh
from jax.sharding import PartitionSpec as P

OFFSET = 2
TAPS = 2 * OFFSET + 1
ROWS = 16
COST = 1
PARTS = 1
LANES = 128
SPAN = 2 * LANES
PAD = LANES // 2
KMOM = ("z", "core")
VMEM = pl.BlockSpec(memory_space=pltpu.VMEM)
SMEM = pl.BlockSpec(memory_space=pltpu.SMEM)
BF16, F32 = jnp.bfloat16, jnp.float32

NEAR = (1, 2, 3)
EARLY = ((1, 0), (1, 1), (2, 0), (2, 1), (0, 0))
PLACES = EARLY + ((3, 0), (3, 1), (4, 0))


def call(kernel, outs, *args, scratch=(), after=()):
    def run(*refs):
        kernel(*refs[: len(args)], *refs[len(args) + len(after) :])

    return pl.pallas_call(
        run,
        out_shape=[jax.ShapeDtypeStruct(shape, dtype) for shape, dtype in outs],
        in_specs=[SMEM if a.ndim == 1 else VMEM for a in args] + [pl.BlockSpec(memory_space=pl.ANY)] * len(after),
        out_specs=[VMEM] * len(outs),
        scratch_shapes=[pltpu.VMEM(shape, dtype) for shape, dtype in scratch],
        cost_estimate=pl.CostEstimate(flops=COST, bytes_accessed=1, transcendentals=0),
        compiler_params=pltpu.CompilerParams(vmem_limit_bytes=40 * 2**20),
    )(*args, *after)


def mixing_index(e_dev):
    rel = np.zeros((e_dev, 2, 8, 3, 8, e_dev), np.int32)
    mom = np.zeros_like(rel)
    for e_out in range(e_dev):
        for tile in range(3):
            for e_in in range(e_dev):
                rel[e_out, :, :, tile, :, e_in] = (tile - 1) * e_dev + e_in - e_out + OFFSET
    for d, (j_to, to_other) in enumerate(PLACES):
        for s, (j_from, from_other) in enumerate(PLACES):
            mom[:, 0, d, :, s, :] = 2 * (j_to + j_from) + to_other - from_other
            mom[:, 1, d, :, s, :] = 2 * (j_from - j_to) + 1 - to_other - from_other
    return rel.reshape(e_dev * 16, -1), mom.reshape(e_dev * 16, -1)


def tables_kernel(moms, pos_ref, offsets_ref, phonon_ref, coupling_ref, rel_ref, mom_ref, first_ref, second_ref,
                  wide_first_ref, wide_second_ref, mix_ref, pair_ref):
    slots = coupling_ref.shape[0]
    taps = jnp.zeros((8, moms), F32)
    row = lax.broadcasted_iota(jnp.int32, (8, moms), 0)
    for s in range(2):
        for w in range(phonon_ref.shape[1]):
            hit = row == (2 * s - 1) * offsets_ref[w] + OFFSET
            taps = taps + jnp.where(hit, phonon_ref[s, w : w + 1, :], 0.0)
    taps = taps.astype(BF16).astype(F32)
    rel, mom = rel_ref[...], (mom_ref[...] * pos_ref[1]) & (moms - 1)
    table = jnp.zeros(rel.shape, F32)
    for r in range(TAPS):
        for q in range(moms):
            table = jnp.where((rel == r) & (mom == q), taps[r : r + 1, q : q + 1], table)
    outs, ins = table.shape
    tall = (lax.broadcasted_iota(jnp.int32, (outs * ROWS, outs), 0) >> 4) == lax.broadcasted_iota(
        jnp.int32, (outs * ROWS, outs), 1)
    flat = lax.broadcasted_iota(jnp.int32, (ins, ins * ROWS), 0) == (
        lax.broadcasted_iota(jnp.int32, (ins, ins * ROWS), 1) >> 4)
    half = jnp.dot(tall.astype(BF16), table.astype(BF16), preferred_element_type=F32).astype(BF16)
    full = jnp.dot(half, flat.astype(BF16), preferred_element_type=F32)
    same = (lax.broadcasted_iota(jnp.int32, full.shape, 0) & (ROWS - 1)) == (
        lax.broadcasted_iota(jnp.int32, full.shape, 1) & (ROWS - 1))
    mix_ref[...] = jnp.where(same, full, 0.0).astype(BF16)
    bonds = jnp.concatenate([coupling_ref[n] for n in range(slots)], axis=1)

    def spread(tall_ref, wide_ref):
        half = jnp.dot(tall_ref[...], bonds, precision=lax.Precision.HIGHEST, preferred_element_type=F32)
        return jnp.dot(half, wide_ref[...], precision=lax.Precision.HIGHEST, preferred_element_type=F32)

    pair_ref[...] = (spread(first_ref, wide_first_ref) * spread(second_ref, wide_second_ref)).astype(BF16)


def tables(pos, phonon, offsets, coupling, e_dev):
    slots, orbs = coupling.shape[0], coupling.shape[1]
    moms = phonon.shape[2]
    rel, mom = mixing_index(e_dev)
    pairs = np.arange(orbs * orbs)
    picks = [(index[:, None] == np.arange(orbs)).astype(np.float32) for index in (pairs // orbs, pairs % orbs)]
    wide = [np.kron(np.eye(slots, dtype=np.float32), pick.T) for pick in picks]
    return call(
        functools.partial(tables_kernel, moms),
        [((rel.shape[0] * ROWS, rel.shape[1] * ROWS), BF16), ((orbs * orbs, slots * orbs * orbs), BF16)],
        pos, offsets, phonon, coupling, *map(jnp.asarray, (rel, mom, *picks, *wide)),
    )


def cut_kernel(groups, pos_ref, green_ref, near_ref, own_ref, give_ref, far_ref, home_ref):
    e_dev, pairs, _ = green_ref.shape
    rows = e_dev * pairs

    def put(ref, at, distance):
        group = (pos_ref[0] + distance) & (groups - 1)
        for chunk in range(2):
            start = pl.multiple_of((chunk * groups + group) * LANES, LANES)
            ref[at, chunk * rows : (chunk + 1) * rows, :] = green_ref[:, :, pl.ds(start, LANES)].reshape(rows, LANES)
        ref[at, 2 * rows :, :] = near_ref[...]

    for i, j in enumerate(NEAR):
        put(own_ref, i, pos_ref[1] * j)
        put(give_ref, i, -pos_ref[1] * j)
    put(far_ref, 0, 4)
    put(home_ref, 0, 0)


def cut(pos, green, near, groups):
    height = 2 * green.shape[0] * green.shape[1] + near.shape[0]
    outs = [((n, height, LANES), BF16) for n in (len(NEAR), len(NEAR), 1, 1)]
    return call(functools.partial(cut_kernel, groups), outs, pos, green, near)


def merge_kernel(chips, own_ref, got_ref, *refs):
    whole = refs[: len(refs) - len(chips) >> 1]
    outs = refs[len(whole) :]
    for out, j in zip(outs, chips):
        out[0] = own_ref[j - 1]
        out[1] = got_ref[j - 1]
    for out, ref in zip(outs[len(chips) :], whole):
        out[...] = ref[...]


def merge(own, got, chips, *whole, after=()):
    outs = [((2, *own.shape[1:]), BF16)] * len(chips) + [(x.shape, BF16) for x in whole]
    return call(functools.partial(merge_kernel, chips), outs, own, got, *whole, after=after)


def stack_kernel(*refs):
    blocks, (out_ref, near_ref) = refs[:-2], refs[-2:]
    rows = out_ref.shape[1]
    at = 0
    for block in blocks:
        for i in range(block.shape[0]):
            out_ref[at] = block[i, 0:rows, :]
            near_ref[at] = block[i, rows:, :]
            at += 1


def stack(*blocks):
    places = sum(b.shape[0] for b in blocks)
    outs = [((places, h, LANES), BF16) for h in (blocks[0].shape[1] - ROWS, ROWS)]
    return call(stack_kernel, outs, *blocks)


def mix_kernel(e_dev, chunk, mix_ref, *refs):
    fields, kept_ref, other_ref = refs[:6], refs[6], refs[7]
    places, height, width = kept_ref.shape
    pairs = height // e_dev
    for g in range(pairs // ROWS):
        tiles = []
        for ref in fields:
            for i in range(ref.shape[0]):
                for e in range(e_dev):
                    tiles.append(ref[i, pl.ds(chunk * height + e * pairs + g * ROWS, ROWS), :])
        mixed = jnp.dot(mix_ref[...], jnp.concatenate(tiles, axis=0), preferred_element_type=F32)
        mixed = mixed.reshape(e_dev, 2, places, ROWS, width)
        for e in range(e_dev):
            rows = pl.ds(e * pairs + g * ROWS, ROWS)
            kept_ref[:, rows, :] = mixed[e, 0]
            other_ref[:, rows, :] = mixed[e, 1].astype(BF16)


def mix(matrix, fields, chunk, e_dev, after=()):
    shape = (len(PLACES), fields[0].shape[1] // 2, LANES)
    return call(functools.partial(mix_kernel, e_dev, chunk), [(shape, F32), (shape, BF16)], matrix, *fields, after=after)


def add_kernel(kept_ref, got_ref, far, three, two, one, home):
    at = 0
    for out in (one, two, home, three, far):
        for i in range(out.shape[0]):
            out[i] = (kept_ref[at] + got_ref[at].astype(F32)).astype(BF16)
            at += 1


def add(kept, got, after=()):
    return call(add_kernel, [((n, *kept.shape[1:]), BF16) for n in (1, 2, 2, 2, 1)], kept, got, after=after)


def pick_kernel(*refs):
    blocks, extra, out = refs[: len(NEAR)], refs[len(NEAR) : -1], refs[-1]
    rows = blocks[0].shape[1]
    for i, block in enumerate(blocks):
        out[i * rows : (i + 1) * rows, :] = block[1]
    at = len(NEAR) * rows
    for near in extra:
        for i in range(near.shape[0]):
            out[at : at + near.shape[1], :] = near[i]
            at += near.shape[1]


def pick(blocks, *extra, after=()):
    height = len(NEAR) * blocks[1].shape[1] + sum(x.shape[0] * x.shape[1] for x in extra)
    return call(pick_kernel, [((height, LANES), BF16)], *blocks[3:0:-1], *extra, after=(blocks[0], *after))[0]


def gather_line(pos_ref, groups, line, base, far_ref, three_ref, two_ref, one_ref, home_ref, given_ref):
    z, way = pos_ref[0], pos_ref[1]
    rows = far_ref.shape[1]

    def put(block, distance):
        group = (z + distance) & (groups - 1)
        line[:, pl.ds(pl.multiple_of(base + group * LANES, LANES), LANES)] = block

    for i, (j, ref) in enumerate(zip(NEAR, (one_ref, two_ref, three_ref))):
        put(ref[0], -way * j)
        put(given_ref[i * rows : (i + 1) * rows, :], way * j)
    put(far_ref[0], 4)
    put(home_ref[0], 0)


def sum_block(line, window_at, near, pair_ref, e_dev):
    slots, pairs = pair_ref.shape[1] // pair_ref.shape[0], pair_ref.shape[0]
    place = lax.broadcasted_iota(jnp.int32, (SPAN, LANES), 0) - lax.broadcasted_iota(jnp.int32, (SPAN, LANES), 1) - PAD
    near = near.astype(F32).astype(jnp.int32)
    hits = [(place == near[n : n + 1, :]).astype(BF16) for n in range(slots)]
    window = line[:, pl.ds(window_at, SPAN)]
    taken = jnp.dot(window, jnp.concatenate(hits, axis=1), preferred_element_type=F32).astype(BF16)
    columns = [
        jnp.concatenate([taken[e * pairs : (e + 1) * pairs, n * LANES : (n + 1) * LANES] for n in range(slots)], axis=0)
        for e in range(e_dev)
    ]
    return jnp.dot(pair_ref[...], jnp.concatenate(columns, axis=1), preferred_element_type=F32).astype(BF16)


def first_kernel(groups, pos_ref, pair_ref, early_ref, late_ref, *refs):
    blocks, (out_ref, nears, tail, line, seen) = refs[:6], refs[6:]
    e_dev, pairs, atoms = out_ref.shape
    rows = e_dev * pairs
    z, way = pos_ref[0], pos_ref[1]
    core = (1 - way) >> 1

    def rank(distance, parity):
        return 2 * ((z + distance) & (groups - 1)) + parity

    at = len(NEAR) * rows
    for i, (j, other) in enumerate(PLACES):
        nears[rank(-way * j, core + way * other)] = early_ref[i] if i < len(EARLY) else late_ref[i - len(EARLY)]
        nears[rank(way * j, core + way - way * other)] = blocks[5][at : at + ROWS, :]
        at += ROWS
    gather_line(pos_ref, groups, seen, 0, *blocks)
    tail[...] = seen[:, groups * LANES - LANES - PAD :]
    line[:, 0:LANES] = jnp.zeros((rows, LANES), BF16)
    line[:, PAD : PAD + groups * LANES] = seen[...]

    def step(b, carry):
        start = pl.multiple_of(b * LANES, LANES)
        total = sum_block(line, start, nears[b], pair_ref, e_dev)
        for e in range(e_dev):
            out_ref[e, :, pl.ds(start, LANES)] = total[:, e * LANES : (e + 1) * LANES]
        return carry

    lax.fori_loop(0, atoms // LANES, step, 0, unroll=True)


def first_sum(pos, pair_maps, nears, blocks, groups, shape):
    rows = shape[0] * shape[1]
    return call(
        functools.partial(first_kernel, groups),
        [((*shape[:2], (groups - 1) * LANES), BF16), ((2 * groups, ROWS, LANES), BF16), ((rows, LANES + PAD), BF16)],
        pos, pair_maps, *nears, *blocks,
        scratch=[((rows, groups * LANES + LANES), BF16), ((rows, groups * LANES), BF16)],
    )


def second_kernel(groups, pos_ref, pair_ref, nears, done_ref, tail_ref, *refs):
    blocks, (out_ref, line, seen) = refs[:6], refs[6:]
    e_dev, pairs, atoms = out_ref.shape
    rows = e_dev * pairs
    first = done_ref.shape[2] // LANES
    width = (groups + 1) * LANES
    out_ref[:, :, 0 : first * LANES] = done_ref[...]
    gather_line(pos_ref, groups, seen, 0, *blocks)
    line[:, width:] = jnp.zeros((rows, LANES), BF16)
    line[:, 0 : LANES + PAD] = tail_ref[...]
    line[:, LANES + PAD : PAD + width] = seen[...]

    def step(b, carry):
        start = pl.multiple_of(b * LANES, LANES)
        total = sum_block(line, start, nears[b + first], pair_ref, e_dev)
        for e in range(e_dev):
            out_ref[e, :, pl.ds(pl.multiple_of(start + first * LANES, LANES), LANES)] = total[:, e * LANES : (e + 1) * LANES]
        return carry

    lax.fori_loop(0, atoms // LANES - first, step, 0, unroll=True)


def second_sum(pos, pair_maps, nears, done, tail, blocks, groups, shape):
    rows = shape[0] * shape[1]
    return call(
        functools.partial(second_kernel, groups),
        [(shape, BF16)],
        pos, pair_maps, nears, done, tail, *blocks,
        scratch=[((rows, (groups + 2) * LANES), BF16), ((rows, groups * LANES), BF16)],
    )[0]


def swap(x):
    return lax.ppermute(x, "core", [(0, 1), (1, 0)])


def round_ring(x, j):
    groups = lax.axis_size("z")
    pairs = [(2 * z + c, 2 * ((z + (j if c == 0 else -j)) % groups) + c) for z in range(groups) for c in range(2)]
    return lax.ppermute(x, KMOM, pairs)


def exchange(far, three, two, one, home):
    return [round_ring(far, 4), round_ring(three, 3), round_ring(two, 2), round_ring(one, 1), home]


def body(green_blocks, phonon, offsets, neighbours, coupling):
    groups, tiles = lax.axis_size("z"), lax.axis_size("energy")
    green = green_blocks[:, 0]
    e_dev, pairs, atoms = green.shape
    rows = e_dev * pairs
    slots = neighbours.shape[1]
    core = lax.axis_index("core")
    pos = jnp.stack([lax.axis_index("z"), 1 - 2 * core])
    forward = [(i, i + 1) for i in range(tiles - 1)]
    backward = [(i + 1, i) for i in range(tiles - 1)]
    atom = lax.axis_index(KMOM) * LANES + jnp.arange(LANES, dtype=jnp.int32)
    steps = (neighbours - atom[:, None]).T.astype(BF16)
    steps = jnp.concatenate([steps, jnp.zeros((ROWS - slots, LANES), BF16)], axis=0)

    own, give, far, home = cut(pos, green, steps, groups)
    far, three, two, one, home = exchange(far, *merge(own, swap(give), (3, 2, 1)), home)
    parts = [stack(one, two, home), stack(three, far)]
    fields, near = zip(*parts)
    low = [lax.ppermute(x, "energy", forward) for x in fields]
    high = [lax.ppermute(x, "energy", backward) for x in fields]
    fields = (*low, *fields, *high)
    matrix, pair_maps = tables(pos, phonon, offsets, coupling, e_dev)
    backs = []
    for chunk in range(2):
        kept, other = mix(matrix, fields, chunk, e_dev)
        backs.append(exchange(*add(kept, swap(other))))
    blocks = [*backs[0], swap(pick(backs[0], *near))]
    done, nears, tail = first_sum(pos, pair_maps, near, blocks, groups, green.shape)
    blocks = [*backs[1], swap(pick(backs[1]))]
    return second_sum(pos, pair_maps, nears, done, tail, blocks, groups, green.shape)[:, None]


def solution(mesh):
    torus = Mesh(mesh.devices.reshape(mesh.shape["energy"], -1, 2), ("energy", *KMOM))
    placed = (P("energy", KMOM, None, None), P(), P(), P(KMOM, None), P())
    return jax.shard_map(body, mesh=torus, in_specs=placed, out_specs=P("energy", KMOM, None, None), check_vma=False)
```

time: 115 us -> 106 us (0.922)
  starting transfers between devices: 66.6 us -> 46.7 us
  waiting for transfers between devices: 28.7 us -> 40.6 us
    ppermute x6 -> x5, starting transfers between devices: 20.8 us -> 8.09 us  [swap(): return lax.ppermute(x, 'core', [(0, 1), (1, 0)])]
    ppermute x16 -> x12, starting transfers between devices: 35.3 us -> 28.1 us  [round_ring(): return lax.ppermute(x, KMOM, pairs)]
    ppermute x16 -> x12, waiting for transfers between devices: 23.8 us -> 30.1 us  [round_ring(): return lax.ppermute(x, KMOM, pairs)]
    ppermute x4, waiting for transfers between devices: 4.89 us -> 9.07 us  [the longest x2 4.98 us: body(): low = [lax.ppermute(x, 'energy', forward) for x in fields]]
    ppermute x6 -> x5, waiting for transfers between devices: 0.02 us -> 1.45 us  [swap(): return lax.ppermute(x, 'core', [(0, 1), (1, 0)])]
    pallas_call x14 -> x13, Pallas kernels: 16.6 us -> 15.6 us  [call(): pl.pallas_call(run, out_shape=[jax.ShapeDtypeStruct(shape, dtype) for sha...]
  transfers between devices with their start and end apart: 26 -> 21, of which waited for: 9 -> 10; matrix products, arithmetic and copies ran while one was open for 0% -> 0% of each run, Pallas kernels for 7% -> 8%
where the time goes in v3:
time: 106 us; the launch traced here: 105 us
  starting transfers between devices  46.7 us (44%)
  waiting for transfers between devices  40.6 us (38%)
  Pallas kernels  15.6 us (15%)
  local copies, waits for them, and re-layouts  1.35 us (1%)
    ppermute x12, waiting for transfers between devices, round_ring(): return lax.ppermute(x, KMOM, pairs)  30.1 us
    ppermute x12, starting transfers between devices, round_ring(): return lax.ppermute(x, KMOM, pairs)  28.1 us
    pallas_call x13, Pallas kernels, call(): pl.pallas_call(run, out_shape=[jax.ShapeDtypeStruct(shape, dtype) for sha...  15.6 us
    ppermute x5, starting transfers between devices, swap(): return lax.ppermute(x, 'core', [(0, 1), (1, 0)])  8.09 us
    ppermute x2, starting transfers between devices, body(): low = [lax.ppermute(x, 'energy', forward) for x in fields]  5.83 us
    ppermute x2, waiting for transfers between devices, body(): low = [lax.ppermute(x, 'energy', forward) for x in fields]  4.98 us
    ppermute x2, starting transfers between devices, body(): high = [lax.ppermute(x, 'energy', backward) for x in fields]  4.74 us
    ppermute x2, waiting for transfers between devices, body(): high = [lax.ppermute(x, 'energy', backward) for x in fields]  4.09 us
  transfers between devices with their start and end apart: 21, of which 10 were waited for; matrix products, arithmetic and copies ran while one was open for 0% of the time, Pallas kernels for 8%

profile of v3, /device:TPU:25, one launch (start us, length us, event | category | flops | bytes accessed | tf_op | source)
XLA Modules:
  0.0 105.4 jit_solution(10969584799569398639)
XLA Ops:
  0.8 1.3 %copy-done = bf16[2,1,144,2048]{3,2,1,0:T(8,128)(2,1)S(1)} copy-done((bf16[2,1,144,2048]{3,2,1,0:T(8,128)(2,1)S(1)}, bf16[2,1,144,2048]{3,2,1,0:T(8,128)(2,1)}, u32[]{:S(2)}) %copy-start) | copy-done | bytes 1179672
  2.0 0.9 shard_map.110
  3.8 1.4 %collective-permute-done.refs_1_ = bf16[3,592,128]{2,1,0:T(8,128)(2,1)S(1)} collective-permute-done((bf16[3,592,128]{2,1,0:T(8,128)(2,1)S(1)}, bf16[3,592,128]{2,1,0:T(8,128)(2,1)S(1)}, u32[]{:S(2)}, u32[]{:S(2)}) %collective-permute-start) | collective-permute-done | bytes 454688 | tf_op jit(solution)/shard_map/ppermute | solution.py:317
  5.3 5.7 %collective-permute-start.1 = (bf16[2,592,128]{2,1,0:T(8,128)(2,1)S(1)}, bf16[2,592,128]{2,1,0:T(8,128)(2,1)S(1)}, u32[]{:S(2)}, u32[]{:S(2)}) collective-permute-start(bf16[2,592,128]{2,1,0:T(8,128)(2,1)S(1)} %get-tuple-element.38), channel_id=1, source_target_pairs={{0,2},{1,15},{2,4},{3,1},{4,6},{5,3},{6,8},{7,5},{8,10},{9,7},{10,... | collective-permute-start | bytes 909320 | tf_op jit(solution)/shard_map/ppermute | solution.py:323
  10.9 1.2 %collective-permute-start.2 = (bf16[2,592,128]{2,1,0:T(8,128)(2,1)S(1)}, bf16[2,592,128]{2,1,0:T(8,128)(2,1)S(1)}, u32[]{:S(2)}, u32[]{:S(2)}) collective-permute-start(bf16[2,592,128]{2,1,0:T(8,128)(2,1)S(1)} %get-tuple-element.39), channel_id=1, source_target_pairs={{0,4},{1,13},{2,6},{3,15},{4,8},{5,1},{6,10},{7,3},{8,12},{9,5},{1... | collective-permute-start | bytes 909320 | tf_op jit(solution)/shard_map/ppermute | solution.py:323
  12.6 5.0 %collective-permute-done.1.refs_0_ = bf16[2,592,128]{2,1,0:T(8,128)(2,1)S(1)} collective-permute-done((bf16[2,592,128]{2,1,0:T(8,128)(2,1)S(1)}, bf16[2,592,128]{2,1,0:T(8,128)(2,1)S(1)}, u32[]{:S(2)}, u32[]{:S(2)}) %collective-permute-start.1) | collective-permute-done | bytes 303136 | tf_op jit(solution)/shard_map/ppermute | solution.py:323
  17.5 5.6 %collective-permute-done.2.refs_1_ = bf16[2,592,128]{2,1,0:T(8,128)(2,1)S(1)} collective-permute-done((bf16[2,592,128]{2,1,0:T(8,128)(2,1)S(1)}, bf16[2,592,128]{2,1,0:T(8,128)(2,1)S(1)}, u32[]{:S(2)}, u32[]{:S(2)}) %collective-permute-start.2) | collective-permute-done | bytes 303136 | tf_op jit(solution)/shard_map/ppermute | solution.py:323
  23.2 2.8 %collective-permute-start.5 = (bf16[5,576,128]{2,1,0:T(8,128)(2,1)S(1)}, bf16[5,576,128]{2,1,0:T(8,128)(2,1)S(1)}, u32[]{:S(2)}, u32[]{:S(2)}) collective-permute-start(bf16[5,576,128]{2,1,0:T(8,128)(2,1)S(1)} %get-tuple-element.46.refs_3_), channel_id=1, source_target_pairs={{0,16},{16,32},{32,48},{48,64},{64,80},{80,96},{96,112},{112,128},... | collective-permute-start | bytes 2211848 | tf_op jit(solution)/shard_map/ppermute | solution.py:348
  25.9 2.5 %collective-permute-start.7 = (bf16[5,576,128]{2,1,0:T(8,128)(2,1)S(1)}, bf16[5,576,128]{2,1,0:T(8,128)(2,1)S(1)}, u32[]{:S(2)}, u32[]{:S(2)}) collective-permute-start(bf16[5,576,128]{2,1,0:T(8,128)(2,1)S(1)} %get-tuple-element.46.refs_3_), channel_id=1, source_target_pairs={{16,0},{32,16},{48,32},{64,48},{80,64},{96,80},{112,96},{128,112},... | collective-permute-start | bytes 2211848 | tf_op jit(solution)/shard_map/ppermute | solution.py:349
  28.5 3.8 %collective-permute-start.4 = (bf16[1,592,128]{2,1,0:T(8,128)(2,1)S(1)}, bf16[1,592,128]{2,1,0:T(8,128)(2,1)S(1)}, u32[]{:S(2)}, u32[]{:S(2)}) collective-permute-start(bf16[1,592,128]{2,1,0:T(8,128)(2,1)S(1)} %get-tuple-element.43), channel_id=1, source_target_pairs={{0,8},{1,9},{2,10},{3,11},{4,12},{5,13},{6,14},{7,15},{8,0},{9,1},... | collective-permute-start | bytes 454664 | tf_op jit(solution)/shard_map/ppermute | solution.py:323
  32.3 10.4 %collective-permute-done.4.refs_1_ = bf16[1,592,128]{2,1,0:T(8,128)(2,1)S(1)} collective-permute-done((bf16[1,592,128]{2,1,0:T(8,128)(2,1)S(1)}, bf16[1,592,128]{2,1,0:T(8,128)(2,1)S(1)}, u32[]{:S(2)}, u32[]{:S(2)}) %collective-permute-start.4) | collective-permute-done | bytes 151584 | tf_op jit(solution)/shard_map/ppermute | solution.py:323
  42.7 3.1 %collective-permute-start.6 = (bf16[3,576,128]{2,1,0:T(8,128)(2,1)S(1)}, bf16[3,576,128]{2,1,0:T(8,128)(2,1)S(1)}, u32[]{:S(2)}, u32[]{:S(2)}) collective-permute-start(bf16[3,576,128]{2,1,0:T(8,128)(2,1)S(1)} %get-tuple-element.47.refs_4_), channel_id=1, source_target_pairs={{0,16},{16,32},{32,48},{48,64},{64,80},{80,96},{96,112},{112,128},... | collective-permute-start | bytes 1327112 | tf_op jit(solution)/shard_map/ppermute | solution.py:348
  45.8 2.2 %collective-permute-start.8 = (bf16[3,576,128]{2,1,0:T(8,128)(2,1)S(1)}, bf16[3,576,128]{2,1,0:T(8,128)(2,1)S(1)}, u32[]{:S(2)}, u32[]{:S(2)}) collective-permute-start(bf16[3,576,128]{2,1,0:T(8,128)(2,1)S(1)} %get-tuple-element.47.refs_4_), channel_id=1, source_target_pairs={{16,0},{32,16},{48,32},{64,48},{80,64},{96,80},{112,96},{128,112},... | collective-permute-start | bytes 1327112 | tf_op jit(solution)/shard_map/ppermute | solution.py:349
  48.1 2.7 %shard_map.109 = (bf16[512,768]{1,0:T(8,128)(2,1)S(1)}, bf16[144,1152]{1,0:T(8,128)(2,1)S(1)}) custom-call(s32[2]{0:T(128)S(1)} %pad_add_fusion.refs_0_, s32[8]{0:T(128)S(1)} %copy-done.8, f32[2,8,16]{2,1,0:T(8,128)S(1)} %copy-done.7, f32[8,12,12]{2,1,0:T(8,128)S(1)} %copy.12.refs_3_, s32[32,48]{1,0:T(8,128)S(1)} %copy-done.5, s32[32,48]{1,0:T(8,128)S(1)} %copy-done.6, ...), custom_call_target="tpu_custom_call" | custom-call | flops 1 | bytes 1 | tf_op jit(solution)/shard_map/pallas_call | solution.py:34
  50.9 5.0 %collective-permute-done.6.refs_2_ = bf16[3,576,128]{2,1,0:T(8,128)(2,1)S(1)} collective-permute-done((bf16[3,576,128]{2,1,0:T(8,128)(2,1)S(1)}, bf16[3,576,128]{2,1,0:T(8,128)(2,1)S(1)}, u32[]{:S(2)}, u32[]{:S(2)}) %collective-permute-start.6) | collective-permute-done | bytes 442400 | tf_op jit(solution)/shard_map/ppermute | solution.py:348
  55.8 4.1 %collective-permute-done.8.refs_6_ = bf16[3,576,128]{2,1,0:T(8,128)(2,1)S(1)} collective-permute-done((bf16[3,576,128]{2,1,0:T(8,128)(2,1)S(1)}, bf16[3,576,128]{2,1,0:T(8,128)(2,1)S(1)}, u32[]{:S(2)}, u32[]{:S(2)}) %collective-permute-start.8) | collective-permute-done | bytes 442400 | tf_op jit(solution)/shard_map/ppermute | solution.py:349
  59.9 2.0 %shard_map.114 = (f32[8,288,128]{2,1,0:T(8,128)S(1)}, bf16[8,288,128]{2,1,0:T(8,128)(2,1)S(1)}) custom-call(bf16[512,768]{1,0:T(8,128)(2,1)S(1)} %get-tuple-element.45.refs_0_, bf16[5,576,128]{2,1,0:T(8,128)(2,1)S(1)} %collective-permute-done.5.refs_1_, bf16[3,576,128]{2,1,0:T(8,128)(2,1)S(1)} %collective-permute-done.6.refs_2_, ...), custom_call_target="tpu_custom_call" | custom-call | flops 1 | bytes 1 | tf_op jit(solution)/shard_map/pallas_call | solution.py:34
  61.9 2.5 %collective-permute-start.9 = (bf16[8,288,128]{2,1,0:T(8,128)(2,1)S(1)}, bf16[8,288,128]{2,1,0:T(8,128)(2,1)S(1)}, u32[]{:S(2)}, u32[]{:S(2)}) collective-permute-start(bf16[8,288,128]{2,1,0:T(8,128)(2,1)S(1)} %get-tuple-element.49), channel_id=1, source_target_pairs={{0,1},{1,0},{2,3},{3,2},{4,5},{5,4},{6,7},{7,6},{8,9},{9,8},{10,11... | collective-permute-start | bytes 1769480 | tf_op jit(solution)/shard_map/ppermute | solution.py:317
  64.5 2.0 %shard_map.118 = (f32[8,288,128]{2,1,0:T(8,128)S(1)}, bf16[8,288,128]{2,1,0:T(8,128)(2,1)S(1)}) custom-call(bf16[512,768]{1,0:T(8,128)(2,1)S(1)} %get-tuple-element.45.refs_0_, bf16[5,576,128]{2,1,0:T(8,128)(2,1)S(1)} %collective-permute-done.5.refs_1_, bf16[3,576,128]{2,1,0:T(8,128)(2,1)S(1)} %collective-permute-done.6.refs_2_, ...), custom_call_target="tpu_custom_call" | custom-call | flops 1 | bytes 1 | tf_op jit(solution)/shard_map/pallas_call | solution.py:34
  66.8 3.7 %collective-permute-start.10 = (bf16[1,288,128]{2,1,0:T(8,128)(2,1)S(1)}, bf16[1,288,128]{2,1,0:T(8,128)(2,1)S(1)}, u32[]{:S(2)}, u32[]{:S(2)}) collective-permute-start(bf16[1,288,128]{2,1,0:T(8,128)(2,1)S(1)} %get-tuple-element.50), channel_id=1, source_target_pairs={{0,8},{1,9},{2,10},{3,11},{4,12},{5,13},{6,14},{7,15},{8,0},{9,1},... | collective-permute-start | bytes 221192 | tf_op jit(solution)/shard_map/ppermute | solution.py:323
  70.4 2.0 %collective-permute-start.13 = (bf16[2,288,128]{2,1,0:T(8,128)(2,1)S(1)}, bf16[2,288,128]{2,1,0:T(8,128)(2,1)S(1)}, u32[]{:S(2)}, u32[]{:S(2)}) collective-permute-start(bf16[2,288,128]{2,1,0:T(8,128)(2,1)S(1)} %get-tuple-element.53), channel_id=1, source_target_pairs={{0,2},{1,15},{2,4},{3,1},{4,6},{5,3},{6,8},{7,5},{8,10},{9,7},{10,... | collective-permute-start | bytes 442376 | tf_op jit(solution)/shard_map/ppermute | solution.py:323
  72.5 3.6 %collective-permute-start.17 = (bf16[2,288,128]{2,1,0:T(8,128)(2,1)S(1)}, bf16[2,288,128]{2,1,0:T(8,128)(2,1)S(1)}, u32[]{:S(2)}, u32[]{:S(2)}) collective-permute-start(bf16[2,288,128]{2,1,0:T(8,128)(2,1)S(1)} %get-tuple-element.61), channel_id=1, source_target_pairs={{0,6},{1,11},{2,8},{3,13},{4,10},{5,15},{6,12},{7,1},{8,14},{9,3},... | collective-permute-start | bytes 442376 | tf_op jit(solution)/shard_map/ppermute | solution.py:323
  76.2 1.3 %collective-permute-done.10.refs_5_.refs_4_ = bf16[1,288,128]{2,1,0:T(8,128)(2,1)S(1)} collective-permute-done((bf16[1,288,128]{2,1,0:T(8,128)(2,1)S(1)}, bf16[1,288,128]{2,1,0:T(8,128)(2,1)S(1)}, u32[]{:S(2)}, u32[]{:S(2)}) %collective-permute-start.10) | collective-permute-done | bytes 73760 | tf_op jit(solution)/shard_map/ppermute | solution.py:323
  77.5 0.9 collective-permute-done.11.refs_2_.refs_5_
  78.3 3.1 %collective-permute-start.19 = (bf16[2,288,128]{2,1,0:T(8,128)(2,1)S(1)}, bf16[2,288,128]{2,1,0:T(8,128)(2,1)S(1)}, u32[]{:S(2)}, u32[]{:S(2)}) collective-permute-start(bf16[2,288,128]{2,1,0:T(8,128)(2,1)S(1)} %get-tuple-element.63), channel_id=1, source_target_pairs={{0,2},{1,15},{2,4},{3,1},{4,6},{5,3},{6,8},{7,5},{8,10},{9,7},{10,... | collective-permute-start | bytes 442376 | tf_op jit(solution)/shard_map/ppermute | solution.py:323
  81.4 4.5 %collective-permute-start.16 = (bf16[1,288,128]{2,1,0:T(8,128)(2,1)S(1)}, bf16[1,288,128]{2,1,0:T(8,128)(2,1)S(1)}, u32[]{:S(2)}, u32[]{:S(2)}) collective-permute-start(bf16[1,288,128]{2,1,0:T(8,128)(2,1)S(1)} %get-tuple-element.60), channel_id=1, source_target_pairs={{0,8},{1,9},{2,10},{3,11},{4,12},{5,13},{6,14},{7,15},{8,0},{9,1},... | collective-permute-start | bytes 221192 | tf_op jit(solution)/shard_map/ppermute | solution.py:323
  86.0 1.0 collective-permute-start.14
  86.9 5.0 %collective-permute-done.16.refs_3_.refs_5_ = bf16[1,288,128]{2,1,0:T(8,128)(2,1)S(1)} collective-permute-done((bf16[1,288,128]{2,1,0:T(8,128)(2,1)S(1)}, bf16[1,288,128]{2,1,0:T(8,128)(2,1)S(1)}, u32[]{:S(2)}, u32[]{:S(2)}) %collective-permute-start.16) | collective-permute-done | bytes 73760 | tf_op jit(solution)/shard_map/ppermute | solution.py:323
  91.9 2.0 %collective-permute-done.19.refs_0_.refs_8_ = bf16[2,288,128]{2,1,0:T(8,128)(2,1)S(1)} collective-permute-done((bf16[2,288,128]{2,1,0:T(8,128)(2,1)S(1)}, bf16[2,288,128]{2,1,0:T(8,128)(2,1)S(1)}, u32[]{:S(2)}, u32[]{:S(2)}) %collective-permute-start.19) | collective-permute-done | bytes 147488 | tf_op jit(solution)/shard_map/ppermute | solution.py:323
  94.0 3.8 %collective-permute-start.20 = (bf16[864,128]{1,0:T(8,128)(2,1)S(1)}, bf16[864,128]{1,0:T(8,128)(2,1)S(1)}, u32[]{:S(2)}, u32[]{:S(2)}) collective-permute-start(bf16[864,128]{1,0:T(8,128)(2,1)S(1)} %shard_map.120), channel_id=1, source_target_pairs={{0,1},{1,0},{2,3},{3,2},{4,5},{5,4},{6,7},{7,6},{8,9},{9,8},{10,11... | collective-permute-start | bytes 663560 | tf_op jit(solution)/shard_map/ppermute | solution.py:317
  97.7 3.0 %shard_map.117 = (bf16[2,144,896]{2,1,0:T(8,128)(2,1)S(1)}, bf16[16,16,128]{2,1,0:T(8,128)(2,1)S(1)}, bf16[288,192]{1,0:T(8,128)(2,1)S(1)}) custom-call(s32[2]{0:T(128)S(1)} %pad_add_fusion.refs_0_, bf16[144,1152]{1,0:T(8,128)(2,1)S(1)} %get-tuple-element.35.refs_1_, bf16[5,16,128]{2,1,0:T(8,128)(2,1)S(1)} %get-tuple-element.41.refs_3_.refs_2_, ...), custom_call_target="tpu_custom_call" | custom-call | flops 1 | bytes 1 | tf_op jit(solution)/shard_map/pallas_call | solution.py:34
  100.8 4.6 %shard_map.121 = bf16[2,144,2048]{2,1,0:T(8,128)(2,1)} custom-call(s32[2]{0:T(128)S(1)} %pad_add_fusion.refs_0_, bf16[144,1152]{1,0:T(8,128)(2,1)S(1)} %get-tuple-element.35.refs_1_, bf16[16,16,128]{2,1,0:T(8,128)(2,1)S(1)} %get-tuple-element.55.refs_2_, bf16[2,144,896]{2,1,0:T(8,128)(2,1)S(1)} %get-tuple-element.56.refs_3_, ...), custom_call_target="tpu_custom_call" | custom-call | flops 1 | bytes 1 | tf_op jit(solution)/shard_map/pallas_call | solution.py:34
  (48 shorter events, 2.7 us)
Async XLA Ops:
  0.8 1.3 %copy-start = (bf16[2,1,144,2048]{3,2,1,0:T(8,128)(2,1)S(1)}, bf16[2,1,144,2048]{3,2,1,0:T(8,128)(2,1)}, u32[]{:S(2)}) copy-start(bf16[2,1,144,2048]{3,2,1,0:T(8,128)(2,1)} %param.11) | copy-start | bytes 3538948
  2.9 45.1 %copy-start.9 = (f32[8,12,12]{2,0,1:T(8,128)S(1)}, f32[8,12,12]{2,0,1:T(8,128)}, u32[]{:S(2)}) copy-start(f32[8,12,12]{2,0,1:T(8,128)} %param.15) | copy-start | bytes 13828
  2.9 45.1 %copy-start.1 = (f32[96,1152]{1,0:T(8,128)S(1)}, f32[96,1152]{1,0:T(8,128)}, u32[]{:S(2)}) copy-start(f32[96,1152]{1,0:T(8,128)} %constant.32.clone.refs_8_) | copy-start | bytes 1327108
  2.9 45.1 %copy-start.2 = (f32[96,1152]{1,0:T(8,128)S(1)}, f32[96,1152]{1,0:T(8,128)}, u32[]{:S(2)}) copy-start(f32[96,1152]{1,0:T(8,128)} %constant.33.clone.refs_9_) | copy-start | bytes 1327108
  2.9 45.1 %copy-start.3 = (f32[144,12]{1,0:T(8,128)S(1)}, f32[144,12]{1,0:T(8,128)}, u32[]{:S(2)}) copy-start(f32[144,12]{1,0:T(8,128)} %constant.30.clone.refs_6_) | copy-start | bytes 20740
  3.0 45.1 %copy-start.4 = (f32[144,12]{1,0:T(8,128)S(1)}, f32[144,12]{1,0:T(8,128)}, u32[]{:S(2)}) copy-start(f32[144,12]{1,0:T(8,128)} %constant.31.clone.refs_7_) | copy-start | bytes 20740
  3.0 45.1 %copy-start.5 = (s32[32,48]{1,0:T(8,128)S(1)}, s32[32,48]{1,0:T(8,128)}, u32[]{:S(2)}) copy-start(s32[32,48]{1,0:T(8,128)} %constant.28.clone.refs_4_) | copy-start | bytes 18436
  3.0 45.1 %copy-start.6 = (s32[32,48]{1,0:T(8,128)S(1)}, s32[32,48]{1,0:T(8,128)}, u32[]{:S(2)}) copy-start(s32[32,48]{1,0:T(8,128)} %constant.29.clone.refs_5_) | copy-start | bytes 18436
  3.0 45.1 %copy-start.7 = (f32[2,8,16]{2,1,0:T(8,128)S(1)}, f32[2,8,16]{2,1,0:T(8,128)}, u32[]{:S(2)}) copy-start(f32[2,8,16]{2,1,0:T(8,128)} %refs_2_.1) | copy-start | bytes 3076
  3.0 45.1 %copy-start.8 = (s32[8]{0:T(128)S(1)}, s32[8]{0:T(128)}, u32[]{:S(2)}) copy-start(s32[8]{0:T(128)} %refs_1_.1) | copy-start | bytes 100
  3.0 2.2 %collective-permute-start = (bf16[3,592,128]{2,1,0:T(8,128)(2,1)S(1)}, bf16[3,592,128]{2,1,0:T(8,128)(2,1)S(1)}, u32[]{:S(2)}, u32[]{:S(2)}) collective-permute-start(bf16[3,592,128]{2,1,0:T(8,128)(2,1)S(1)} %get-tuple-element.37), channel_id=1, source_target_pairs={{0,1},{1,0},{2,3},{3,2},{4,5},{5,4},{6,7},{7,6},{8,9},{9,8},{10,11... | collective-permute-start | bytes 1363976 | tf_op jit(solution)/shard_map/ppermute | solution.py:317
  5.3 12.3 %collective-permute-start.1 = (bf16[2,592,128]{2,1,0:T(8,128)(2,1)S(1)}, bf16[2,592,128]{2,1,0:T(8,128)(2,1)S(1)}, u32[]{:S(2)}, u32[]{:S(2)}) collective-permute-start(bf16[2,592,128]{2,1,0:T(8,128)(2,1)S(1)} %get-tuple-element.38), channel_id=1, source_target_pairs={{0,2},{1,15},{2,4},{3,1},{4,6},{5,3},{6,8},{7,5},{8,10},{9,7},{10,... | collective-permute-start | bytes 909320 | tf_op jit(solution)/shard_map/ppermute | solution.py:323
  10.9 12.2 %collective-permute-start.2 = (bf16[2,592,128]{2,1,0:T(8,128)(2,1)S(1)}, bf16[2,592,128]{2,1,0:T(8,128)(2,1)S(1)}, u32[]{:S(2)}, u32[]{:S(2)}) collective-permute-start(bf16[2,592,128]{2,1,0:T(8,128)(2,1)S(1)} %get-tuple-element.39), channel_id=1, source_target_pairs={{0,4},{1,13},{2,6},{3,15},{4,8},{5,1},{6,10},{7,3},{8,12},{9,5},{1... | collective-permute-start | bytes 909320 | tf_op jit(solution)/shard_map/ppermute | solution.py:323
  12.1 30.6 %collective-permute-start.3 = (bf16[2,592,128]{2,1,0:T(8,128)(2,1)S(1)}, bf16[2,592,128]{2,1,0:T(8,128)(2,1)S(1)}, u32[]{:S(2)}, u32[]{:S(2)}) collective-permute-start(bf16[2,592,128]{2,1,0:T(8,128)(2,1)S(1)} %get-tuple-element.42), channel_id=1, source_target_pairs={{0,6},{1,11},{2,8},{3,13},{4,10},{5,15},{6,12},{7,1},{8,14},{9,3},... | collective-permute-start | bytes 909320 | tf_op jit(solution)/shard_map/ppermute | solution.py:323
  23.2 36.8 %collective-permute-start.5 = (bf16[5,576,128]{2,1,0:T(8,128)(2,1)S(1)}, bf16[5,576,128]{2,1,0:T(8,128)(2,1)S(1)}, u32[]{:S(2)}, u32[]{:S(2)}) collective-permute-start(bf16[5,576,128]{2,1,0:T(8,128)(2,1)S(1)} %get-tuple-element.46.refs_3_), channel_id=1, source_target_pairs={{0,16},{16,32},{32,48},{48,64},{64,80},{80,96},{96,112},{112,128},... | collective-permute-start | bytes 2211848 | tf_op jit(solution)/shard_map/ppermute | solution.py:348
  25.9 34.0 %collective-permute-start.7 = (bf16[5,576,128]{2,1,0:T(8,128)(2,1)S(1)}, bf16[5,576,128]{2,1,0:T(8,128)(2,1)S(1)}, u32[]{:S(2)}, u32[]{:S(2)}) collective-permute-start(bf16[5,576,128]{2,1,0:T(8,128)(2,1)S(1)} %get-tuple-element.46.refs_3_), channel_id=1, source_target_pairs={{16,0},{32,16},{48,32},{64,48},{80,64},{96,80},{112,96},{128,112},... | collective-permute-start | bytes 2211848 | tf_op jit(solution)/shard_map/ppermute | solution.py:349
  28.5 14.2 %collective-permute-start.4 = (bf16[1,592,128]{2,1,0:T(8,128)(2,1)S(1)}, bf16[1,592,128]{2,1,0:T(8,128)(2,1)S(1)}, u32[]{:S(2)}, u32[]{:S(2)}) collective-permute-start(bf16[1,592,128]{2,1,0:T(8,128)(2,1)S(1)} %get-tuple-element.43), channel_id=1, source_target_pairs={{0,8},{1,9},{2,10},{3,11},{4,12},{5,13},{6,14},{7,15},{8,0},{9,1},... | collective-permute-start | bytes 454664 | tf_op jit(solution)/shard_map/ppermute | solution.py:323
  42.7 13.1 %collective-permute-start.6 = (bf16[3,576,128]{2,1,0:T(8,128)(2,1)S(1)}, bf16[3,576,128]{2,1,0:T(8,128)(2,1)S(1)}, u32[]{:S(2)}, u32[]{:S(2)}) collective-permute-start(bf16[3,576,128]{2,1,0:T(8,128)(2,1)S(1)} %get-tuple-element.47.refs_4_), channel_id=1, source_target_pairs={{0,16},{16,32},{32,48},{48,64},{64,80},{80,96},{96,112},{112,128},... | collective-permute-start | bytes 1327112 | tf_op jit(solution)/shard_map/ppermute | solution.py:348
  45.8 14.2 %collective-permute-start.8 = (bf16[3,576,128]{2,1,0:T(8,128)(2,1)S(1)}, bf16[3,576,128]{2,1,0:T(8,128)(2,1)S(1)}, u32[]{:S(2)}, u32[]{:S(2)}) collective-permute-start(bf16[3,576,128]{2,1,0:T(8,128)(2,1)S(1)} %get-tuple-element.47.refs_4_), channel_id=1, source_target_pairs={{16,0},{32,16},{48,32},{64,48},{80,64},{96,80},{112,96},{128,112},... | collective-permute-start | bytes 1327112 | tf_op jit(solution)/shard_map/ppermute | solution.py:349
  61.9 4.6 %collective-permute-start.9 = (bf16[8,288,128]{2,1,0:T(8,128)(2,1)S(1)}, bf16[8,288,128]{2,1,0:T(8,128)(2,1)S(1)}, u32[]{:S(2)}, u32[]{:S(2)}) collective-permute-start(bf16[8,288,128]{2,1,0:T(8,128)(2,1)S(1)} %get-tuple-element.49), channel_id=1, source_target_pairs={{0,1},{1,0},{2,3},{3,2},{4,5},{5,4},{6,7},{7,6},{8,9},{9,8},{10,11... | collective-permute-start | bytes 1769480 | tf_op jit(solution)/shard_map/ppermute | solution.py:317
  66.5 6.0 %collective-permute-start.15 = (bf16[8,288,128]{2,1,0:T(8,128)(2,1)S(1)}, bf16[8,288,128]{2,1,0:T(8,128)(2,1)S(1)}, u32[]{:S(2)}, u32[]{:S(2)}) collective-permute-start(bf16[8,288,128]{2,1,0:T(8,128)(2,1)S(1)} %get-tuple-element.59), channel_id=1, source_target_pairs={{0,1},{1,0},{2,3},{3,2},{4,5},{5,4},{6,7},{7,6},{8,9},{9,8},{10,11... | collective-permute-start | bytes 1769480 | tf_op jit(solution)/shard_map/ppermute | solution.py:317
  66.7 11.7 %collective-permute-start.11 = (bf16[2,288,128]{2,1,0:T(8,128)(2,1)S(1)}, bf16[2,288,128]{2,1,0:T(8,128)(2,1)S(1)}, u32[]{:S(2)}, u32[]{:S(2)}) collective-permute-start(bf16[2,288,128]{2,1,0:T(8,128)(2,1)S(1)} %get-tuple-element.51), channel_id=1, source_target_pairs={{0,6},{1,11},{2,8},{3,13},{4,10},{5,15},{6,12},{7,1},{8,14},{9,3},... | collective-permute-start | bytes 442376 | tf_op jit(solution)/shard_map/ppermute | solution.py:323
  66.8 10.7 %collective-permute-start.10 = (bf16[1,288,128]{2,1,0:T(8,128)(2,1)S(1)}, bf16[1,288,128]{2,1,0:T(8,128)(2,1)S(1)}, u32[]{:S(2)}, u32[]{:S(2)}) collective-permute-start(bf16[1,288,128]{2,1,0:T(8,128)(2,1)S(1)} %get-tuple-element.50), channel_id=1, source_target_pairs={{0,8},{1,9},{2,10},{3,11},{4,12},{5,13},{6,14},{7,15},{8,0},{9,1},... | collective-permute-start | bytes 221192 | tf_op jit(solution)/shard_map/ppermute | solution.py:323
  70.4 11.0 %collective-permute-start.12 = (bf16[2,288,128]{2,1,0:T(8,128)(2,1)S(1)}, bf16[2,288,128]{2,1,0:T(8,128)(2,1)S(1)}, u32[]{:S(2)}, u32[]{:S(2)}) collective-permute-start(bf16[2,288,128]{2,1,0:T(8,128)(2,1)S(1)} %get-tuple-element.52), channel_id=1, source_target_pairs={{0,4},{1,13},{2,6},{3,15},{4,8},{5,1},{6,10},{7,3},{8,12},{9,5},{1... | collective-permute-start | bytes 442376 | tf_op jit(solution)/shard_map/ppermute | solution.py:323
  70.4 15.5 %collective-permute-start.13 = (bf16[2,288,128]{2,1,0:T(8,128)(2,1)S(1)}, bf16[2,288,128]{2,1,0:T(8,128)(2,1)S(1)}, u32[]{:S(2)}, u32[]{:S(2)}) collective-permute-start(bf16[2,288,128]{2,1,0:T(8,128)(2,1)S(1)} %get-tuple-element.53), channel_id=1, source_target_pairs={{0,2},{1,15},{2,4},{3,1},{4,6},{5,3},{6,8},{7,5},{8,10},{9,7},{10,... | collective-permute-start | bytes 442376 | tf_op jit(solution)/shard_map/ppermute | solution.py:323
  72.5 19.4 %collective-permute-start.17 = (bf16[2,288,128]{2,1,0:T(8,128)(2,1)S(1)}, bf16[2,288,128]{2,1,0:T(8,128)(2,1)S(1)}, u32[]{:S(2)}, u32[]{:S(2)}) collective-permute-start(bf16[2,288,128]{2,1,0:T(8,128)(2,1)S(1)} %get-tuple-element.61), channel_id=1, source_target_pairs={{0,6},{1,11},{2,8},{3,13},{4,10},{5,15},{6,12},{7,1},{8,14},{9,3},... | collective-permute-start | bytes 442376 | tf_op jit(solution)/shard_map/ppermute | solution.py:323
  77.5 14.5 %collective-permute-start.18 = (bf16[2,288,128]{2,1,0:T(8,128)(2,1)S(1)}, bf16[2,288,128]{2,1,0:T(8,128)(2,1)S(1)}, u32[]{:S(2)}, u32[]{:S(2)}) collective-permute-start(bf16[2,288,128]{2,1,0:T(8,128)(2,1)S(1)} %get-tuple-element.62), channel_id=1, source_target_pairs={{0,4},{1,13},{2,6},{3,15},{4,8},{5,1},{6,10},{7,3},{8,12},{9,5},{1... | collective-permute-start | bytes 442376 | tf_op jit(solution)/shard_map/ppermute | solution.py:323
  78.3 15.6 %collective-permute-start.19 = (bf16[2,288,128]{2,1,0:T(8,128)(2,1)S(1)}, bf16[2,288,128]{2,1,0:T(8,128)(2,1)S(1)}, u32[]{:S(2)}, u32[]{:S(2)}) collective-permute-start(bf16[2,288,128]{2,1,0:T(8,128)(2,1)S(1)} %get-tuple-element.63), channel_id=1, source_target_pairs={{0,2},{1,15},{2,4},{3,1},{4,6},{5,3},{6,8},{7,5},{8,10},{9,7},{10,... | collective-permute-start | bytes 442376 | tf_op jit(solution)/shard_map/ppermute | solution.py:323
  81.4 10.5 %collective-permute-start.16 = (bf16[1,288,128]{2,1,0:T(8,128)(2,1)S(1)}, bf16[1,288,128]{2,1,0:T(8,128)(2,1)S(1)}, u32[]{:S(2)}, u32[]{:S(2)}) collective-permute-start(bf16[1,288,128]{2,1,0:T(8,128)(2,1)S(1)} %get-tuple-element.60), channel_id=1, source_target_pairs={{0,8},{1,9},{2,10},{3,11},{4,12},{5,13},{6,14},{7,15},{8,0},{9,1},... | collective-permute-start | bytes 221192 | tf_op jit(solution)/shard_map/ppermute | solution.py:323
  86.0 11.8 %collective-permute-start.14 = (bf16[992,128]{1,0:T(8,128)(2,1)S(1)}, bf16[992,128]{1,0:T(8,128)(2,1)S(1)}, u32[]{:S(2)}, u32[]{:S(2)}) collective-permute-start(bf16[992,128]{1,0:T(8,128)(2,1)S(1)} %shard_map.116), channel_id=1, source_target_pairs={{0,1},{1,0},{2,3},{3,2},{4,5},{5,4},{6,7},{7,6},{8,9},{9,8},{10,11... | collective-permute-start | bytes 761864 | tf_op jit(solution)/shard_map/ppermute | solution.py:317
  94.0 6.8 %collective-permute-start.20 = (bf16[864,128]{1,0:T(8,128)(2,1)S(1)}, bf16[864,128]{1,0:T(8,128)(2,1)S(1)}, u32[]{:S(2)}, u32[]{:S(2)}) collective-permute-start(bf16[864,128]{1,0:T(8,128)(2,1)S(1)} %shard_map.120), channel_id=1, source_target_pairs={{0,1},{1,0},{2,3},{3,2},{4,5},{5,4},{6,7},{7,6},{8,9},{9,8},{10,11... | collective-permute-start | bytes 663560 | tf_op jit(solution)/shard_map/ppermute | solution.py:317

commit v4 on v3

--- a/solution.py
+++ b/solution.py
@@ -24,7 +24,10 @@
 
 NEAR = (1, 2, 3)
 EARLY = ((1, 0), (1, 1), (2, 0), (2, 1), (0, 0))
-PLACES = EARLY + ((3, 0), (3, 1), (4, 0))
+LATE = ((3, 0), (3, 1), (4, 0))
+PLACES = EARLY + LATE
+SEEN = ((-1, EARLY), (0, EARLY), (1, EARLY), (0, LATE))
+LAST = ((-1, LATE), (1, LATE))
 
 
 def call(kernel, outs, *args, scratch=(), after=()):
@@ -43,21 +46,20 @@
 
 
 def mixing_index(e_dev):
-    rel = np.zeros((e_dev, 2, 8, 3, 8, e_dev), np.int32)
+    columns = [(tile, place, e) for parts in (SEEN, LAST) for tile, part in parts for place in part for e in range(e_dev)]
+    rel = np.zeros((e_dev, 2, len(PLACES), len(columns)), np.int32)
     mom = np.zeros_like(rel)
-    for e_out in range(e_dev):
-        for tile in range(3):
-            for e_in in range(e_dev):
-                rel[e_out, :, :, tile, :, e_in] = (tile - 1) * e_dev + e_in - e_out + OFFSET
-    for d, (j_to, to_other) in enumerate(PLACES):
-        for s, (j_from, from_other) in enumerate(PLACES):
-            mom[:, 0, d, :, s, :] = 2 * (j_to + j_from) + to_other - from_other
-            mom[:, 1, d, :, s, :] = 2 * (j_from - j_to) + 1 - to_other - from_other
-    return rel.reshape(e_dev * 16, -1), mom.reshape(e_dev * 16, -1)
+    for at, (tile, (j_from, from_other), e_in) in enumerate(columns):
+        for e_out in range(e_dev):
+            rel[e_out, ..., at] = tile * e_dev + e_in - e_out + OFFSET
+        for d, (j_to, to_other) in enumerate(PLACES):
+            mom[:, 0, d, at] = 2 * (j_to + j_from) + to_other - from_other
+            mom[:, 1, d, at] = 2 * (j_from - j_to) + 1 - to_other - from_other
+    return rel.reshape(-1, len(columns)), mom.reshape(-1, len(columns))
 
 
 def tables_kernel(moms, pos_ref, offsets_ref, phonon_ref, coupling_ref, rel_ref, mom_ref, first_ref, second_ref,
-                  wide_first_ref, wide_second_ref, mix_ref, pair_ref):
+                  wide_first_ref, wide_second_ref, seen_ref, last_ref, pair_ref):
     slots = coupling_ref.shape[0]
     taps = jnp.zeros((8, moms), F32)
     row = lax.broadcasted_iota(jnp.int32, (8, moms), 0)
@@ -74,13 +76,17 @@
     outs, ins = table.shape
     tall = (lax.broadcasted_iota(jnp.int32, (outs * ROWS, outs), 0) >> 4) == lax.broadcasted_iota(
         jnp.int32, (outs * ROWS, outs), 1)
-    flat = lax.broadcasted_iota(jnp.int32, (ins, ins * ROWS), 0) == (
-        lax.broadcasted_iota(jnp.int32, (ins, ins * ROWS), 1) >> 4)
     half = jnp.dot(tall.astype(BF16), table.astype(BF16), preferred_element_type=F32).astype(BF16)
-    full = jnp.dot(half, flat.astype(BF16), preferred_element_type=F32)
-    same = (lax.broadcasted_iota(jnp.int32, full.shape, 0) & (ROWS - 1)) == (
-        lax.broadcasted_iota(jnp.int32, full.shape, 1) & (ROWS - 1))
-    mix_ref[...] = jnp.where(same, full, 0.0).astype(BF16)
+    start = 0
+    for ref in (seen_ref, last_ref):
+        height, width = ref.shape
+        flat = lax.broadcasted_iota(jnp.int32, (ins, width), 0) == (
+            (lax.broadcasted_iota(jnp.int32, (ins, width), 1) + start) >> 4)
+        full = jnp.dot(half, flat.astype(BF16), preferred_element_type=F32)
+        same = (lax.broadcasted_iota(jnp.int32, ref.shape, 0) & (ROWS - 1)) == (
+            lax.broadcasted_iota(jnp.int32, ref.shape, 1) & (ROWS - 1))
+        ref[...] = jnp.where(same, full, 0.0).astype(BF16)
+        start += width
     bonds = jnp.concatenate([coupling_ref[n] for n in range(slots)], axis=1)
 
     def spread(tall_ref, wide_ref):
@@ -99,33 +105,38 @@
     wide = [np.kron(np.eye(slots, dtype=np.float32), pick.T) for pick in picks]
     return call(
         functools.partial(tables_kernel, moms),
-        [((rel.shape[0] * ROWS, rel.shape[1] * ROWS), BF16), ((orbs * orbs, slots * orbs * orbs), BF16)],
+        [((rel.shape[0] * ROWS, n * e_dev * ROWS), BF16) for n in (sum(len(p) for _, p in x) for x in (SEEN, LAST))]
+        + [((orbs * orbs, slots * orbs * orbs), BF16)],
         pos, offsets, phonon, coupling, *map(jnp.asarray, (rel, mom, *picks, *wide)),
     )
 
 
-def cut_kernel(groups, pos_ref, green_ref, near_ref, own_ref, give_ref, far_ref, home_ref):
+def cut_kernel(groups, pos_ref, near_ref, green_ref, own_ref, give_ref, far_ref, home_ref):
     e_dev, pairs, _ = green_ref.shape
     rows = e_dev * pairs
+    z, way = pos_ref[0], pos_ref[1]
+    first = (2 * z + ((1 - way) >> 1)) * LANES
+    steps = (near_ref[...] - first - lax.broadcasted_iota(jnp.int32, near_ref.shape, 1)).astype(F32)
+    steps = jnp.concatenate([steps, jnp.zeros((ROWS - steps.shape[0], LANES), F32)], axis=0).astype(BF16)
 
     def put(ref, at, distance):
-        group = (pos_ref[0] + distance) & (groups - 1)
+        group = (z + distance) & (groups - 1)
         for chunk in range(2):
             start = pl.multiple_of((chunk * groups + group) * LANES, LANES)
             ref[at, chunk * rows : (chunk + 1) * rows, :] = green_ref[:, :, pl.ds(start, LANES)].reshape(rows, LANES)
-        ref[at, 2 * rows :, :] = near_ref[...]
+        ref[at, 2 * rows :, :] = steps
 
     for i, j in enumerate(NEAR):
-        put(own_ref, i, pos_ref[1] * j)
-        put(give_ref, i, -pos_ref[1] * j)
+        put(own_ref, i, way * j)
+        put(give_ref, i, -way * j)
     put(far_ref, 0, 4)
     put(home_ref, 0, 0)
 
 
-def cut(pos, green, near, groups):
-    height = 2 * green.shape[0] * green.shape[1] + near.shape[0]
+def cut(pos, near, green, groups):
+    height = 2 * green.shape[0] * green.shape[1] + ROWS
     outs = [((n, height, LANES), BF16) for n in (len(NEAR), len(NEAR), 1, 1)]
-    return call(functools.partial(cut_kernel, groups), outs, pos, green, near)
+    return call(functools.partial(cut_kernel, groups), outs, pos, near, green)
 
 
 def merge_kernel(chips, own_ref, got_ref, *refs):
@@ -160,13 +171,13 @@
     return call(stack_kernel, outs, *blocks)
 
 
-def mix_kernel(e_dev, chunk, mix_ref, *refs):
-    fields, kept_ref, other_ref = refs[:6], refs[6], refs[7]
+def mix_kernel(e_dev, chunk, fields, mix_ref, *refs):
+    refs, sums, (kept_ref, other_ref) = refs[:fields], refs[fields:-2], refs[-2:]
     places, height, width = kept_ref.shape
     pairs = height // e_dev
     for g in range(pairs // ROWS):
         tiles = []
-        for ref in fields:
+        for ref in refs:
             for i in range(ref.shape[0]):
                 for e in range(e_dev):
                     tiles.append(ref[i, pl.ds(chunk * height + e * pairs + g * ROWS, ROWS), :])
@@ -174,13 +185,15 @@
         mixed = mixed.reshape(e_dev, 2, places, ROWS, width)
         for e in range(e_dev):
             rows = pl.ds(e * pairs + g * ROWS, ROWS)
-            kept_ref[:, rows, :] = mixed[e, 0]
-            other_ref[:, rows, :] = mixed[e, 1].astype(BF16)
-
-
-def mix(matrix, fields, chunk, e_dev, after=()):
+            for i, out in enumerate((kept_ref, other_ref)):
+                total = mixed[e, i] + sums[i][:, rows, :] if sums else mixed[e, i]
+                out[:, rows, :] = total.astype(out.dtype)
+
+
+def mix(matrix, fields, chunk, e_dev, sums=(), after=()):
     shape = (len(PLACES), fields[0].shape[1] // 2, LANES)
-    return call(functools.partial(mix_kernel, e_dev, chunk), [(shape, F32), (shape, BF16)], matrix, *fields, after=after)
+    outs = [(shape, F32), (shape, BF16 if sums else F32)]
+    return call(functools.partial(mix_kernel, e_dev, chunk, len(fields)), outs, matrix, *fields, *sums, after=after)
 
 
 def add_kernel(kept_ref, got_ref, far, three, two, one, home):
@@ -332,26 +345,21 @@
     green = green_blocks[:, 0]
     e_dev, pairs, atoms = green.shape
     rows = e_dev * pairs
-    slots = neighbours.shape[1]
     core = lax.axis_index("core")
     pos = jnp.stack([lax.axis_index("z"), 1 - 2 * core])
     forward = [(i, i + 1) for i in range(tiles - 1)]
     backward = [(i + 1, i) for i in range(tiles - 1)]
-    atom = lax.axis_index(KMOM) * LANES + jnp.arange(LANES, dtype=jnp.int32)
-    steps = (neighbours - atom[:, None]).T.astype(BF16)
-    steps = jnp.concatenate([steps, jnp.zeros((ROWS - slots, LANES), BF16)], axis=0)
-
-    own, give, far, home = cut(pos, green, steps, groups)
+    own, give, far, home = cut(pos, neighbours.T, green, groups)
     far, three, two, one, home = exchange(far, *merge(own, swap(give), (3, 2, 1)), home)
     parts = [stack(one, two, home), stack(three, far)]
     fields, near = zip(*parts)
     low = [lax.ppermute(x, "energy", forward) for x in fields]
     high = [lax.ppermute(x, "energy", backward) for x in fields]
-    fields = (*low, *fields, *high)
-    matrix, pair_maps = tables(pos, phonon, offsets, coupling, e_dev)
+    seen, last, pair_maps = tables(pos, phonon, offsets, coupling, e_dev)
+    sums = [mix(seen, (low[0], fields[0], high[0], fields[1]), chunk, e_dev) for chunk in range(2)]
     backs = []
     for chunk in range(2):
-        kept, other = mix(matrix, fields, chunk, e_dev)
+        kept, other = mix(last, (low[1], high[1]), chunk, e_dev, sums[chunk], after=sums[1][:1])
         backs.append(exchange(*add(kept, swap(other))))
     blocks = [*backs[0], swap(pick(backs[0], *near))]
     done, nears, tail = first_sum(pos, pair_maps, near, blocks, groups, green.shape)

time: 106 us -> 104 us (0.981); the launches traced: 105 us -> 102 us
  waiting for transfers between devices: 40.6 us -> 32.5 us
  starting transfers between devices: 46.7 us -> 50.8 us
    ppermute x12, starting transfers between devices: 28.1 us -> 35 us  [round_ring(): return lax.ppermute(x, KMOM, pairs)]
    ppermute x12, waiting for transfers between devices: 30.1 us -> 24.7 us  [round_ring(): return lax.ppermute(x, KMOM, pairs)]
    ppermute x2, waiting for transfers between devices: 4.98 us -> 1.56 us  [body(): low = [lax.ppermute(x, 'energy', forward) for x in fields]]
    ppermute x5, starting transfers between devices: 8.09 us -> 5.26 us  [swap(): return lax.ppermute(x, 'core', [(0, 1), (1, 0)])]
    pallas_call x13 -> x15, Pallas kernels: 15.6 us -> 16.5 us  [call(): pl.pallas_call(run, out_shape=[jax.ShapeDtypeStruct(shape, dtype) for sha...]
  transfers between devices with their start and end apart: 21 -> 21, of which waited for: 10 -> 9; matrix products, arithmetic and copies ran while one was open for 0% -> 0% of each run, Pallas kernels for 8% -> 10%
where the time goes in v4:
time: 104 us; the launch traced here: 102 us
  starting transfers between devices  50.8 us (49%)
  waiting for transfers between devices  32.5 us (31%)
  Pallas kernels  16.5 us (16%)
  local copies, waits for them, and re-layouts  2.03 us (2%)
    ppermute x12, starting transfers between devices, round_ring(): return lax.ppermute(x, KMOM, pairs)  35 us
    ppermute x12, waiting for transfers between devices, round_ring(): return lax.ppermute(x, KMOM, pairs)  24.7 us
    pallas_call x15, Pallas kernels, call(): pl.pallas_call(run, out_shape=[jax.ShapeDtypeStruct(shape, dtype) for sha...  16.5 us
    ppermute x2, starting transfers between devices, body(): low = [lax.ppermute(x, 'energy', forward) for x in fields]  5.83 us
    ppermute x5, starting transfers between devices, swap(): return lax.ppermute(x, 'core', [(0, 1), (1, 0)])  5.26 us
    ppermute x2, starting transfers between devices, body(): high = [lax.ppermute(x, 'energy', backward) for x in fields]  4.74 us
    ppermute x2, waiting for transfers between devices, body(): high = [lax.ppermute(x, 'energy', backward) for x in fields]  4.09 us
    ppermute x5, waiting for transfers between devices, swap(): return lax.ppermute(x, 'core', [(0, 1), (1, 0)])  2.19 us
  transfers between devices with their start and end apart: 21, of which 9 were waited for; matrix products, arithmetic and copies ran while one was open for 0% of the time, Pallas kernels for 10%

profile of v4, /device:TPU:25, one launch (start us, length us, event | category | flops | bytes accessed | tf_op | source)
XLA Modules:
  0.0 102.2 jit_solution(11953741941504550835)
XLA Ops:
  0.1 1.3 %copy-done = bf16[2,1,144,2048]{3,2,1,0:T(8,128)(2,1)S(1)} copy-done((bf16[2,1,144,2048]{3,2,1,0:T(8,128)(2,1)S(1)}, bf16[2,1,144,2048]{3,2,1,0:T(8,128)(2,1)}, u32[]{:S(2)}) %copy-start) | copy-done | bytes 1179672
  2.0 0.8 shard_map.110
  3.0 0.8 collective-permute-start
  3.8 1.4 %collective-permute-done.refs_1_ = bf16[3,592,128]{2,1,0:T(8,128)(2,1)S(1)} collective-permute-done((bf16[3,592,128]{2,1,0:T(8,128)(2,1)S(1)}, bf16[3,592,128]{2,1,0:T(8,128)(2,1)S(1)}, u32[]{:S(2)}, u32[]{:S(2)}) %collective-permute-start) | collective-permute-done | bytes 454688 | tf_op jit(solution)/shard_map/ppermute | solution.py:330
  5.3 5.7 %collective-permute-start.1 = (bf16[2,592,128]{2,1,0:T(8,128)(2,1)S(1)}, bf16[2,592,128]{2,1,0:T(8,128)(2,1)S(1)}, u32[]{:S(2)}, u32[]{:S(2)}) collective-permute-start(bf16[2,592,128]{2,1,0:T(8,128)(2,1)S(1)} %get-tuple-element.43), channel_id=1, source_target_pairs={{0,2},{1,15},{2,4},{3,1},{4,6},{5,3},{6,8},{7,5},{8,10},{9,7},{10,... | collective-permute-start | bytes 909320 | tf_op jit(solution)/shard_map/ppermute | solution.py:336
  10.9 1.2 %collective-permute-start.2 = (bf16[2,592,128]{2,1,0:T(8,128)(2,1)S(1)}, bf16[2,592,128]{2,1,0:T(8,128)(2,1)S(1)}, u32[]{:S(2)}, u32[]{:S(2)}) collective-permute-start(bf16[2,592,128]{2,1,0:T(8,128)(2,1)S(1)} %get-tuple-element.44), channel_id=1, source_target_pairs={{0,4},{1,13},{2,6},{3,15},{4,8},{5,1},{6,10},{7,3},{8,12},{9,5},{1... | collective-permute-start | bytes 909320 | tf_op jit(solution)/shard_map/ppermute | solution.py:336
  12.5 5.0 %collective-permute-done.1.refs_0_ = bf16[2,592,128]{2,1,0:T(8,128)(2,1)S(1)} collective-permute-done((bf16[2,592,128]{2,1,0:T(8,128)(2,1)S(1)}, bf16[2,592,128]{2,1,0:T(8,128)(2,1)S(1)}, u32[]{:S(2)}, u32[]{:S(2)}) %collective-permute-start.1) | collective-permute-done | bytes 303136 | tf_op jit(solution)/shard_map/ppermute | solution.py:336
  17.5 5.6 %collective-permute-done.2.refs_1_ = bf16[2,592,128]{2,1,0:T(8,128)(2,1)S(1)} collective-permute-done((bf16[2,592,128]{2,1,0:T(8,128)(2,1)S(1)}, bf16[2,592,128]{2,1,0:T(8,128)(2,1)S(1)}, u32[]{:S(2)}, u32[]{:S(2)}) %collective-permute-start.2) | collective-permute-done | bytes 303136 | tf_op jit(solution)/shard_map/ppermute | solution.py:336
  23.1 2.8 %collective-permute-start.7 = (bf16[5,576,128]{2,1,0:T(8,128)(2,1)S(1)}, bf16[5,576,128]{2,1,0:T(8,128)(2,1)S(1)}, u32[]{:S(2)}, u32[]{:S(2)}) collective-permute-start(bf16[5,576,128]{2,1,0:T(8,128)(2,1)S(1)} %get-tuple-element.53.refs_2_), channel_id=1, source_target_pairs={{0,16},{16,32},{32,48},{48,64},{64,80},{80,96},{96,112},{112,128},... | collective-permute-start | bytes 2211848 | tf_op jit(solution)/shard_map/ppermute | solution.py:356
  25.9 2.5 %collective-permute-start.8 = (bf16[5,576,128]{2,1,0:T(8,128)(2,1)S(1)}, bf16[5,576,128]{2,1,0:T(8,128)(2,1)S(1)}, u32[]{:S(2)}, u32[]{:S(2)}) collective-permute-start(bf16[5,576,128]{2,1,0:T(8,128)(2,1)S(1)} %get-tuple-element.53.refs_2_), channel_id=1, source_target_pairs={{16,0},{32,16},{48,32},{64,48},{80,64},{96,80},{112,96},{128,112},... | collective-permute-start | bytes 2211848 | tf_op jit(solution)/shard_map/ppermute | solution.py:357
  28.4 3.8 %collective-permute-start.4 = (bf16[1,592,128]{2,1,0:T(8,128)(2,1)S(1)}, bf16[1,592,128]{2,1,0:T(8,128)(2,1)S(1)}, u32[]{:S(2)}, u32[]{:S(2)}) collective-permute-start(bf16[1,592,128]{2,1,0:T(8,128)(2,1)S(1)} %get-tuple-element.48), channel_id=1, source_target_pairs={{0,8},{1,9},{2,10},{3,11},{4,12},{5,13},{6,14},{7,15},{8,0},{9,1},... | collective-permute-start | bytes 454664 | tf_op jit(solution)/shard_map/ppermute | solution.py:336
  32.3 10.4 %collective-permute-done.4.refs_1_ = bf16[1,592,128]{2,1,0:T(8,128)(2,1)S(1)} collective-permute-done((bf16[1,592,128]{2,1,0:T(8,128)(2,1)S(1)}, bf16[1,592,128]{2,1,0:T(8,128)(2,1)S(1)}, u32[]{:S(2)}, u32[]{:S(2)}) %collective-permute-start.4) | collective-permute-done | bytes 151584 | tf_op jit(solution)/shard_map/ppermute | solution.py:336
  42.7 3.1 %collective-permute-start.5 = (bf16[3,576,128]{2,1,0:T(8,128)(2,1)S(1)}, bf16[3,576,128]{2,1,0:T(8,128)(2,1)S(1)}, u32[]{:S(2)}, u32[]{:S(2)}) collective-permute-start(bf16[3,576,128]{2,1,0:T(8,128)(2,1)S(1)} %get-tuple-element.51.refs_4_), channel_id=1, source_target_pairs={{0,16},{16,32},{32,48},{48,64},{64,80},{80,96},{96,112},{112,128},... | collective-permute-start | bytes 1327112 | tf_op jit(solution)/shard_map/ppermute | solution.py:356
  45.7 2.2 %collective-permute-start.6 = (bf16[3,576,128]{2,1,0:T(8,128)(2,1)S(1)}, bf16[3,576,128]{2,1,0:T(8,128)(2,1)S(1)}, u32[]{:S(2)}, u32[]{:S(2)}) collective-permute-start(bf16[3,576,128]{2,1,0:T(8,128)(2,1)S(1)} %get-tuple-element.51.refs_4_), channel_id=1, source_target_pairs={{16,0},{32,16},{48,32},{64,48},{80,64},{96,80},{112,96},{128,112},... | collective-permute-start | bytes 1327112 | tf_op jit(solution)/shard_map/ppermute | solution.py:357
  48.1 2.8 %shard_map.109 = (bf16[512,576]{1,0:T(8,128)(2,1)S(1)}, bf16[512,192]{1,0:T(8,128)(2,1)S(1)}, bf16[144,1152]{1,0:T(8,128)(2,1)S(1)}) custom-call(s32[2]{0:T(128)S(1)} %pad_add_fusion.refs_0_, s32[8]{0:T(128)S(1)} %copy-done.9, f32[2,8,16]{2,1,0:T(8,128)S(1)} %copy-done.7, f32[8,12,12]{2,1,0:T(8,128)S(1)} %copy.12.refs_3_, s32[32,48]{1,0:T(8,128)S(1)} %copy-done.5, ...), custom_call_target="tpu_custom_call" | custom-call | flops 1 | bytes 1 | tf_op jit(solution)/shard_map/pallas_call | solution.py:37
  50.9 1.7 %shard_map.115 = (f32[8,288,128]{2,1,0:T(8,128)S(1)}, f32[8,288,128]{2,1,0:T(8,128)S(1)}) custom-call(bf16[512,576]{1,0:T(8,128)(2,1)S(1)} %get-tuple-element.52.refs_0_, bf16[5,576,128]{2,1,0:T(8,128)(2,1)S(1)} %collective-permute-done.7.refs_1_, bf16[5,576,128]{2,1,0:T(8,128)(2,1)S(1)} %get-tuple-element.53.refs_2_, ...), custom_call_target="tpu_custom_call" | custom-call | flops 1 | bytes 1 | tf_op jit(solution)/shard_map/pallas_call | solution.py:37
  52.6 1.7 %shard_map.114 = (f32[8,288,128]{2,1,0:T(8,128)S(1)}, f32[8,288,128]{2,1,0:T(8,128)S(1)}) custom-call(bf16[512,576]{1,0:T(8,128)(2,1)S(1)} %get-tuple-element.52.refs_0_, bf16[5,576,128]{2,1,0:T(8,128)(2,1)S(1)} %collective-permute-done.7.refs_1_, bf16[5,576,128]{2,1,0:T(8,128)(2,1)S(1)} %get-tuple-element.53.refs_2_, ...), custom_call_target="tpu_custom_call" | custom-call | flops 1 | bytes 1 | tf_op jit(solution)/shard_map/pallas_call | solution.py:37
  54.3 1.6 %collective-permute-done.5.refs_1_ = bf16[3,576,128]{2,1,0:T(8,128)(2,1)S(1)} collective-permute-done((bf16[3,576,128]{2,1,0:T(8,128)(2,1)S(1)}, bf16[3,576,128]{2,1,0:T(8,128)(2,1)S(1)}, u32[]{:S(2)}, u32[]{:S(2)}) %collective-permute-start.5) | collective-permute-done | bytes 442400 | tf_op jit(solution)/shard_map/ppermute | solution.py:356
  55.8 4.1 %collective-permute-done.6.refs_2_ = bf16[3,576,128]{2,1,0:T(8,128)(2,1)S(1)} collective-permute-done((bf16[3,576,128]{2,1,0:T(8,128)(2,1)S(1)}, bf16[3,576,128]{2,1,0:T(8,128)(2,1)S(1)}, u32[]{:S(2)}, u32[]{:S(2)}) %collective-permute-start.6) | collective-permute-done | bytes 442400 | tf_op jit(solution)/shard_map/ppermute | solution.py:357
  59.9 0.8 shard_map.116
  60.7 2.5 %collective-permute-start.9 = (bf16[8,288,128]{2,1,0:T(8,128)(2,1)S(1)}, bf16[8,288,128]{2,1,0:T(8,128)(2,1)S(1)}, u32[]{:S(2)}, u32[]{:S(2)}) collective-permute-start(bf16[8,288,128]{2,1,0:T(8,128)(2,1)S(1)} %get-tuple-element.58), channel_id=1, source_target_pairs={{0,1},{1,0},{2,3},{3,2},{4,5},{5,4},{6,7},{7,6},{8,9},{9,8},{10,11... | collective-permute-start | bytes 1769480 | tf_op jit(solution)/shard_map/ppermute | solution.py:330
  63.2 0.8 shard_map.120
  65.7 3.3 %collective-permute-start.10 = (bf16[1,288,128]{2,1,0:T(8,128)(2,1)S(1)}, bf16[1,288,128]{2,1,0:T(8,128)(2,1)S(1)}, u32[]{:S(2)}, u32[]{:S(2)}) collective-permute-start(bf16[1,288,128]{2,1,0:T(8,128)(2,1)S(1)} %get-tuple-element.59), channel_id=1, source_target_pairs={{0,8},{1,9},{2,10},{3,11},{4,12},{5,13},{6,14},{7,15},{8,0},{9,1},... | collective-permute-start | bytes 221192 | tf_op jit(solution)/shard_map/ppermute | solution.py:336
  68.9 1.9 %collective-permute-start.13 = (bf16[2,288,128]{2,1,0:T(8,128)(2,1)S(1)}, bf16[2,288,128]{2,1,0:T(8,128)(2,1)S(1)}, u32[]{:S(2)}, u32[]{:S(2)}) collective-permute-start(bf16[2,288,128]{2,1,0:T(8,128)(2,1)S(1)} %get-tuple-element.62), channel_id=1, source_target_pairs={{0,2},{1,15},{2,4},{3,1},{4,6},{5,3},{6,8},{7,5},{8,10},{9,7},{10,... | collective-permute-start | bytes 442376 | tf_op jit(solution)/shard_map/ppermute | solution.py:336
  71.0 3.6 %collective-permute-start.17 = (bf16[2,288,128]{2,1,0:T(8,128)(2,1)S(1)}, bf16[2,288,128]{2,1,0:T(8,128)(2,1)S(1)}, u32[]{:S(2)}, u32[]{:S(2)}) collective-permute-start(bf16[2,288,128]{2,1,0:T(8,128)(2,1)S(1)} %get-tuple-element.71), channel_id=1, source_target_pairs={{0,6},{1,11},{2,8},{3,13},{4,10},{5,15},{6,12},{7,1},{8,14},{9,3},... | collective-permute-start | bytes 442376 | tf_op jit(solution)/shard_map/ppermute | solution.py:336
  74.6 5.9 %collective-permute-start.18 = (bf16[2,288,128]{2,1,0:T(8,128)(2,1)S(1)}, bf16[2,288,128]{2,1,0:T(8,128)(2,1)S(1)}, u32[]{:S(2)}, u32[]{:S(2)}) collective-permute-start(bf16[2,288,128]{2,1,0:T(8,128)(2,1)S(1)} %get-tuple-element.72), channel_id=1, source_target_pairs={{0,4},{1,13},{2,6},{3,15},{4,8},{5,1},{6,10},{7,3},{8,12},{9,5},{1... | collective-permute-start | bytes 442376 | tf_op jit(solution)/shard_map/ppermute | solution.py:336
  80.5 3.0 %collective-permute-start.19 = (bf16[2,288,128]{2,1,0:T(8,128)(2,1)S(1)}, bf16[2,288,128]{2,1,0:T(8,128)(2,1)S(1)}, u32[]{:S(2)}, u32[]{:S(2)}) collective-permute-start(bf16[2,288,128]{2,1,0:T(8,128)(2,1)S(1)} %get-tuple-element.73), channel_id=1, source_target_pairs={{0,2},{1,15},{2,4},{3,1},{4,6},{5,3},{6,8},{7,5},{8,10},{9,7},{10,... | collective-permute-start | bytes 442376 | tf_op jit(solution)/shard_map/ppermute | solution.py:336
  83.5 5.5 %collective-permute-start.16 = (bf16[1,288,128]{2,1,0:T(8,128)(2,1)S(1)}, bf16[1,288,128]{2,1,0:T(8,128)(2,1)S(1)}, u32[]{:S(2)}, u32[]{:S(2)}) collective-permute-start(bf16[1,288,128]{2,1,0:T(8,128)(2,1)S(1)} %get-tuple-element.70), channel_id=1, source_target_pairs={{0,8},{1,9},{2,10},{3,11},{4,12},{5,13},{6,14},{7,15},{8,0},{9,1},... | collective-permute-start | bytes 221192 | tf_op jit(solution)/shard_map/ppermute | solution.py:336
  89.1 3.2 %collective-permute-done.16.refs_3_.refs_5_ = bf16[1,288,128]{2,1,0:T(8,128)(2,1)S(1)} collective-permute-done((bf16[1,288,128]{2,1,0:T(8,128)(2,1)S(1)}, bf16[1,288,128]{2,1,0:T(8,128)(2,1)S(1)}, u32[]{:S(2)}, u32[]{:S(2)}) %collective-permute-start.16) | collective-permute-done | bytes 73760 | tf_op jit(solution)/shard_map/ppermute | solution.py:336
  92.8 1.8 %collective-permute-start.20 = (bf16[864,128]{1,0:T(8,128)(2,1)S(1)}, bf16[864,128]{1,0:T(8,128)(2,1)S(1)}, u32[]{:S(2)}, u32[]{:S(2)}) collective-permute-start(bf16[864,128]{1,0:T(8,128)(2,1)S(1)} %shard_map.122), channel_id=1, source_target_pairs={{0,1},{1,0},{2,3},{3,2},{4,5},{5,4},{6,7},{7,6},{8,9},{9,8},{10,11... | collective-permute-start | bytes 663560 | tf_op jit(solution)/shard_map/ppermute | solution.py:330
  94.6 3.0 %shard_map.119 = (bf16[2,144,896]{2,1,0:T(8,128)(2,1)S(1)}, bf16[16,16,128]{2,1,0:T(8,128)(2,1)S(1)}, bf16[288,192]{1,0:T(8,128)(2,1)S(1)}) custom-call(s32[2]{0:T(128)S(1)} %pad_add_fusion.refs_0_, bf16[144,1152]{1,0:T(8,128)(2,1)S(1)} %get-tuple-element.40.refs_1_, bf16[5,16,128]{2,1,0:T(8,128)(2,1)S(1)} %get-tuple-element.46.refs_3_.refs_2_, ...), custom_call_target="tpu_custom_call" | custom-call | flops 1 | bytes 1 | tf_op jit(solution)/shard_map/pallas_call | solution.py:37
  97.7 4.6 %shard_map.123 = bf16[2,144,2048]{2,1,0:T(8,128)(2,1)} custom-call(s32[2]{0:T(128)S(1)} %pad_add_fusion.refs_0_, bf16[144,1152]{1,0:T(8,128)(2,1)S(1)} %get-tuple-element.40.refs_1_, bf16[16,16,128]{2,1,0:T(8,128)(2,1)S(1)} %get-tuple-element.64.refs_2_, bf16[2,144,896]{2,1,0:T(8,128)(2,1)S(1)} %get-tuple-element.65.refs_3_, ...), custom_call_target="tpu_custom_call" | custom-call | flops 1 | bytes 1 | tf_op jit(solution)/shard_map/pallas_call | solution.py:37
  (49 shorter events, 3.9 us)
Async XLA Ops:
  0.1 1.3 %copy-start = (bf16[2,1,144,2048]{3,2,1,0:T(8,128)(2,1)S(1)}, bf16[2,1,144,2048]{3,2,1,0:T(8,128)(2,1)}, u32[]{:S(2)}) copy-start(bf16[2,1,144,2048]{3,2,1,0:T(8,128)(2,1)} %param.11) | copy-start | bytes 3538948
  1.3 0.7 copy-start.8
  2.9 45.1 %copy-start.10 = (f32[8,12,12]{2,0,1:T(8,128)S(1)}, f32[8,12,12]{2,0,1:T(8,128)}, u32[]{:S(2)}) copy-start(f32[8,12,12]{2,0,1:T(8,128)} %param.15) | copy-start | bytes 13828
  2.9 45.1 %copy-start.1 = (f32[96,1152]{1,0:T(8,128)S(1)}, f32[96,1152]{1,0:T(8,128)}, u32[]{:S(2)}) copy-start(f32[96,1152]{1,0:T(8,128)} %constant.28.clone.refs_8_) | copy-start | bytes 1327108
  2.9 45.1 %copy-start.2 = (f32[96,1152]{1,0:T(8,128)S(1)}, f32[96,1152]{1,0:T(8,128)}, u32[]{:S(2)}) copy-start(f32[96,1152]{1,0:T(8,128)} %constant.29.clone.refs_9_) | copy-start | bytes 1327108
  2.9 45.1 %copy-start.3 = (f32[144,12]{1,0:T(8,128)S(1)}, f32[144,12]{1,0:T(8,128)}, u32[]{:S(2)}) copy-start(f32[144,12]{1,0:T(8,128)} %constant.26.clone.refs_6_) | copy-start | bytes 20740
  2.9 45.1 %copy-start.4 = (f32[144,12]{1,0:T(8,128)S(1)}, f32[144,12]{1,0:T(8,128)}, u32[]{:S(2)}) copy-start(f32[144,12]{1,0:T(8,128)} %constant.27.clone.refs_7_) | copy-start | bytes 20740
  3.0 45.1 %copy-start.5 = (s32[32,48]{1,0:T(8,128)S(1)}, s32[32,48]{1,0:T(8,128)}, u32[]{:S(2)}) copy-start(s32[32,48]{1,0:T(8,128)} %constant.24.clone.refs_4_) | copy-start | bytes 18436
  3.0 45.1 %copy-start.6 = (s32[32,48]{1,0:T(8,128)S(1)}, s32[32,48]{1,0:T(8,128)}, u32[]{:S(2)}) copy-start(s32[32,48]{1,0:T(8,128)} %constant.25.clone.refs_5_) | copy-start | bytes 18436
  3.0 45.1 %copy-start.7 = (f32[2,8,16]{2,1,0:T(8,128)S(1)}, f32[2,8,16]{2,1,0:T(8,128)}, u32[]{:S(2)}) copy-start(f32[2,8,16]{2,1,0:T(8,128)} %refs_2_.1) | copy-start | bytes 3076
  3.0 45.1 %copy-start.9 = (s32[8]{0:T(128)S(1)}, s32[8]{0:T(128)}, u32[]{:S(2)}) copy-start(s32[8]{0:T(128)} %refs_1_.1) | copy-start | bytes 100
  3.0 2.2 %collective-permute-start = (bf16[3,592,128]{2,1,0:T(8,128)(2,1)S(1)}, bf16[3,592,128]{2,1,0:T(8,128)(2,1)S(1)}, u32[]{:S(2)}, u32[]{:S(2)}) collective-permute-start(bf16[3,592,128]{2,1,0:T(8,128)(2,1)S(1)} %get-tuple-element.42), channel_id=1, source_target_pairs={{0,1},{1,0},{2,3},{3,2},{4,5},{5,4},{6,7},{7,6},{8,9},{9,8},{10,11... | collective-permute-start | bytes 1363976 | tf_op jit(solution)/shard_map/ppermute | solution.py:330
  5.3 12.3 %collective-permute-start.1 = (bf16[2,592,128]{2,1,0:T(8,128)(2,1)S(1)}, bf16[2,592,128]{2,1,0:T(8,128)(2,1)S(1)}, u32[]{:S(2)}, u32[]{:S(2)}) collective-permute-start(bf16[2,592,128]{2,1,0:T(8,128)(2,1)S(1)} %get-tuple-element.43), channel_id=1, source_target_pairs={{0,2},{1,15},{2,4},{3,1},{4,6},{5,3},{6,8},{7,5},{8,10},{9,7},{10,... | collective-permute-start | bytes 909320 | tf_op jit(solution)/shard_map/ppermute | solution.py:336
  10.9 12.2 %collective-permute-start.2 = (bf16[2,592,128]{2,1,0:T(8,128)(2,1)S(1)}, bf16[2,592,128]{2,1,0:T(8,128)(2,1)S(1)}, u32[]{:S(2)}, u32[]{:S(2)}) collective-permute-start(bf16[2,592,128]{2,1,0:T(8,128)(2,1)S(1)} %get-tuple-element.44), channel_id=1, source_target_pairs={{0,4},{1,13},{2,6},{3,15},{4,8},{5,1},{6,10},{7,3},{8,12},{9,5},{1... | collective-permute-start | bytes 909320 | tf_op jit(solution)/shard_map/ppermute | solution.py:336
  12.1 30.6 %collective-permute-start.3 = (bf16[2,592,128]{2,1,0:T(8,128)(2,1)S(1)}, bf16[2,592,128]{2,1,0:T(8,128)(2,1)S(1)}, u32[]{:S(2)}, u32[]{:S(2)}) collective-permute-start(bf16[2,592,128]{2,1,0:T(8,128)(2,1)S(1)} %get-tuple-element.47), channel_id=1, source_target_pairs={{0,6},{1,11},{2,8},{3,13},{4,10},{5,15},{6,12},{7,1},{8,14},{9,3},... | collective-permute-start | bytes 909320 | tf_op jit(solution)/shard_map/ppermute | solution.py:336
  23.1 27.7 %collective-permute-start.7 = (bf16[5,576,128]{2,1,0:T(8,128)(2,1)S(1)}, bf16[5,576,128]{2,1,0:T(8,128)(2,1)S(1)}, u32[]{:S(2)}, u32[]{:S(2)}) collective-permute-start(bf16[5,576,128]{2,1,0:T(8,128)(2,1)S(1)} %get-tuple-element.53.refs_2_), channel_id=1, source_target_pairs={{0,16},{16,32},{32,48},{48,64},{64,80},{80,96},{96,112},{112,128},... | collective-permute-start | bytes 2211848 | tf_op jit(solution)/shard_map/ppermute | solution.py:356
  25.9 24.9 %collective-permute-start.8 = (bf16[5,576,128]{2,1,0:T(8,128)(2,1)S(1)}, bf16[5,576,128]{2,1,0:T(8,128)(2,1)S(1)}, u32[]{:S(2)}, u32[]{:S(2)}) collective-permute-start(bf16[5,576,128]{2,1,0:T(8,128)(2,1)S(1)} %get-tuple-element.53.refs_2_), channel_id=1, source_target_pairs={{16,0},{32,16},{48,32},{64,48},{80,64},{96,80},{112,96},{128,112},... | collective-permute-start | bytes 2211848 | tf_op jit(solution)/shard_map/ppermute | solution.py:357
  28.4 14.2 %collective-permute-start.4 = (bf16[1,592,128]{2,1,0:T(8,128)(2,1)S(1)}, bf16[1,592,128]{2,1,0:T(8,128)(2,1)S(1)}, u32[]{:S(2)}, u32[]{:S(2)}) collective-permute-start(bf16[1,592,128]{2,1,0:T(8,128)(2,1)S(1)} %get-tuple-element.48), channel_id=1, source_target_pairs={{0,8},{1,9},{2,10},{3,11},{4,12},{5,13},{6,14},{7,15},{8,0},{9,1},... | collective-permute-start | bytes 454664 | tf_op jit(solution)/shard_map/ppermute | solution.py:336
  42.7 13.1 %collective-permute-start.5 = (bf16[3,576,128]{2,1,0:T(8,128)(2,1)S(1)}, bf16[3,576,128]{2,1,0:T(8,128)(2,1)S(1)}, u32[]{:S(2)}, u32[]{:S(2)}) collective-permute-start(bf16[3,576,128]{2,1,0:T(8,128)(2,1)S(1)} %get-tuple-element.51.refs_4_), channel_id=1, source_target_pairs={{0,16},{16,32},{32,48},{48,64},{64,80},{80,96},{96,112},{112,128},... | collective-permute-start | bytes 1327112 | tf_op jit(solution)/shard_map/ppermute | solution.py:356
  45.7 14.2 %collective-permute-start.6 = (bf16[3,576,128]{2,1,0:T(8,128)(2,1)S(1)}, bf16[3,576,128]{2,1,0:T(8,128)(2,1)S(1)}, u32[]{:S(2)}, u32[]{:S(2)}) collective-permute-start(bf16[3,576,128]{2,1,0:T(8,128)(2,1)S(1)} %get-tuple-element.51.refs_4_), channel_id=1, source_target_pairs={{16,0},{32,16},{48,32},{64,48},{80,64},{96,80},{112,96},{128,112},... | collective-permute-start | bytes 1327112 | tf_op jit(solution)/shard_map/ppermute | solution.py:357
  60.7 4.1 %collective-permute-start.9 = (bf16[8,288,128]{2,1,0:T(8,128)(2,1)S(1)}, bf16[8,288,128]{2,1,0:T(8,128)(2,1)S(1)}, u32[]{:S(2)}, u32[]{:S(2)}) collective-permute-start(bf16[8,288,128]{2,1,0:T(8,128)(2,1)S(1)} %get-tuple-element.58), channel_id=1, source_target_pairs={{0,1},{1,0},{2,3},{3,2},{4,5},{5,4},{6,7},{7,6},{8,9},{9,8},{10,11... | collective-permute-start | bytes 1769480 | tf_op jit(solution)/shard_map/ppermute | solution.py:330
  64.0 6.9 %collective-permute-start.15 = (bf16[8,288,128]{2,1,0:T(8,128)(2,1)S(1)}, bf16[8,288,128]{2,1,0:T(8,128)(2,1)S(1)}, u32[]{:S(2)}, u32[]{:S(2)}) collective-permute-start(bf16[8,288,128]{2,1,0:T(8,128)(2,1)S(1)} %get-tuple-element.69), channel_id=1, source_target_pairs={{0,1},{1,0},{2,3},{3,2},{4,5},{5,4},{6,7},{7,6},{8,9},{9,8},{10,11... | collective-permute-start | bytes 1769480 | tf_op jit(solution)/shard_map/ppermute | solution.py:330
  64.9 15.6 %collective-permute-start.11 = (bf16[2,288,128]{2,1,0:T(8,128)(2,1)S(1)}, bf16[2,288,128]{2,1,0:T(8,128)(2,1)S(1)}, u32[]{:S(2)}, u32[]{:S(2)}) collective-permute-start(bf16[2,288,128]{2,1,0:T(8,128)(2,1)S(1)} %get-tuple-element.60), channel_id=1, source_target_pairs={{0,6},{1,11},{2,8},{3,13},{4,10},{5,15},{6,12},{7,1},{8,14},{9,3},... | collective-permute-start | bytes 442376 | tf_op jit(solution)/shard_map/ppermute | solution.py:336
  65.2 18.3 %collective-permute-start.12 = (bf16[2,288,128]{2,1,0:T(8,128)(2,1)S(1)}, bf16[2,288,128]{2,1,0:T(8,128)(2,1)S(1)}, u32[]{:S(2)}, u32[]{:S(2)}) collective-permute-start(bf16[2,288,128]{2,1,0:T(8,128)(2,1)S(1)} %get-tuple-element.61), channel_id=1, source_target_pairs={{0,4},{1,13},{2,6},{3,15},{4,8},{5,1},{6,10},{7,3},{8,12},{9,5},{1... | collective-permute-start | bytes 442376 | tf_op jit(solution)/shard_map/ppermute | solution.py:336
  65.7 8.9 %collective-permute-start.10 = (bf16[1,288,128]{2,1,0:T(8,128)(2,1)S(1)}, bf16[1,288,128]{2,1,0:T(8,128)(2,1)S(1)}, u32[]{:S(2)}, u32[]{:S(2)}) collective-permute-start(bf16[1,288,128]{2,1,0:T(8,128)(2,1)S(1)} %get-tuple-element.59), channel_id=1, source_target_pairs={{0,8},{1,9},{2,10},{3,11},{4,12},{5,13},{6,14},{7,15},{8,0},{9,1},... | collective-permute-start | bytes 221192 | tf_op jit(solution)/shard_map/ppermute | solution.py:336
  68.9 20.0 %collective-permute-start.13 = (bf16[2,288,128]{2,1,0:T(8,128)(2,1)S(1)}, bf16[2,288,128]{2,1,0:T(8,128)(2,1)S(1)}, u32[]{:S(2)}, u32[]{:S(2)}) collective-permute-start(bf16[2,288,128]{2,1,0:T(8,128)(2,1)S(1)} %get-tuple-element.62), channel_id=1, source_target_pairs={{0,2},{1,15},{2,4},{3,1},{4,6},{5,3},{6,8},{7,5},{8,10},{9,7},{10,... | collective-permute-start | bytes 442376 | tf_op jit(solution)/shard_map/ppermute | solution.py:336
  71.0 21.3 %collective-permute-start.17 = (bf16[2,288,128]{2,1,0:T(8,128)(2,1)S(1)}, bf16[2,288,128]{2,1,0:T(8,128)(2,1)S(1)}, u32[]{:S(2)}, u32[]{:S(2)}) collective-permute-start(bf16[2,288,128]{2,1,0:T(8,128)(2,1)S(1)} %get-tuple-element.71), channel_id=1, source_target_pairs={{0,6},{1,11},{2,8},{3,13},{4,10},{5,15},{6,12},{7,1},{8,14},{9,3},... | collective-permute-start | bytes 442376 | tf_op jit(solution)/shard_map/ppermute | solution.py:336
  74.6 17.7 %collective-permute-start.18 = (bf16[2,288,128]{2,1,0:T(8,128)(2,1)S(1)}, bf16[2,288,128]{2,1,0:T(8,128)(2,1)S(1)}, u32[]{:S(2)}, u32[]{:S(2)}) collective-permute-start(bf16[2,288,128]{2,1,0:T(8,128)(2,1)S(1)} %get-tuple-element.72), channel_id=1, source_target_pairs={{0,4},{1,13},{2,6},{3,15},{4,8},{5,1},{6,10},{7,3},{8,12},{9,5},{1... | collective-permute-start | bytes 442376 | tf_op jit(solution)/shard_map/ppermute | solution.py:336
  80.5 12.3 %collective-permute-start.19 = (bf16[2,288,128]{2,1,0:T(8,128)(2,1)S(1)}, bf16[2,288,128]{2,1,0:T(8,128)(2,1)S(1)}, u32[]{:S(2)}, u32[]{:S(2)}) collective-permute-start(bf16[2,288,128]{2,1,0:T(8,128)(2,1)S(1)} %get-tuple-element.73), channel_id=1, source_target_pairs={{0,2},{1,15},{2,4},{3,1},{4,6},{5,3},{6,8},{7,5},{8,10},{9,7},{10,... | collective-permute-start | bytes 442376 | tf_op jit(solution)/shard_map/ppermute | solution.py:336
  83.5 8.8 %collective-permute-start.16 = (bf16[1,288,128]{2,1,0:T(8,128)(2,1)S(1)}, bf16[1,288,128]{2,1,0:T(8,128)(2,1)S(1)}, u32[]{:S(2)}, u32[]{:S(2)}) collective-permute-start(bf16[1,288,128]{2,1,0:T(8,128)(2,1)S(1)} %get-tuple-element.70), channel_id=1, source_target_pairs={{0,8},{1,9},{2,10},{3,11},{4,12},{5,13},{6,14},{7,15},{8,0},{9,1},... | collective-permute-start | bytes 221192 | tf_op jit(solution)/shard_map/ppermute | solution.py:336
  89.0 5.7 %collective-permute-start.14 = (bf16[992,128]{1,0:T(8,128)(2,1)S(1)}, bf16[992,128]{1,0:T(8,128)(2,1)S(1)}, u32[]{:S(2)}, u32[]{:S(2)}) collective-permute-start(bf16[992,128]{1,0:T(8,128)(2,1)S(1)} %shard_map.118), channel_id=1, source_target_pairs={{0,1},{1,0},{2,3},{3,2},{4,5},{5,4},{6,7},{7,6},{8,9},{9,8},{10,11... | collective-permute-start | bytes 761864 | tf_op jit(solution)/shard_map/ppermute | solution.py:330
  92.8 4.8 %collective-permute-start.20 = (bf16[864,128]{1,0:T(8,128)(2,1)S(1)}, bf16[864,128]{1,0:T(8,128)(2,1)S(1)}, u32[]{:S(2)}, u32[]{:S(2)}) collective-permute-start(bf16[864,128]{1,0:T(8,128)(2,1)S(1)} %shard_map.122), channel_id=1, source_target_pairs={{0,1},{1,0},{2,3},{3,2},{4,5},{5,4},{6,7},{7,6},{8,9},{9,8},{10,11... | collective-permute-start | bytes 663560 | tf_op jit(solution)/shard_map/ppermute | solution.py:330

commit v5 on v4

--- a/solution.py
+++ b/solution.py
@@ -13,6 +13,7 @@
 TAPS = 2 * OFFSET + 1
 ROWS = 16
 COST = 1
+TABLES = 20000000000
 PARTS = 1
 LANES = 128
 SPAN = 2 * LANES
@@ -30,7 +31,7 @@
 LAST = ((-1, LATE), (1, LATE))
 
 
-def call(kernel, outs, *args, scratch=(), after=()):
+def call(kernel, outs, *args, scratch=(), after=(), cost=COST):
     def run(*refs):
         kernel(*refs[: len(args)], *refs[len(args) + len(after) :])
 
@@ -40,7 +41,7 @@
         in_specs=[SMEM if a.ndim == 1 else VMEM for a in args] + [pl.BlockSpec(memory_space=pl.ANY)] * len(after),
         out_specs=[VMEM] * len(outs),
         scratch_shapes=[pltpu.VMEM(shape, dtype) for shape, dtype in scratch],
-        cost_estimate=pl.CostEstimate(flops=COST, bytes_accessed=1, transcendentals=0),
+        cost_estimate=pl.CostEstimate(flops=cost, bytes_accessed=1, transcendentals=0),
         compiler_params=pltpu.CompilerParams(vmem_limit_bytes=40 * 2**20),
     )(*args, *after)
 
@@ -108,6 +109,7 @@
         [((rel.shape[0] * ROWS, n * e_dev * ROWS), BF16) for n in (sum(len(p) for _, p in x) for x in (SEEN, LAST))]
         + [((orbs * orbs, slots * orbs * orbs), BF16)],
         pos, offsets, phonon, coupling, *map(jnp.asarray, (rel, mom, *picks, *wide)),
+        cost=TABLES,
     )
 
 

time: 104 us -> 103 us (level); the launches traced: 102 us -> 102 us
    ppermute x12, starting transfers between devices: 35 us -> 30.9 us  [round_ring(): return lax.ppermute(x, KMOM, pairs)]
    ppermute x5, starting transfers between devices: 5.26 us -> 8.84 us  [swap(): return lax.ppermute(x, 'core', [(0, 1), (1, 0)])]
    ppermute x12, waiting for transfers between devices: 24.7 us -> 23.4 us  [round_ring(): return lax.ppermute(x, KMOM, pairs)]
    ppermute x2, waiting for transfers between devices: 4.09 us -> 5.16 us  [body(): high = [lax.ppermute(x, 'energy', backward) for x in fields]]
  transfers between devices with their start and end apart: 21 -> 21, of which waited for: 9 -> 10; matrix products, arithmetic and copies ran while one was open for 0% -> 0% of each run, Pallas kernels for 10% -> 10%
where the time goes in v5:
time: 103 us; the launch traced here: 102 us
  starting transfers between devices  50.3 us (49%)
  waiting for transfers between devices  33.1 us (32%)
  Pallas kernels  16.5 us (16%)
  local copies, waits for them, and re-layouts  2.02 us (2%)
    ppermute x12, starting transfers between devices, round_ring(): return lax.ppermute(x, KMOM, pairs)  30.9 us
    ppermute x12, waiting for transfers between devices, round_ring(): return lax.ppermute(x, KMOM, pairs)  23.4 us
    pallas_call x15, Pallas kernels, call(): pl.pallas_call(run, out_shape=[jax.ShapeDtypeStruct(shape, dtype) for sha...  16.5 us
    ppermute x5, starting transfers between devices, swap(): return lax.ppermute(x, 'core', [(0, 1), (1, 0)])  8.84 us
    ppermute x2, starting transfers between devices, body(): low = [lax.ppermute(x, 'energy', forward) for x in fields]  5.56 us
    ppermute x2, waiting for transfers between devices, body(): high = [lax.ppermute(x, 'energy', backward) for x in fields]  5.16 us
    ppermute x2, starting transfers between devices, body(): high = [lax.ppermute(x, 'energy', backward) for x in fields]  5.01 us
    ppermute x2, waiting for transfers between devices, body(): low = [lax.ppermute(x, 'energy', forward) for x in fields]  2.33 us
  transfers between devices with their start and end apart: 21, of which 10 were waited for; matrix products, arithmetic and copies ran while one was open for 0% of the time, Pallas kernels for 10%

profile of v5, /device:TPU:25, one launch (start us, length us, event | category | flops | bytes accessed | tf_op | source)
XLA Modules:
  0.0 102.3 jit_solution(18168982154984029655)
XLA Ops:
  0.1 1.3 %copy-done = bf16[2,1,144,2048]{3,2,1,0:T(8,128)(2,1)S(1)} copy-done((bf16[2,1,144,2048]{3,2,1,0:T(8,128)(2,1)S(1)}, bf16[2,1,144,2048]{3,2,1,0:T(8,128)(2,1)}, u32[]{:S(2)}) %copy-start) | copy-done | bytes 1179672
  2.0 0.8 shard_map.110
  3.8 1.4 %collective-permute-done.refs_1_ = bf16[3,592,128]{2,1,0:T(8,128)(2,1)S(1)} collective-permute-done((bf16[3,592,128]{2,1,0:T(8,128)(2,1)S(1)}, bf16[3,592,128]{2,1,0:T(8,128)(2,1)S(1)}, u32[]{:S(2)}, u32[]{:S(2)}) %collective-permute-start) | collective-permute-done | bytes 454688 | tf_op jit(solution)/shard_map/ppermute | solution.py:332
  5.3 5.7 %collective-permute-start.1 = (bf16[2,592,128]{2,1,0:T(8,128)(2,1)S(1)}, bf16[2,592,128]{2,1,0:T(8,128)(2,1)S(1)}, u32[]{:S(2)}, u32[]{:S(2)}) collective-permute-start(bf16[2,592,128]{2,1,0:T(8,128)(2,1)S(1)} %get-tuple-element.43), channel_id=1, source_target_pairs={{0,2},{1,15},{2,4},{3,1},{4,6},{5,3},{6,8},{7,5},{8,10},{9,7},{10,... | collective-permute-start | bytes 909320 | tf_op jit(solution)/shard_map/ppermute | solution.py:338
  10.9 1.2 %collective-permute-start.2 = (bf16[2,592,128]{2,1,0:T(8,128)(2,1)S(1)}, bf16[2,592,128]{2,1,0:T(8,128)(2,1)S(1)}, u32[]{:S(2)}, u32[]{:S(2)}) collective-permute-start(bf16[2,592,128]{2,1,0:T(8,128)(2,1)S(1)} %get-tuple-element.44), channel_id=1, source_target_pairs={{0,4},{1,13},{2,6},{3,15},{4,8},{5,1},{6,10},{7,3},{8,12},{9,5},{1... | collective-permute-start | bytes 909320 | tf_op jit(solution)/shard_map/ppermute | solution.py:338
  12.5 4.5 %collective-permute-start.4 = (bf16[1,592,128]{2,1,0:T(8,128)(2,1)S(1)}, bf16[1,592,128]{2,1,0:T(8,128)(2,1)S(1)}, u32[]{:S(2)}, u32[]{:S(2)}) collective-permute-start(bf16[1,592,128]{2,1,0:T(8,128)(2,1)S(1)} %get-tuple-element.48), channel_id=1, source_target_pairs={{0,8},{1,9},{2,10},{3,11},{4,12},{5,13},{6,14},{7,15},{8,0},{9,1},... | collective-permute-start | bytes 454664 | tf_op jit(solution)/shard_map/ppermute | solution.py:338
  17.5 6.6 %collective-permute-done.2.refs_1_ = bf16[2,592,128]{2,1,0:T(8,128)(2,1)S(1)} collective-permute-done((bf16[2,592,128]{2,1,0:T(8,128)(2,1)S(1)}, bf16[2,592,128]{2,1,0:T(8,128)(2,1)S(1)}, u32[]{:S(2)}, u32[]{:S(2)}) %collective-permute-start.2) | collective-permute-done | bytes 303136 | tf_op jit(solution)/shard_map/ppermute | solution.py:338
  24.2 2.8 %collective-permute-start.7 = (bf16[5,576,128]{2,1,0:T(8,128)(2,1)S(1)}, bf16[5,576,128]{2,1,0:T(8,128)(2,1)S(1)}, u32[]{:S(2)}, u32[]{:S(2)}) collective-permute-start(bf16[5,576,128]{2,1,0:T(8,128)(2,1)S(1)} %get-tuple-element.53.refs_2_), channel_id=1, source_target_pairs={{0,16},{16,32},{32,48},{48,64},{64,80},{80,96},{96,112},{112,128},... | collective-permute-start | bytes 2211848 | tf_op jit(solution)/shard_map/ppermute | solution.py:358
  27.0 2.5 %collective-permute-start.8 = (bf16[5,576,128]{2,1,0:T(8,128)(2,1)S(1)}, bf16[5,576,128]{2,1,0:T(8,128)(2,1)S(1)}, u32[]{:S(2)}, u32[]{:S(2)}) collective-permute-start(bf16[5,576,128]{2,1,0:T(8,128)(2,1)S(1)} %get-tuple-element.53.refs_2_), channel_id=1, source_target_pairs={{16,0},{32,16},{48,32},{64,48},{80,64},{96,80},{112,96},{128,112},... | collective-permute-start | bytes 2211848 | tf_op jit(solution)/shard_map/ppermute | solution.py:359
  29.5 7.9 %collective-permute-done.3.refs_0_ = bf16[2,592,128]{2,1,0:T(8,128)(2,1)S(1)} collective-permute-done((bf16[2,592,128]{2,1,0:T(8,128)(2,1)S(1)}, bf16[2,592,128]{2,1,0:T(8,128)(2,1)S(1)}, u32[]{:S(2)}, u32[]{:S(2)}) %collective-permute-start.3) | collective-permute-done | bytes 303136 | tf_op jit(solution)/shard_map/ppermute | solution.py:338
  37.4 2.8 %collective-permute-start.5 = (bf16[3,576,128]{2,1,0:T(8,128)(2,1)S(1)}, bf16[3,576,128]{2,1,0:T(8,128)(2,1)S(1)}, u32[]{:S(2)}, u32[]{:S(2)}) collective-permute-start(bf16[3,576,128]{2,1,0:T(8,128)(2,1)S(1)} %get-tuple-element.51.refs_4_), channel_id=1, source_target_pairs={{0,16},{16,32},{32,48},{48,64},{64,80},{80,96},{96,112},{112,128},... | collective-permute-start | bytes 1327112 | tf_op jit(solution)/shard_map/ppermute | solution.py:358
  40.2 2.5 %collective-permute-start.6 = (bf16[3,576,128]{2,1,0:T(8,128)(2,1)S(1)}, bf16[3,576,128]{2,1,0:T(8,128)(2,1)S(1)}, u32[]{:S(2)}, u32[]{:S(2)}) collective-permute-start(bf16[3,576,128]{2,1,0:T(8,128)(2,1)S(1)} %get-tuple-element.51.refs_4_), channel_id=1, source_target_pairs={{16,0},{32,16},{48,32},{64,48},{80,64},{96,80},{112,96},{128,112},... | collective-permute-start | bytes 1327112 | tf_op jit(solution)/shard_map/ppermute | solution.py:359
  42.8 2.8 %shard_map.109 = (bf16[512,576]{1,0:T(8,128)(2,1)S(1)}, bf16[512,192]{1,0:T(8,128)(2,1)S(1)}, bf16[144,1152]{1,0:T(8,128)(2,1)S(1)}) custom-call(s32[2]{0:T(128)S(1)} %pad_add_fusion.refs_0_, s32[8]{0:T(128)S(1)} %copy-done.3, f32[2,8,16]{2,1,0:T(8,128)S(1)} %copy-done.2, f32[8,12,12]{2,1,0:T(8,128)S(1)} %copy.12.refs_3_, s32[32,48]{1,0:T(8,128)S(1)} %copy-done.8, ...), custom_call_target="tpu_custom_call" | custom-call | flops 20000000000 | bytes 1 | tf_op jit(solution)/shard_map/pallas_call | solution.py:38
  45.9 1.7 %shard_map.115 = (f32[8,288,128]{2,1,0:T(8,128)S(1)}, f32[8,288,128]{2,1,0:T(8,128)S(1)}) custom-call(bf16[512,576]{1,0:T(8,128)(2,1)S(1)} %get-tuple-element.52.refs_0_, bf16[5,576,128]{2,1,0:T(8,128)(2,1)S(1)} %collective-permute-done.7.refs_1_, bf16[5,576,128]{2,1,0:T(8,128)(2,1)S(1)} %get-tuple-element.53.refs_2_, ...), custom_call_target="tpu_custom_call" | custom-call | flops 1 | bytes 1 | tf_op jit(solution)/shard_map/pallas_call | solution.py:38
  47.6 1.7 %shard_map.114 = (f32[8,288,128]{2,1,0:T(8,128)S(1)}, f32[8,288,128]{2,1,0:T(8,128)S(1)}) custom-call(bf16[512,576]{1,0:T(8,128)(2,1)S(1)} %get-tuple-element.52.refs_0_, bf16[5,576,128]{2,1,0:T(8,128)(2,1)S(1)} %collective-permute-done.7.refs_1_, bf16[5,576,128]{2,1,0:T(8,128)(2,1)S(1)} %get-tuple-element.53.refs_2_, ...), custom_call_target="tpu_custom_call" | custom-call | flops 1 | bytes 1 | tf_op jit(solution)/shard_map/pallas_call | solution.py:38
  49.3 2.3 %collective-permute-done.5.refs_1_ = bf16[3,576,128]{2,1,0:T(8,128)(2,1)S(1)} collective-permute-done((bf16[3,576,128]{2,1,0:T(8,128)(2,1)S(1)}, bf16[3,576,128]{2,1,0:T(8,128)(2,1)S(1)}, u32[]{:S(2)}, u32[]{:S(2)}) %collective-permute-start.5) | collective-permute-done | bytes 442400 | tf_op jit(solution)/shard_map/ppermute | solution.py:358
  51.6 4.9 %collective-permute-done.6.refs_2_ = bf16[3,576,128]{2,1,0:T(8,128)(2,1)S(1)} collective-permute-done((bf16[3,576,128]{2,1,0:T(8,128)(2,1)S(1)}, bf16[3,576,128]{2,1,0:T(8,128)(2,1)S(1)}, u32[]{:S(2)}, u32[]{:S(2)}) %collective-permute-start.6) | collective-permute-done | bytes 442400 | tf_op jit(solution)/shard_map/ppermute | solution.py:359
  56.5 0.8 shard_map.116
  57.3 3.0 %collective-permute-start.9 = (bf16[8,288,128]{2,1,0:T(8,128)(2,1)S(1)}, bf16[8,288,128]{2,1,0:T(8,128)(2,1)S(1)}, u32[]{:S(2)}, u32[]{:S(2)}) collective-permute-start(bf16[8,288,128]{2,1,0:T(8,128)(2,1)S(1)} %get-tuple-element.58), channel_id=1, source_target_pairs={{0,1},{1,0},{2,3},{3,2},{4,5},{5,4},{6,7},{7,6},{8,9},{9,8},{10,11... | collective-permute-start | bytes 1769480 | tf_op jit(solution)/shard_map/ppermute | solution.py:332
  60.2 0.8 shard_map.120
  62.0 1.2 %collective-permute-start.11 = (bf16[2,288,128]{2,1,0:T(8,128)(2,1)S(1)}, bf16[2,288,128]{2,1,0:T(8,128)(2,1)S(1)}, u32[]{:S(2)}, u32[]{:S(2)}) collective-permute-start(bf16[2,288,128]{2,1,0:T(8,128)(2,1)S(1)} %get-tuple-element.60), channel_id=1, source_target_pairs={{0,6},{1,11},{2,8},{3,13},{4,10},{5,15},{6,12},{7,1},{8,14},{9,3},... | collective-permute-start | bytes 442376 | tf_op jit(solution)/shard_map/ppermute | solution.py:338
  63.8 3.3 %collective-permute-start.10 = (bf16[1,288,128]{2,1,0:T(8,128)(2,1)S(1)}, bf16[1,288,128]{2,1,0:T(8,128)(2,1)S(1)}, u32[]{:S(2)}, u32[]{:S(2)}) collective-permute-start(bf16[1,288,128]{2,1,0:T(8,128)(2,1)S(1)} %get-tuple-element.59), channel_id=1, source_target_pairs={{0,8},{1,9},{2,10},{3,11},{4,12},{5,13},{6,14},{7,15},{8,0},{9,1},... | collective-permute-start | bytes 221192 | tf_op jit(solution)/shard_map/ppermute | solution.py:338
  67.1 2.1 %collective-permute-start.13 = (bf16[2,288,128]{2,1,0:T(8,128)(2,1)S(1)}, bf16[2,288,128]{2,1,0:T(8,128)(2,1)S(1)}, u32[]{:S(2)}, u32[]{:S(2)}) collective-permute-start(bf16[2,288,128]{2,1,0:T(8,128)(2,1)S(1)} %get-tuple-element.62), channel_id=1, source_target_pairs={{0,2},{1,15},{2,4},{3,1},{4,6},{5,3},{6,8},{7,5},{8,10},{9,7},{10,... | collective-permute-start | bytes 442376 | tf_op jit(solution)/shard_map/ppermute | solution.py:338
  69.3 1.6 %collective-permute-start.17 = (bf16[2,288,128]{2,1,0:T(8,128)(2,1)S(1)}, bf16[2,288,128]{2,1,0:T(8,128)(2,1)S(1)}, u32[]{:S(2)}, u32[]{:S(2)}) collective-permute-start(bf16[2,288,128]{2,1,0:T(8,128)(2,1)S(1)} %get-tuple-element.71), channel_id=1, source_target_pairs={{0,6},{1,11},{2,8},{3,13},{4,10},{5,15},{6,12},{7,1},{8,14},{9,3},... | collective-permute-start | bytes 442376 | tf_op jit(solution)/shard_map/ppermute | solution.py:338
  71.0 2.8 %collective-permute-done.10.refs_5_.refs_4_ = bf16[1,288,128]{2,1,0:T(8,128)(2,1)S(1)} collective-permute-done((bf16[1,288,128]{2,1,0:T(8,128)(2,1)S(1)}, bf16[1,288,128]{2,1,0:T(8,128)(2,1)S(1)}, u32[]{:S(2)}, u32[]{:S(2)}) %collective-permute-start.10) | collective-permute-done | bytes 73760 | tf_op jit(solution)/shard_map/ppermute | solution.py:338
  73.7 4.4 %collective-permute-start.18 = (bf16[2,288,128]{2,1,0:T(8,128)(2,1)S(1)}, bf16[2,288,128]{2,1,0:T(8,128)(2,1)S(1)}, u32[]{:S(2)}, u32[]{:S(2)}) collective-permute-start(bf16[2,288,128]{2,1,0:T(8,128)(2,1)S(1)} %get-tuple-element.72), channel_id=1, source_target_pairs={{0,4},{1,13},{2,6},{3,15},{4,8},{5,1},{6,10},{7,3},{8,12},{9,5},{1... | collective-permute-start | bytes 442376 | tf_op jit(solution)/shard_map/ppermute | solution.py:338
  78.1 1.9 %collective-permute-start.19 = (bf16[2,288,128]{2,1,0:T(8,128)(2,1)S(1)}, bf16[2,288,128]{2,1,0:T(8,128)(2,1)S(1)}, u32[]{:S(2)}, u32[]{:S(2)}) collective-permute-start(bf16[2,288,128]{2,1,0:T(8,128)(2,1)S(1)} %get-tuple-element.73), channel_id=1, source_target_pairs={{0,2},{1,15},{2,4},{3,1},{4,6},{5,3},{6,8},{7,5},{8,10},{9,7},{10,... | collective-permute-start | bytes 442376 | tf_op jit(solution)/shard_map/ppermute | solution.py:338
  80.0 4.0 %collective-permute-start.16 = (bf16[1,288,128]{2,1,0:T(8,128)(2,1)S(1)}, bf16[1,288,128]{2,1,0:T(8,128)(2,1)S(1)}, u32[]{:S(2)}, u32[]{:S(2)}) collective-permute-start(bf16[1,288,128]{2,1,0:T(8,128)(2,1)S(1)} %get-tuple-element.70), channel_id=1, source_target_pairs={{0,8},{1,9},{2,10},{3,11},{4,12},{5,13},{6,14},{7,15},{8,0},{9,1},... | collective-permute-start | bytes 221192 | tf_op jit(solution)/shard_map/ppermute | solution.py:338
  84.6 5.6 %collective-permute-done.16.refs_3_.refs_5_ = bf16[1,288,128]{2,1,0:T(8,128)(2,1)S(1)} collective-permute-done((bf16[1,288,128]{2,1,0:T(8,128)(2,1)S(1)}, bf16[1,288,128]{2,1,0:T(8,128)(2,1)S(1)}, u32[]{:S(2)}, u32[]{:S(2)}) %collective-permute-start.16) | collective-permute-done | bytes 73760 | tf_op jit(solution)/shard_map/ppermute | solution.py:338
  90.2 4.4 %collective-permute-start.20 = (bf16[864,128]{1,0:T(8,128)(2,1)S(1)}, bf16[864,128]{1,0:T(8,128)(2,1)S(1)}, u32[]{:S(2)}, u32[]{:S(2)}) collective-permute-start(bf16[864,128]{1,0:T(8,128)(2,1)S(1)} %shard_map.122), channel_id=1, source_target_pairs={{0,1},{1,0},{2,3},{3,2},{4,5},{5,4},{6,7},{7,6},{8,9},{9,8},{10,11... | collective-permute-start | bytes 663560 | tf_op jit(solution)/shard_map/ppermute | solution.py:332
  94.7 3.0 %shard_map.119 = (bf16[2,144,896]{2,1,0:T(8,128)(2,1)S(1)}, bf16[16,16,128]{2,1,0:T(8,128)(2,1)S(1)}, bf16[288,192]{1,0:T(8,128)(2,1)S(1)}) custom-call(s32[2]{0:T(128)S(1)} %pad_add_fusion.refs_0_, bf16[144,1152]{1,0:T(8,128)(2,1)S(1)} %get-tuple-element.40.refs_1_, bf16[5,16,128]{2,1,0:T(8,128)(2,1)S(1)} %get-tuple-element.46.refs_3_.refs_2_, ...), custom_call_target="tpu_custom_call" | custom-call | flops 1 | bytes 1 | tf_op jit(solution)/shard_map/pallas_call | solution.py:38
  97.7 4.6 %shard_map.123 = bf16[2,144,2048]{2,1,0:T(8,128)(2,1)} custom-call(s32[2]{0:T(128)S(1)} %pad_add_fusion.refs_0_, bf16[144,1152]{1,0:T(8,128)(2,1)S(1)} %get-tuple-element.40.refs_1_, bf16[16,16,128]{2,1,0:T(8,128)(2,1)S(1)} %get-tuple-element.64.refs_2_, bf16[2,144,896]{2,1,0:T(8,128)(2,1)S(1)} %get-tuple-element.65.refs_3_, ...), custom_call_target="tpu_custom_call" | custom-call | flops 1 | bytes 1 | tf_op jit(solution)/shard_map/pallas_call | solution.py:38
  (49 shorter events, 5.2 us)
Async XLA Ops:
  0.1 1.3 %copy-start = (bf16[2,1,144,2048]{3,2,1,0:T(8,128)(2,1)S(1)}, bf16[2,1,144,2048]{3,2,1,0:T(8,128)(2,1)}, u32[]{:S(2)}) copy-start(bf16[2,1,144,2048]{3,2,1,0:T(8,128)(2,1)} %param.11) | copy-start | bytes 3538948
  1.3 0.7 copy-start.1
  2.0 15.0 %copy-start.10 = (f32[8,12,12]{2,0,1:T(8,128)S(1)}, f32[8,12,12]{2,0,1:T(8,128)}, u32[]{:S(2)}) copy-start(f32[8,12,12]{2,0,1:T(8,128)} %param.15) | copy-start | bytes 13828
  2.9 39.8 %copy-start.2 = (f32[2,8,16]{2,1,0:T(8,128)S(1)}, f32[2,8,16]{2,1,0:T(8,128)}, u32[]{:S(2)}) copy-start(f32[2,8,16]{2,1,0:T(8,128)} %refs_2_.1) | copy-start | bytes 3076
  2.9 39.8 %copy-start.3 = (s32[8]{0:T(128)S(1)}, s32[8]{0:T(128)}, u32[]{:S(2)}) copy-start(s32[8]{0:T(128)} %refs_1_.1) | copy-start | bytes 100
  2.9 39.8 %copy-start.4 = (f32[96,1152]{1,0:T(8,128)S(1)}, f32[96,1152]{1,0:T(8,128)}, u32[]{:S(2)}) copy-start(f32[96,1152]{1,0:T(8,128)} %constant.28.clone.refs_8_) | copy-start | bytes 1327108
  2.9 39.8 %copy-start.5 = (f32[96,1152]{1,0:T(8,128)S(1)}, f32[96,1152]{1,0:T(8,128)}, u32[]{:S(2)}) copy-start(f32[96,1152]{1,0:T(8,128)} %constant.29.clone.refs_9_) | copy-start | bytes 1327108
  2.9 39.8 %copy-start.6 = (f32[144,12]{1,0:T(8,128)S(1)}, f32[144,12]{1,0:T(8,128)}, u32[]{:S(2)}) copy-start(f32[144,12]{1,0:T(8,128)} %constant.26.clone.refs_6_) | copy-start | bytes 20740
  3.0 39.8 %copy-start.7 = (f32[144,12]{1,0:T(8,128)S(1)}, f32[144,12]{1,0:T(8,128)}, u32[]{:S(2)}) copy-start(f32[144,12]{1,0:T(8,128)} %constant.27.clone.refs_7_) | copy-start | bytes 20740
  3.0 39.8 %copy-start.8 = (s32[32,48]{1,0:T(8,128)S(1)}, s32[32,48]{1,0:T(8,128)}, u32[]{:S(2)}) copy-start(s32[32,48]{1,0:T(8,128)} %constant.24.clone.refs_4_) | copy-start | bytes 18436
  3.0 39.8 %copy-start.9 = (s32[32,48]{1,0:T(8,128)S(1)}, s32[32,48]{1,0:T(8,128)}, u32[]{:S(2)}) copy-start(s32[32,48]{1,0:T(8,128)} %constant.25.clone.refs_5_) | copy-start | bytes 18436
  3.0 2.2 %collective-permute-start = (bf16[3,592,128]{2,1,0:T(8,128)(2,1)S(1)}, bf16[3,592,128]{2,1,0:T(8,128)(2,1)S(1)}, u32[]{:S(2)}, u32[]{:S(2)}) collective-permute-start(bf16[3,592,128]{2,1,0:T(8,128)(2,1)S(1)} %get-tuple-element.42), channel_id=1, source_target_pairs={{0,1},{1,0},{2,3},{3,2},{4,5},{5,4},{6,7},{7,6},{8,9},{9,8},{10,11... | collective-permute-start | bytes 1363976 | tf_op jit(solution)/shard_map/ppermute | solution.py:332
  5.3 12.3 %collective-permute-start.1 = (bf16[2,592,128]{2,1,0:T(8,128)(2,1)S(1)}, bf16[2,592,128]{2,1,0:T(8,128)(2,1)S(1)}, u32[]{:S(2)}, u32[]{:S(2)}) collective-permute-start(bf16[2,592,128]{2,1,0:T(8,128)(2,1)S(1)} %get-tuple-element.43), channel_id=1, source_target_pairs={{0,2},{1,15},{2,4},{3,1},{4,6},{5,3},{6,8},{7,5},{8,10},{9,7},{10,... | collective-permute-start | bytes 909320 | tf_op jit(solution)/shard_map/ppermute | solution.py:338
  10.9 13.2 %collective-permute-start.2 = (bf16[2,592,128]{2,1,0:T(8,128)(2,1)S(1)}, bf16[2,592,128]{2,1,0:T(8,128)(2,1)S(1)}, u32[]{:S(2)}, u32[]{:S(2)}) collective-permute-start(bf16[2,592,128]{2,1,0:T(8,128)(2,1)S(1)} %get-tuple-element.44), channel_id=1, source_target_pairs={{0,4},{1,13},{2,6},{3,15},{4,8},{5,1},{6,10},{7,3},{8,12},{9,5},{1... | collective-permute-start | bytes 909320 | tf_op jit(solution)/shard_map/ppermute | solution.py:338
  12.1 25.3 %collective-permute-start.3 = (bf16[2,592,128]{2,1,0:T(8,128)(2,1)S(1)}, bf16[2,592,128]{2,1,0:T(8,128)(2,1)S(1)}, u32[]{:S(2)}, u32[]{:S(2)}) collective-permute-start(bf16[2,592,128]{2,1,0:T(8,128)(2,1)S(1)} %get-tuple-element.47), channel_id=1, source_target_pairs={{0,6},{1,11},{2,8},{3,13},{4,10},{5,15},{6,12},{7,1},{8,14},{9,3},... | collective-permute-start | bytes 909320 | tf_op jit(solution)/shard_map/ppermute | solution.py:338
  12.5 17.0 %collective-permute-start.4 = (bf16[1,592,128]{2,1,0:T(8,128)(2,1)S(1)}, bf16[1,592,128]{2,1,0:T(8,128)(2,1)S(1)}, u32[]{:S(2)}, u32[]{:S(2)}) collective-permute-start(bf16[1,592,128]{2,1,0:T(8,128)(2,1)S(1)} %get-tuple-element.48), channel_id=1, source_target_pairs={{0,8},{1,9},{2,10},{3,11},{4,12},{5,13},{6,14},{7,15},{8,0},{9,1},... | collective-permute-start | bytes 454664 | tf_op jit(solution)/shard_map/ppermute | solution.py:338
  24.2 21.4 %collective-permute-start.7 = (bf16[5,576,128]{2,1,0:T(8,128)(2,1)S(1)}, bf16[5,576,128]{2,1,0:T(8,128)(2,1)S(1)}, u32[]{:S(2)}, u32[]{:S(2)}) collective-permute-start(bf16[5,576,128]{2,1,0:T(8,128)(2,1)S(1)} %get-tuple-element.53.refs_2_), channel_id=1, source_target_pairs={{0,16},{16,32},{32,48},{48,64},{64,80},{80,96},{96,112},{112,128},... | collective-permute-start | bytes 2211848 | tf_op jit(solution)/shard_map/ppermute | solution.py:358
  27.0 18.9 %collective-permute-start.8 = (bf16[5,576,128]{2,1,0:T(8,128)(2,1)S(1)}, bf16[5,576,128]{2,1,0:T(8,128)(2,1)S(1)}, u32[]{:S(2)}, u32[]{:S(2)}) collective-permute-start(bf16[5,576,128]{2,1,0:T(8,128)(2,1)S(1)} %get-tuple-element.53.refs_2_), channel_id=1, source_target_pairs={{16,0},{32,16},{48,32},{64,48},{80,64},{96,80},{112,96},{128,112},... | collective-permute-start | bytes 2211848 | tf_op jit(solution)/shard_map/ppermute | solution.py:359
  37.4 14.1 %collective-permute-start.5 = (bf16[3,576,128]{2,1,0:T(8,128)(2,1)S(1)}, bf16[3,576,128]{2,1,0:T(8,128)(2,1)S(1)}, u32[]{:S(2)}, u32[]{:S(2)}) collective-permute-start(bf16[3,576,128]{2,1,0:T(8,128)(2,1)S(1)} %get-tuple-element.51.refs_4_), channel_id=1, source_target_pairs={{0,16},{16,32},{32,48},{48,64},{64,80},{80,96},{96,112},{112,128},... | collective-permute-start | bytes 1327112 | tf_op jit(solution)/shard_map/ppermute | solution.py:358
  40.2 16.3 %collective-permute-start.6 = (bf16[3,576,128]{2,1,0:T(8,128)(2,1)S(1)}, bf16[3,576,128]{2,1,0:T(8,128)(2,1)S(1)}, u32[]{:S(2)}, u32[]{:S(2)}) collective-permute-start(bf16[3,576,128]{2,1,0:T(8,128)(2,1)S(1)} %get-tuple-element.51.refs_4_), channel_id=1, source_target_pairs={{16,0},{32,16},{48,32},{64,48},{80,64},{96,80},{112,96},{128,112},... | collective-permute-start | bytes 1327112 | tf_op jit(solution)/shard_map/ppermute | solution.py:359
  57.3 4.6 %collective-permute-start.9 = (bf16[8,288,128]{2,1,0:T(8,128)(2,1)S(1)}, bf16[8,288,128]{2,1,0:T(8,128)(2,1)S(1)}, u32[]{:S(2)}, u32[]{:S(2)}) collective-permute-start(bf16[8,288,128]{2,1,0:T(8,128)(2,1)S(1)} %get-tuple-element.58), channel_id=1, source_target_pairs={{0,1},{1,0},{2,3},{3,2},{4,5},{5,4},{6,7},{7,6},{8,9},{9,8},{10,11... | collective-permute-start | bytes 1769480 | tf_op jit(solution)/shard_map/ppermute | solution.py:332
  61.0 8.2 %collective-permute-start.15 = (bf16[8,288,128]{2,1,0:T(8,128)(2,1)S(1)}, bf16[8,288,128]{2,1,0:T(8,128)(2,1)S(1)}, u32[]{:S(2)}, u32[]{:S(2)}) collective-permute-start(bf16[8,288,128]{2,1,0:T(8,128)(2,1)S(1)} %get-tuple-element.69), channel_id=1, source_target_pairs={{0,1},{1,0},{2,3},{3,2},{4,5},{5,4},{6,7},{7,6},{8,9},{9,8},{10,11... | collective-permute-start | bytes 1769480 | tf_op jit(solution)/shard_map/ppermute | solution.py:332
  62.0 16.1 %collective-permute-start.11 = (bf16[2,288,128]{2,1,0:T(8,128)(2,1)S(1)}, bf16[2,288,128]{2,1,0:T(8,128)(2,1)S(1)}, u32[]{:S(2)}, u32[]{:S(2)}) collective-permute-start(bf16[2,288,128]{2,1,0:T(8,128)(2,1)S(1)} %get-tuple-element.60), channel_id=1, source_target_pairs={{0,6},{1,11},{2,8},{3,13},{4,10},{5,15},{6,12},{7,1},{8,14},{9,3},... | collective-permute-start | bytes 442376 | tf_op jit(solution)/shard_map/ppermute | solution.py:338
  63.2 16.9 %collective-permute-start.12 = (bf16[2,288,128]{2,1,0:T(8,128)(2,1)S(1)}, bf16[2,288,128]{2,1,0:T(8,128)(2,1)S(1)}, u32[]{:S(2)}, u32[]{:S(2)}) collective-permute-start(bf16[2,288,128]{2,1,0:T(8,128)(2,1)S(1)} %get-tuple-element.61), channel_id=1, source_target_pairs={{0,4},{1,13},{2,6},{3,15},{4,8},{5,1},{6,10},{7,3},{8,12},{9,5},{1... | collective-permute-start | bytes 442376 | tf_op jit(solution)/shard_map/ppermute | solution.py:338
  63.8 10.0 %collective-permute-start.10 = (bf16[1,288,128]{2,1,0:T(8,128)(2,1)S(1)}, bf16[1,288,128]{2,1,0:T(8,128)(2,1)S(1)}, u32[]{:S(2)}, u32[]{:S(2)}) collective-permute-start(bf16[1,288,128]{2,1,0:T(8,128)(2,1)S(1)} %get-tuple-element.59), channel_id=1, source_target_pairs={{0,8},{1,9},{2,10},{3,11},{4,12},{5,13},{6,14},{7,15},{8,0},{9,1},... | collective-permute-start | bytes 221192 | tf_op jit(solution)/shard_map/ppermute | solution.py:338
  67.1 16.9 %collective-permute-start.13 = (bf16[2,288,128]{2,1,0:T(8,128)(2,1)S(1)}, bf16[2,288,128]{2,1,0:T(8,128)(2,1)S(1)}, u32[]{:S(2)}, u32[]{:S(2)}) collective-permute-start(bf16[2,288,128]{2,1,0:T(8,128)(2,1)S(1)} %get-tuple-element.62), channel_id=1, source_target_pairs={{0,2},{1,15},{2,4},{3,1},{4,6},{5,3},{6,8},{7,5},{8,10},{9,7},{10,... | collective-permute-start | bytes 442376 | tf_op jit(solution)/shard_map/ppermute | solution.py:338
  69.3 20.9 %collective-permute-start.17 = (bf16[2,288,128]{2,1,0:T(8,128)(2,1)S(1)}, bf16[2,288,128]{2,1,0:T(8,128)(2,1)S(1)}, u32[]{:S(2)}, u32[]{:S(2)}) collective-permute-start(bf16[2,288,128]{2,1,0:T(8,128)(2,1)S(1)} %get-tuple-element.71), channel_id=1, source_target_pairs={{0,6},{1,11},{2,8},{3,13},{4,10},{5,15},{6,12},{7,1},{8,14},{9,3},... | collective-permute-start | bytes 442376 | tf_op jit(solution)/shard_map/ppermute | solution.py:338
  73.7 16.5 %collective-permute-start.18 = (bf16[2,288,128]{2,1,0:T(8,128)(2,1)S(1)}, bf16[2,288,128]{2,1,0:T(8,128)(2,1)S(1)}, u32[]{:S(2)}, u32[]{:S(2)}) collective-permute-start(bf16[2,288,128]{2,1,0:T(8,128)(2,1)S(1)} %get-tuple-element.72), channel_id=1, source_target_pairs={{0,4},{1,13},{2,6},{3,15},{4,8},{5,1},{6,10},{7,3},{8,12},{9,5},{1... | collective-permute-start | bytes 442376 | tf_op jit(solution)/shard_map/ppermute | solution.py:338
  78.1 12.1 %collective-permute-start.19 = (bf16[2,288,128]{2,1,0:T(8,128)(2,1)S(1)}, bf16[2,288,128]{2,1,0:T(8,128)(2,1)S(1)}, u32[]{:S(2)}, u32[]{:S(2)}) collective-permute-start(bf16[2,288,128]{2,1,0:T(8,128)(2,1)S(1)} %get-tuple-element.73), channel_id=1, source_target_pairs={{0,2},{1,15},{2,4},{3,1},{4,6},{5,3},{6,8},{7,5},{8,10},{9,7},{10,... | collective-permute-start | bytes 442376 | tf_op jit(solution)/shard_map/ppermute | solution.py:338
  80.0 10.2 %collective-permute-start.16 = (bf16[1,288,128]{2,1,0:T(8,128)(2,1)S(1)}, bf16[1,288,128]{2,1,0:T(8,128)(2,1)S(1)}, u32[]{:S(2)}, u32[]{:S(2)}) collective-permute-start(bf16[1,288,128]{2,1,0:T(8,128)(2,1)S(1)} %get-tuple-element.70), channel_id=1, source_target_pairs={{0,8},{1,9},{2,10},{3,11},{4,12},{5,13},{6,14},{7,15},{8,0},{9,1},... | collective-permute-start | bytes 221192 | tf_op jit(solution)/shard_map/ppermute | solution.py:338
  84.0 10.7 %collective-permute-start.14 = (bf16[992,128]{1,0:T(8,128)(2,1)S(1)}, bf16[992,128]{1,0:T(8,128)(2,1)S(1)}, u32[]{:S(2)}, u32[]{:S(2)}) collective-permute-start(bf16[992,128]{1,0:T(8,128)(2,1)S(1)} %shard_map.118), channel_id=1, source_target_pairs={{0,1},{1,0},{2,3},{3,2},{4,5},{5,4},{6,7},{7,6},{8,9},{9,8},{10,11... | collective-permute-start | bytes 761864 | tf_op jit(solution)/shard_map/ppermute | solution.py:332
  90.2 7.5 %collective-permute-start.20 = (bf16[864,128]{1,0:T(8,128)(2,1)S(1)}, bf16[864,128]{1,0:T(8,128)(2,1)S(1)}, u32[]{:S(2)}, u32[]{:S(2)}) collective-permute-start(bf16[864,128]{1,0:T(8,128)(2,1)S(1)} %shard_map.122), channel_id=1, source_target_pairs={{0,1},{1,0},{2,3},{3,2},{4,5},{5,4},{6,7},{7,6},{8,9},{9,8},{10,11... | collective-permute-start | bytes 663560 | tf_op jit(solution)/shard_map/ppermute | solution.py:332

commit v6 on v5

--- a/solution.py
+++ b/solution.py
@@ -213,7 +213,7 @@
 def pick_kernel(*refs):
     blocks, extra, out = refs[: len(NEAR)], refs[len(NEAR) : -1], refs[-1]
     rows = blocks[0].shape[1]
-    for i, block in enumerate(blocks):
+    for i, block in enumerate(reversed(blocks)):
         out[i * rows : (i + 1) * rows, :] = block[1]
     at = len(NEAR) * rows
     for near in extra:
@@ -224,7 +224,7 @@
 
 def pick(blocks, *extra, after=()):
     height = len(NEAR) * blocks[1].shape[1] + sum(x.shape[0] * x.shape[1] for x in extra)
-    return call(pick_kernel, [((height, LANES), BF16)], *blocks[3:0:-1], *extra, after=(blocks[0], *after))[0]
+    return call(pick_kernel, [((height, LANES), BF16)], *blocks[1:4], *extra, after=(blocks[0], *after))[0]
 
 
 def gather_line(pos_ref, groups, line, base, far_ref, three_ref, two_ref, one_ref, home_ref, given_ref):

time: 103 us -> 103 us (level)
  no operation moved by 1% of the time
where the time goes in v6:
time: 103 us; the launch traced here: 102 us
  starting transfers between devices  50.3 us (49%)
  waiting for transfers between devices  33.1 us (32%)
  Pallas kernels  16.5 us (16%)
  local copies, waits for them, and re-layouts  2.02 us (2%)
    ppermute x12, starting transfers between devices, round_ring(): return lax.ppermute(x, KMOM, pairs)  30.9 us
    ppermute x12, waiting for transfers between devices, round_ring(): return lax.ppermute(x, KMOM, pairs)  23.4 us
    pallas_call x15, Pallas kernels, call(): pl.pallas_call(run, out_shape=[jax.ShapeDtypeStruct(shape, dtype) for sha...  16.5 us
    ppermute x5, starting transfers between devices, swap(): return lax.ppermute(x, 'core', [(0, 1), (1, 0)])  8.84 us
    ppermute x2, starting transfers between devices, body(): low = [lax.ppermute(x, 'energy', forward) for x in fields]  5.56 us
    ppermute x2, waiting for transfers between devices, body(): high = [lax.ppermute(x, 'energy', backward) for x in fields]  5.16 us
    ppermute x2, starting transfers between devices, body(): high = [lax.ppermute(x, 'energy', backward) for x in fields]  5.01 us
    ppermute x2, waiting for transfers between devices, body(): low = [lax.ppermute(x, 'energy', forward) for x in fields]  2.33 us
  transfers between devices with their start and end apart: 21, of which 10 were waited for; matrix products, arithmetic and copies ran while one was open for 0% of the time, Pallas kernels for 10%

profile of v6, /device:TPU:25, one launch (start us, length us, event | category | flops | bytes accessed | tf_op | source)
XLA Modules:
  0.0 102.3 jit_solution(15405576271129829405)
XLA Ops:
  0.1 1.3 %copy-done = bf16[2,1,144,2048]{3,2,1,0:T(8,128)(2,1)S(1)} copy-done((bf16[2,1,144,2048]{3,2,1,0:T(8,128)(2,1)S(1)}, bf16[2,1,144,2048]{3,2,1,0:T(8,128)(2,1)}, u32[]{:S(2)}) %copy-start) | copy-done | bytes 1179672
  2.0 0.8 shard_map.110
  3.8 1.4 %collective-permute-done.refs_1_ = bf16[3,592,128]{2,1,0:T(8,128)(2,1)S(1)} collective-permute-done((bf16[3,592,128]{2,1,0:T(8,128)(2,1)S(1)}, bf16[3,592,128]{2,1,0:T(8,128)(2,1)S(1)}, u32[]{:S(2)}, u32[]{:S(2)}) %collective-permute-start) | collective-permute-done | bytes 454688 | tf_op jit(solution)/shard_map/ppermute | solution.py:332
  5.3 5.7 %collective-permute-start.1 = (bf16[2,592,128]{2,1,0:T(8,128)(2,1)S(1)}, bf16[2,592,128]{2,1,0:T(8,128)(2,1)S(1)}, u32[]{:S(2)}, u32[]{:S(2)}) collective-permute-start(bf16[2,592,128]{2,1,0:T(8,128)(2,1)S(1)} %get-tuple-element.43), channel_id=1, source_target_pairs={{0,2},{1,15},{2,4},{3,1},{4,6},{5,3},{6,8},{7,5},{8,10},{9,7},{10,... | collective-permute-start | bytes 909320 | tf_op jit(solution)/shard_map/ppermute | solution.py:338
  10.9 1.2 %collective-permute-start.2 = (bf16[2,592,128]{2,1,0:T(8,128)(2,1)S(1)}, bf16[2,592,128]{2,1,0:T(8,128)(2,1)S(1)}, u32[]{:S(2)}, u32[]{:S(2)}) collective-permute-start(bf16[2,592,128]{2,1,0:T(8,128)(2,1)S(1)} %get-tuple-element.44), channel_id=1, source_target_pairs={{0,4},{1,13},{2,6},{3,15},{4,8},{5,1},{6,10},{7,3},{8,12},{9,5},{1... | collective-permute-start | bytes 909320 | tf_op jit(solution)/shard_map/ppermute | solution.py:338
  12.5 4.5 %collective-permute-start.4 = (bf16[1,592,128]{2,1,0:T(8,128)(2,1)S(1)}, bf16[1,592,128]{2,1,0:T(8,128)(2,1)S(1)}, u32[]{:S(2)}, u32[]{:S(2)}) collective-permute-start(bf16[1,592,128]{2,1,0:T(8,128)(2,1)S(1)} %get-tuple-element.48), channel_id=1, source_target_pairs={{0,8},{1,9},{2,10},{3,11},{4,12},{5,13},{6,14},{7,15},{8,0},{9,1},... | collective-permute-start | bytes 454664 | tf_op jit(solution)/shard_map/ppermute | solution.py:338
  17.5 6.6 %collective-permute-done.2.refs_1_ = bf16[2,592,128]{2,1,0:T(8,128)(2,1)S(1)} collective-permute-done((bf16[2,592,128]{2,1,0:T(8,128)(2,1)S(1)}, bf16[2,592,128]{2,1,0:T(8,128)(2,1)S(1)}, u32[]{:S(2)}, u32[]{:S(2)}) %collective-permute-start.2) | collective-permute-done | bytes 303136 | tf_op jit(solution)/shard_map/ppermute | solution.py:338
  24.2 2.8 %collective-permute-start.7 = (bf16[5,576,128]{2,1,0:T(8,128)(2,1)S(1)}, bf16[5,576,128]{2,1,0:T(8,128)(2,1)S(1)}, u32[]{:S(2)}, u32[]{:S(2)}) collective-permute-start(bf16[5,576,128]{2,1,0:T(8,128)(2,1)S(1)} %get-tuple-element.53.refs_2_), channel_id=1, source_target_pairs={{0,16},{16,32},{32,48},{48,64},{64,80},{80,96},{96,112},{112,128},... | collective-permute-start | bytes 2211848 | tf_op jit(solution)/shard_map/ppermute | solution.py:358
  27.0 2.5 %collective-permute-start.8 = (bf16[5,576,128]{2,1,0:T(8,128)(2,1)S(1)}, bf16[5,576,128]{2,1,0:T(8,128)(2,1)S(1)}, u32[]{:S(2)}, u32[]{:S(2)}) collective-permute-start(bf16[5,576,128]{2,1,0:T(8,128)(2,1)S(1)} %get-tuple-element.53.refs_2_), channel_id=1, source_target_pairs={{16,0},{32,16},{48,32},{64,48},{80,64},{96,80},{112,96},{128,112},... | collective-permute-start | bytes 2211848 | tf_op jit(solution)/shard_map/ppermute | solution.py:359
  29.5 7.9 %collective-permute-done.3.refs_0_ = bf16[2,592,128]{2,1,0:T(8,128)(2,1)S(1)} collective-permute-done((bf16[2,592,128]{2,1,0:T(8,128)(2,1)S(1)}, bf16[2,592,128]{2,1,0:T(8,128)(2,1)S(1)}, u32[]{:S(2)}, u32[]{:S(2)}) %collective-permute-start.3) | collective-permute-done | bytes 303136 | tf_op jit(solution)/shard_map/ppermute | solution.py:338
  37.4 2.8 %collective-permute-start.5 = (bf16[3,576,128]{2,1,0:T(8,128)(2,1)S(1)}, bf16[3,576,128]{2,1,0:T(8,128)(2,1)S(1)}, u32[]{:S(2)}, u32[]{:S(2)}) collective-permute-start(bf16[3,576,128]{2,1,0:T(8,128)(2,1)S(1)} %get-tuple-element.51.refs_4_), channel_id=1, source_target_pairs={{0,16},{16,32},{32,48},{48,64},{64,80},{80,96},{96,112},{112,128},... | collective-permute-start | bytes 1327112 | tf_op jit(solution)/shard_map/ppermute | solution.py:358
  40.2 2.5 %collective-permute-start.6 = (bf16[3,576,128]{2,1,0:T(8,128)(2,1)S(1)}, bf16[3,576,128]{2,1,0:T(8,128)(2,1)S(1)}, u32[]{:S(2)}, u32[]{:S(2)}) collective-permute-start(bf16[3,576,128]{2,1,0:T(8,128)(2,1)S(1)} %get-tuple-element.51.refs_4_), channel_id=1, source_target_pairs={{16,0},{32,16},{48,32},{64,48},{80,64},{96,80},{112,96},{128,112},... | collective-permute-start | bytes 1327112 | tf_op jit(solution)/shard_map/ppermute | solution.py:359
  42.8 2.8 %shard_map.109 = (bf16[512,576]{1,0:T(8,128)(2,1)S(1)}, bf16[512,192]{1,0:T(8,128)(2,1)S(1)}, bf16[144,1152]{1,0:T(8,128)(2,1)S(1)}) custom-call(s32[2]{0:T(128)S(1)} %pad_add_fusion.refs_0_, s32[8]{0:T(128)S(1)} %copy-done.3, f32[2,8,16]{2,1,0:T(8,128)S(1)} %copy-done.2, f32[8,12,12]{2,1,0:T(8,128)S(1)} %copy.12.refs_3_, s32[32,48]{1,0:T(8,128)S(1)} %copy-done.8, ...), custom_call_target="tpu_custom_call" | custom-call | flops 20000000000 | bytes 1 | tf_op jit(solution)/shard_map/pallas_call | solution.py:38
  45.9 1.7 %shard_map.115 = (f32[8,288,128]{2,1,0:T(8,128)S(1)}, f32[8,288,128]{2,1,0:T(8,128)S(1)}) custom-call(bf16[512,576]{1,0:T(8,128)(2,1)S(1)} %get-tuple-element.52.refs_0_, bf16[5,576,128]{2,1,0:T(8,128)(2,1)S(1)} %collective-permute-done.7.refs_1_, bf16[5,576,128]{2,1,0:T(8,128)(2,1)S(1)} %get-tuple-element.53.refs_2_, ...), custom_call_target="tpu_custom_call" | custom-call | flops 1 | bytes 1 | tf_op jit(solution)/shard_map/pallas_call | solution.py:38
  47.6 1.7 %shard_map.114 = (f32[8,288,128]{2,1,0:T(8,128)S(1)}, f32[8,288,128]{2,1,0:T(8,128)S(1)}) custom-call(bf16[512,576]{1,0:T(8,128)(2,1)S(1)} %get-tuple-element.52.refs_0_, bf16[5,576,128]{2,1,0:T(8,128)(2,1)S(1)} %collective-permute-done.7.refs_1_, bf16[5,576,128]{2,1,0:T(8,128)(2,1)S(1)} %get-tuple-element.53.refs_2_, ...), custom_call_target="tpu_custom_call" | custom-call | flops 1 | bytes 1 | tf_op jit(solution)/shard_map/pallas_call | solution.py:38
  49.3 2.3 %collective-permute-done.5.refs_1_ = bf16[3,576,128]{2,1,0:T(8,128)(2,1)S(1)} collective-permute-done((bf16[3,576,128]{2,1,0:T(8,128)(2,1)S(1)}, bf16[3,576,128]{2,1,0:T(8,128)(2,1)S(1)}, u32[]{:S(2)}, u32[]{:S(2)}) %collective-permute-start.5) | collective-permute-done | bytes 442400 | tf_op jit(solution)/shard_map/ppermute | solution.py:358
  51.6 4.9 %collective-permute-done.6.refs_2_ = bf16[3,576,128]{2,1,0:T(8,128)(2,1)S(1)} collective-permute-done((bf16[3,576,128]{2,1,0:T(8,128)(2,1)S(1)}, bf16[3,576,128]{2,1,0:T(8,128)(2,1)S(1)}, u32[]{:S(2)}, u32[]{:S(2)}) %collective-permute-start.6) | collective-permute-done | bytes 442400 | tf_op jit(solution)/shard_map/ppermute | solution.py:359
  56.5 0.8 shard_map.116
  57.3 3.0 %collective-permute-start.9 = (bf16[8,288,128]{2,1,0:T(8,128)(2,1)S(1)}, bf16[8,288,128]{2,1,0:T(8,128)(2,1)S(1)}, u32[]{:S(2)}, u32[]{:S(2)}) collective-permute-start(bf16[8,288,128]{2,1,0:T(8,128)(2,1)S(1)} %get-tuple-element.58), channel_id=1, source_target_pairs={{0,1},{1,0},{2,3},{3,2},{4,5},{5,4},{6,7},{7,6},{8,9},{9,8},{10,11... | collective-permute-start | bytes 1769480 | tf_op jit(solution)/shard_map/ppermute | solution.py:332
  60.2 0.8 shard_map.120
  62.0 1.2 %collective-permute-start.11 = (bf16[2,288,128]{2,1,0:T(8,128)(2,1)S(1)}, bf16[2,288,128]{2,1,0:T(8,128)(2,1)S(1)}, u32[]{:S(2)}, u32[]{:S(2)}) collective-permute-start(bf16[2,288,128]{2,1,0:T(8,128)(2,1)S(1)} %get-tuple-element.60), channel_id=1, source_target_pairs={{0,6},{1,11},{2,8},{3,13},{4,10},{5,15},{6,12},{7,1},{8,14},{9,3},... | collective-permute-start | bytes 442376 | tf_op jit(solution)/shard_map/ppermute | solution.py:338
  63.8 3.3 %collective-permute-start.10 = (bf16[1,288,128]{2,1,0:T(8,128)(2,1)S(1)}, bf16[1,288,128]{2,1,0:T(8,128)(2,1)S(1)}, u32[]{:S(2)}, u32[]{:S(2)}) collective-permute-start(bf16[1,288,128]{2,1,0:T(8,128)(2,1)S(1)} %get-tuple-element.59), channel_id=1, source_target_pairs={{0,8},{1,9},{2,10},{3,11},{4,12},{5,13},{6,14},{7,15},{8,0},{9,1},... | collective-permute-start | bytes 221192 | tf_op jit(solution)/shard_map/ppermute | solution.py:338
  67.1 2.1 %collective-permute-start.13 = (bf16[2,288,128]{2,1,0:T(8,128)(2,1)S(1)}, bf16[2,288,128]{2,1,0:T(8,128)(2,1)S(1)}, u32[]{:S(2)}, u32[]{:S(2)}) collective-permute-start(bf16[2,288,128]{2,1,0:T(8,128)(2,1)S(1)} %get-tuple-element.62), channel_id=1, source_target_pairs={{0,2},{1,15},{2,4},{3,1},{4,6},{5,3},{6,8},{7,5},{8,10},{9,7},{10,... | collective-permute-start | bytes 442376 | tf_op jit(solution)/shard_map/ppermute | solution.py:338
  69.3 1.6 %collective-permute-start.17 = (bf16[2,288,128]{2,1,0:T(8,128)(2,1)S(1)}, bf16[2,288,128]{2,1,0:T(8,128)(2,1)S(1)}, u32[]{:S(2)}, u32[]{:S(2)}) collective-permute-start(bf16[2,288,128]{2,1,0:T(8,128)(2,1)S(1)} %get-tuple-element.71), channel_id=1, source_target_pairs={{0,6},{1,11},{2,8},{3,13},{4,10},{5,15},{6,12},{7,1},{8,14},{9,3},... | collective-permute-start | bytes 442376 | tf_op jit(solution)/shard_map/ppermute | solution.py:338
  71.0 2.8 %collective-permute-done.10.refs_5_.refs_4_ = bf16[1,288,128]{2,1,0:T(8,128)(2,1)S(1)} collective-permute-done((bf16[1,288,128]{2,1,0:T(8,128)(2,1)S(1)}, bf16[1,288,128]{2,1,0:T(8,128)(2,1)S(1)}, u32[]{:S(2)}, u32[]{:S(2)}) %collective-permute-start.10) | collective-permute-done | bytes 73760 | tf_op jit(solution)/shard_map/ppermute | solution.py:338
  73.7 4.4 %collective-permute-start.18 = (bf16[2,288,128]{2,1,0:T(8,128)(2,1)S(1)}, bf16[2,288,128]{2,1,0:T(8,128)(2,1)S(1)}, u32[]{:S(2)}, u32[]{:S(2)}) collective-permute-start(bf16[2,288,128]{2,1,0:T(8,128)(2,1)S(1)} %get-tuple-element.72), channel_id=1, source_target_pairs={{0,4},{1,13},{2,6},{3,15},{4,8},{5,1},{6,10},{7,3},{8,12},{9,5},{1... | collective-permute-start | bytes 442376 | tf_op jit(solution)/shard_map/ppermute | solution.py:338
  78.1 1.9 %collective-permute-start.19 = (bf16[2,288,128]{2,1,0:T(8,128)(2,1)S(1)}, bf16[2,288,128]{2,1,0:T(8,128)(2,1)S(1)}, u32[]{:S(2)}, u32[]{:S(2)}) collective-permute-start(bf16[2,288,128]{2,1,0:T(8,128)(2,1)S(1)} %get-tuple-element.73), channel_id=1, source_target_pairs={{0,2},{1,15},{2,4},{3,1},{4,6},{5,3},{6,8},{7,5},{8,10},{9,7},{10,... | collective-permute-start | bytes 442376 | tf_op jit(solution)/shard_map/ppermute | solution.py:338
  80.0 4.0 %collective-permute-start.16 = (bf16[1,288,128]{2,1,0:T(8,128)(2,1)S(1)}, bf16[1,288,128]{2,1,0:T(8,128)(2,1)S(1)}, u32[]{:S(2)}, u32[]{:S(2)}) collective-permute-start(bf16[1,288,128]{2,1,0:T(8,128)(2,1)S(1)} %get-tuple-element.70), channel_id=1, source_target_pairs={{0,8},{1,9},{2,10},{3,11},{4,12},{5,13},{6,14},{7,15},{8,0},{9,1},... | collective-permute-start | bytes 221192 | tf_op jit(solution)/shard_map/ppermute | solution.py:338
  84.6 5.6 %collective-permute-done.16.refs_3_.refs_5_ = bf16[1,288,128]{2,1,0:T(8,128)(2,1)S(1)} collective-permute-done((bf16[1,288,128]{2,1,0:T(8,128)(2,1)S(1)}, bf16[1,288,128]{2,1,0:T(8,128)(2,1)S(1)}, u32[]{:S(2)}, u32[]{:S(2)}) %collective-permute-start.16) | collective-permute-done | bytes 73760 | tf_op jit(solution)/shard_map/ppermute | solution.py:338
  90.2 4.4 %collective-permute-start.20 = (bf16[864,128]{1,0:T(8,128)(2,1)S(1)}, bf16[864,128]{1,0:T(8,128)(2,1)S(1)}, u32[]{:S(2)}, u32[]{:S(2)}) collective-permute-start(bf16[864,128]{1,0:T(8,128)(2,1)S(1)} %shard_map.122), channel_id=1, source_target_pairs={{0,1},{1,0},{2,3},{3,2},{4,5},{5,4},{6,7},{7,6},{8,9},{9,8},{10,11... | collective-permute-start | bytes 663560 | tf_op jit(solution)/shard_map/ppermute | solution.py:332
  94.7 3.0 %shard_map.119 = (bf16[2,144,896]{2,1,0:T(8,128)(2,1)S(1)}, bf16[16,16,128]{2,1,0:T(8,128)(2,1)S(1)}, bf16[288,192]{1,0:T(8,128)(2,1)S(1)}) custom-call(s32[2]{0:T(128)S(1)} %pad_add_fusion.refs_0_, bf16[144,1152]{1,0:T(8,128)(2,1)S(1)} %get-tuple-element.40.refs_1_, bf16[5,16,128]{2,1,0:T(8,128)(2,1)S(1)} %get-tuple-element.46.refs_3_.refs_2_, ...), custom_call_target="tpu_custom_call" | custom-call | flops 1 | bytes 1 | tf_op jit(solution)/shard_map/pallas_call | solution.py:38
  97.7 4.6 %shard_map.123 = bf16[2,144,2048]{2,1,0:T(8,128)(2,1)} custom-call(s32[2]{0:T(128)S(1)} %pad_add_fusion.refs_0_, bf16[144,1152]{1,0:T(8,128)(2,1)S(1)} %get-tuple-element.40.refs_1_, bf16[16,16,128]{2,1,0:T(8,128)(2,1)S(1)} %get-tuple-element.64.refs_2_, bf16[2,144,896]{2,1,0:T(8,128)(2,1)S(1)} %get-tuple-element.65.refs_3_, ...), custom_call_target="tpu_custom_call" | custom-call | flops 1 | bytes 1 | tf_op jit(solution)/shard_map/pallas_call | solution.py:38
  (49 shorter events, 5.2 us)
Async XLA Ops:
  0.1 1.3 %copy-start = (bf16[2,1,144,2048]{3,2,1,0:T(8,128)(2,1)S(1)}, bf16[2,1,144,2048]{3,2,1,0:T(8,128)(2,1)}, u32[]{:S(2)}) copy-start(bf16[2,1,144,2048]{3,2,1,0:T(8,128)(2,1)} %param.11) | copy-start | bytes 3538948
  1.3 0.7 copy-start.1
  2.0 15.0 %copy-start.10 = (f32[8,12,12]{2,0,1:T(8,128)S(1)}, f32[8,12,12]{2,0,1:T(8,128)}, u32[]{:S(2)}) copy-start(f32[8,12,12]{2,0,1:T(8,128)} %param.15) | copy-start | bytes 13828
  2.9 39.8 %copy-start.2 = (f32[2,8,16]{2,1,0:T(8,128)S(1)}, f32[2,8,16]{2,1,0:T(8,128)}, u32[]{:S(2)}) copy-start(f32[2,8,16]{2,1,0:T(8,128)} %refs_2_.1) | copy-start | bytes 3076
  2.9 39.8 %copy-start.3 = (s32[8]{0:T(128)S(1)}, s32[8]{0:T(128)}, u32[]{:S(2)}) copy-start(s32[8]{0:T(128)} %refs_1_.1) | copy-start | bytes 100
  2.9 39.8 %copy-start.4 = (f32[96,1152]{1,0:T(8,128)S(1)}, f32[96,1152]{1,0:T(8,128)}, u32[]{:S(2)}) copy-start(f32[96,1152]{1,0:T(8,128)} %constant.28.clone.refs_8_) | copy-start | bytes 1327108
  2.9 39.8 %copy-start.5 = (f32[96,1152]{1,0:T(8,128)S(1)}, f32[96,1152]{1,0:T(8,128)}, u32[]{:S(2)}) copy-start(f32[96,1152]{1,0:T(8,128)} %constant.29.clone.refs_9_) | copy-start | bytes 1327108
  2.9 39.8 %copy-start.6 = (f32[144,12]{1,0:T(8,128)S(1)}, f32[144,12]{1,0:T(8,128)}, u32[]{:S(2)}) copy-start(f32[144,12]{1,0:T(8,128)} %constant.26.clone.refs_6_) | copy-start | bytes 20740
  3.0 39.8 %copy-start.7 = (f32[144,12]{1,0:T(8,128)S(1)}, f32[144,12]{1,0:T(8,128)}, u32[]{:S(2)}) copy-start(f32[144,12]{1,0:T(8,128)} %constant.27.clone.refs_7_) | copy-start | bytes 20740
  3.0 39.8 %copy-start.8 = (s32[32,48]{1,0:T(8,128)S(1)}, s32[32,48]{1,0:T(8,128)}, u32[]{:S(2)}) copy-start(s32[32,48]{1,0:T(8,128)} %constant.24.clone.refs_4_) | copy-start | bytes 18436
  3.0 39.8 %copy-start.9 = (s32[32,48]{1,0:T(8,128)S(1)}, s32[32,48]{1,0:T(8,128)}, u32[]{:S(2)}) copy-start(s32[32,48]{1,0:T(8,128)} %constant.25.clone.refs_5_) | copy-start | bytes 18436
  3.0 2.2 %collective-permute-start = (bf16[3,592,128]{2,1,0:T(8,128)(2,1)S(1)}, bf16[3,592,128]{2,1,0:T(8,128)(2,1)S(1)}, u32[]{:S(2)}, u32[]{:S(2)}) collective-permute-start(bf16[3,592,128]{2,1,0:T(8,128)(2,1)S(1)} %get-tuple-element.42), channel_id=1, source_target_pairs={{0,1},{1,0},{2,3},{3,2},{4,5},{5,4},{6,7},{7,6},{8,9},{9,8},{10,11... | collective-permute-start | bytes 1363976 | tf_op jit(solution)/shard_map/ppermute | solution.py:332
  5.3 12.3 %collective-permute-start.1 = (bf16[2,592,128]{2,1,0:T(8,128)(2,1)S(1)}, bf16[2,592,128]{2,1,0:T(8,128)(2,1)S(1)}, u32[]{:S(2)}, u32[]{:S(2)}) collective-permute-start(bf16[2,592,128]{2,1,0:T(8,128)(2,1)S(1)} %get-tuple-element.43), channel_id=1, source_target_pairs={{0,2},{1,15},{2,4},{3,1},{4,6},{5,3},{6,8},{7,5},{8,10},{9,7},{10,... | collective-permute-start | bytes 909320 | tf_op jit(solution)/shard_map/ppermute | solution.py:338
  10.9 13.2 %collective-permute-start.2 = (bf16[2,592,128]{2,1,0:T(8,128)(2,1)S(1)}, bf16[2,592,128]{2,1,0:T(8,128)(2,1)S(1)}, u32[]{:S(2)}, u32[]{:S(2)}) collective-permute-start(bf16[2,592,128]{2,1,0:T(8,128)(2,1)S(1)} %get-tuple-element.44), channel_id=1, source_target_pairs={{0,4},{1,13},{2,6},{3,15},{4,8},{5,1},{6,10},{7,3},{8,12},{9,5},{1... | collective-permute-start | bytes 909320 | tf_op jit(solution)/shard_map/ppermute | solution.py:338
  12.1 25.3 %collective-permute-start.3 = (bf16[2,592,128]{2,1,0:T(8,128)(2,1)S(1)}, bf16[2,592,128]{2,1,0:T(8,128)(2,1)S(1)}, u32[]{:S(2)}, u32[]{:S(2)}) collective-permute-start(bf16[2,592,128]{2,1,0:T(8,128)(2,1)S(1)} %get-tuple-element.47), channel_id=1, source_target_pairs={{0,6},{1,11},{2,8},{3,13},{4,10},{5,15},{6,12},{7,1},{8,14},{9,3},... | collective-permute-start | bytes 909320 | tf_op jit(solution)/shard_map/ppermute | solution.py:338
  12.5 17.0 %collective-permute-start.4 = (bf16[1,592,128]{2,1,0:T(8,128)(2,1)S(1)}, bf16[1,592,128]{2,1,0:T(8,128)(2,1)S(1)}, u32[]{:S(2)}, u32[]{:S(2)}) collective-permute-start(bf16[1,592,128]{2,1,0:T(8,128)(2,1)S(1)} %get-tuple-element.48), channel_id=1, source_target_pairs={{0,8},{1,9},{2,10},{3,11},{4,12},{5,13},{6,14},{7,15},{8,0},{9,1},... | collective-permute-start | bytes 454664 | tf_op jit(solution)/shard_map/ppermute | solution.py:338
  24.2 21.4 %collective-permute-start.7 = (bf16[5,576,128]{2,1,0:T(8,128)(2,1)S(1)}, bf16[5,576,128]{2,1,0:T(8,128)(2,1)S(1)}, u32[]{:S(2)}, u32[]{:S(2)}) collective-permute-start(bf16[5,576,128]{2,1,0:T(8,128)(2,1)S(1)} %get-tuple-element.53.refs_2_), channel_id=1, source_target_pairs={{0,16},{16,32},{32,48},{48,64},{64,80},{80,96},{96,112},{112,128},... | collective-permute-start | bytes 2211848 | tf_op jit(solution)/shard_map/ppermute | solution.py:358
  27.0 18.9 %collective-permute-start.8 = (bf16[5,576,128]{2,1,0:T(8,128)(2,1)S(1)}, bf16[5,576,128]{2,1,0:T(8,128)(2,1)S(1)}, u32[]{:S(2)}, u32[]{:S(2)}) collective-permute-start(bf16[5,576,128]{2,1,0:T(8,128)(2,1)S(1)} %get-tuple-element.53.refs_2_), channel_id=1, source_target_pairs={{16,0},{32,16},{48,32},{64,48},{80,64},{96,80},{112,96},{128,112},... | collective-permute-start | bytes 2211848 | tf_op jit(solution)/shard_map/ppermute | solution.py:359
  37.4 14.1 %collective-permute-start.5 = (bf16[3,576,128]{2,1,0:T(8,128)(2,1)S(1)}, bf16[3,576,128]{2,1,0:T(8,128)(2,1)S(1)}, u32[]{:S(2)}, u32[]{:S(2)}) collective-permute-start(bf16[3,576,128]{2,1,0:T(8,128)(2,1)S(1)} %get-tuple-element.51.refs_4_), channel_id=1, source_target_pairs={{0,16},{16,32},{32,48},{48,64},{64,80},{80,96},{96,112},{112,128},... | collective-permute-start | bytes 1327112 | tf_op jit(solution)/shard_map/ppermute | solution.py:358
  40.2 16.3 %collective-permute-start.6 = (bf16[3,576,128]{2,1,0:T(8,128)(2,1)S(1)}, bf16[3,576,128]{2,1,0:T(8,128)(2,1)S(1)}, u32[]{:S(2)}, u32[]{:S(2)}) collective-permute-start(bf16[3,576,128]{2,1,0:T(8,128)(2,1)S(1)} %get-tuple-element.51.refs_4_), channel_id=1, source_target_pairs={{16,0},{32,16},{48,32},{64,48},{80,64},{96,80},{112,96},{128,112},... | collective-permute-start | bytes 1327112 | tf_op jit(solution)/shard_map/ppermute | solution.py:359
  57.3 4.6 %collective-permute-start.9 = (bf16[8,288,128]{2,1,0:T(8,128)(2,1)S(1)}, bf16[8,288,128]{2,1,0:T(8,128)(2,1)S(1)}, u32[]{:S(2)}, u32[]{:S(2)}) collective-permute-start(bf16[8,288,128]{2,1,0:T(8,128)(2,1)S(1)} %get-tuple-element.58), channel_id=1, source_target_pairs={{0,1},{1,0},{2,3},{3,2},{4,5},{5,4},{6,7},{7,6},{8,9},{9,8},{10,11... | collective-permute-start | bytes 1769480 | tf_op jit(solution)/shard_map/ppermute | solution.py:332
  61.0 8.2 %collective-permute-start.15 = (bf16[8,288,128]{2,1,0:T(8,128)(2,1)S(1)}, bf16[8,288,128]{2,1,0:T(8,128)(2,1)S(1)}, u32[]{:S(2)}, u32[]{:S(2)}) collective-permute-start(bf16[8,288,128]{2,1,0:T(8,128)(2,1)S(1)} %get-tuple-element.69), channel_id=1, source_target_pairs={{0,1},{1,0},{2,3},{3,2},{4,5},{5,4},{6,7},{7,6},{8,9},{9,8},{10,11... | collective-permute-start | bytes 1769480 | tf_op jit(solution)/shard_map/ppermute | solution.py:332
  62.0 16.1 %collective-permute-start.11 = (bf16[2,288,128]{2,1,0:T(8,128)(2,1)S(1)}, bf16[2,288,128]{2,1,0:T(8,128)(2,1)S(1)}, u32[]{:S(2)}, u32[]{:S(2)}) collective-permute-start(bf16[2,288,128]{2,1,0:T(8,128)(2,1)S(1)} %get-tuple-element.60), channel_id=1, source_target_pairs={{0,6},{1,11},{2,8},{3,13},{4,10},{5,15},{6,12},{7,1},{8,14},{9,3},... | collective-permute-start | bytes 442376 | tf_op jit(solution)/shard_map/ppermute | solution.py:338
  63.2 16.9 %collective-permute-start.12 = (bf16[2,288,128]{2,1,0:T(8,128)(2,1)S(1)}, bf16[2,288,128]{2,1,0:T(8,128)(2,1)S(1)}, u32[]{:S(2)}, u32[]{:S(2)}) collective-permute-start(bf16[2,288,128]{2,1,0:T(8,128)(2,1)S(1)} %get-tuple-element.61), channel_id=1, source_target_pairs={{0,4},{1,13},{2,6},{3,15},{4,8},{5,1},{6,10},{7,3},{8,12},{9,5},{1... | collective-permute-start | bytes 442376 | tf_op jit(solution)/shard_map/ppermute | solution.py:338
  63.8 10.0 %collective-permute-start.10 = (bf16[1,288,128]{2,1,0:T(8,128)(2,1)S(1)}, bf16[1,288,128]{2,1,0:T(8,128)(2,1)S(1)}, u32[]{:S(2)}, u32[]{:S(2)}) collective-permute-start(bf16[1,288,128]{2,1,0:T(8,128)(2,1)S(1)} %get-tuple-element.59), channel_id=1, source_target_pairs={{0,8},{1,9},{2,10},{3,11},{4,12},{5,13},{6,14},{7,15},{8,0},{9,1},... | collective-permute-start | bytes 221192 | tf_op jit(solution)/shard_map/ppermute | solution.py:338
  67.1 16.9 %collective-permute-start.13 = (bf16[2,288,128]{2,1,0:T(8,128)(2,1)S(1)}, bf16[2,288,128]{2,1,0:T(8,128)(2,1)S(1)}, u32[]{:S(2)}, u32[]{:S(2)}) collective-permute-start(bf16[2,288,128]{2,1,0:T(8,128)(2,1)S(1)} %get-tuple-element.62), channel_id=1, source_target_pairs={{0,2},{1,15},{2,4},{3,1},{4,6},{5,3},{6,8},{7,5},{8,10},{9,7},{10,... | collective-permute-start | bytes 442376 | tf_op jit(solution)/shard_map/ppermute | solution.py:338
  69.3 20.9 %collective-permute-start.17 = (bf16[2,288,128]{2,1,0:T(8,128)(2,1)S(1)}, bf16[2,288,128]{2,1,0:T(8,128)(2,1)S(1)}, u32[]{:S(2)}, u32[]{:S(2)}) collective-permute-start(bf16[2,288,128]{2,1,0:T(8,128)(2,1)S(1)} %get-tuple-element.71), channel_id=1, source_target_pairs={{0,6},{1,11},{2,8},{3,13},{4,10},{5,15},{6,12},{7,1},{8,14},{9,3},... | collective-permute-start | bytes 442376 | tf_op jit(solution)/shard_map/ppermute | solution.py:338
  73.7 16.5 %collective-permute-start.18 = (bf16[2,288,128]{2,1,0:T(8,128)(2,1)S(1)}, bf16[2,288,128]{2,1,0:T(8,128)(2,1)S(1)}, u32[]{:S(2)}, u32[]{:S(2)}) collective-permute-start(bf16[2,288,128]{2,1,0:T(8,128)(2,1)S(1)} %get-tuple-element.72), channel_id=1, source_target_pairs={{0,4},{1,13},{2,6},{3,15},{4,8},{5,1},{6,10},{7,3},{8,12},{9,5},{1... | collective-permute-start | bytes 442376 | tf_op jit(solution)/shard_map/ppermute | solution.py:338
  78.1 12.1 %collective-permute-start.19 = (bf16[2,288,128]{2,1,0:T(8,128)(2,1)S(1)}, bf16[2,288,128]{2,1,0:T(8,128)(2,1)S(1)}, u32[]{:S(2)}, u32[]{:S(2)}) collective-permute-start(bf16[2,288,128]{2,1,0:T(8,128)(2,1)S(1)} %get-tuple-element.73), channel_id=1, source_target_pairs={{0,2},{1,15},{2,4},{3,1},{4,6},{5,3},{6,8},{7,5},{8,10},{9,7},{10,... | collective-permute-start | bytes 442376 | tf_op jit(solution)/shard_map/ppermute | solution.py:338
  80.0 10.2 %collective-permute-start.16 = (bf16[1,288,128]{2,1,0:T(8,128)(2,1)S(1)}, bf16[1,288,128]{2,1,0:T(8,128)(2,1)S(1)}, u32[]{:S(2)}, u32[]{:S(2)}) collective-permute-start(bf16[1,288,128]{2,1,0:T(8,128)(2,1)S(1)} %get-tuple-element.70), channel_id=1, source_target_pairs={{0,8},{1,9},{2,10},{3,11},{4,12},{5,13},{6,14},{7,15},{8,0},{9,1},... | collective-permute-start | bytes 221192 | tf_op jit(solution)/shard_map/ppermute | solution.py:338
  84.0 10.7 %collective-permute-start.14 = (bf16[992,128]{1,0:T(8,128)(2,1)S(1)}, bf16[992,128]{1,0:T(8,128)(2,1)S(1)}, u32[]{:S(2)}, u32[]{:S(2)}) collective-permute-start(bf16[992,128]{1,0:T(8,128)(2,1)S(1)} %shard_map.118), channel_id=1, source_target_pairs={{0,1},{1,0},{2,3},{3,2},{4,5},{5,4},{6,7},{7,6},{8,9},{9,8},{10,11... | collective-permute-start | bytes 761864 | tf_op jit(solution)/shard_map/ppermute | solution.py:332
  90.2 7.5 %collective-permute-start.20 = (bf16[864,128]{1,0:T(8,128)(2,1)S(1)}, bf16[864,128]{1,0:T(8,128)(2,1)S(1)}, u32[]{:S(2)}, u32[]{:S(2)}) collective-permute-start(bf16[864,128]{1,0:T(8,128)(2,1)S(1)} %shard_map.122), channel_id=1, source_target_pairs={{0,1},{1,0},{2,3},{3,2},{4,5},{5,4},{6,7},{7,6},{8,9},{9,8},{10,11... | collective-permute-start | bytes 663560 | tf_op jit(solution)/shard_map/ppermute | solution.py:332
